TPU v7x, 256 devices: a whole 4x4x8 slice. The times are simulated.
256 devices in a mesh: clip: 4 (over z_lo), seq: 16 (over x, y), expert: 4 (over z_hi, core).
Axes of the slice: x: 4, y: 4, z: 8 (z_hi: 2, z_lo: 4; z = z_hi * 4 + z_lo), core: 2. Of those that a mesh axis runs over, the one named last changes fastest.
Arguments:
- tokens: bfloat16 [262144, 1024], P(('clip', 'seq'), 'expert'), parts along dimension 0, may hold values from -55 to 55
- slot_keys: bfloat16 [1024, 32], P('expert'), may hold values from -0.390625 to 0.390625
- w_in: bfloat16 [32, 1024, 4096], P('expert', None, 'seq'), may hold values from -1.5 to 1.5
- w_out: bfloat16 [32, 4096, 1024], P('expert', 'seq'), may hold values from -0.09375 to 0.09375
Outputs:
- mixed_out: float32 [262144, 1024], P(('clip', 'seq'), 'expert'), parts along dimension 0
There are 4 independent parts, one for each index of `clip`. A program takes and returns all parts, laid end to end along the dimension named above; an argument that names none is the same for every part. Nothing has to cross between parts.
All inputs are finite; a program needn't handle non-finite values.
Results may differ from a plain program's by a relative error of at most 0.015.
Values may be sent and summed in bfloat16 or wider, within the bound.
No kernel may reach another device: no remote copies, remote signals or barrier semaphores. Data moves between devices by JAX's collectives and lax.ppermute only.
A program may use at most 64 MiB of HBM per device.

v0:
```python
import jax
import jax.numpy as jnp
from jax import lax
from jax.sharding import PartitionSpec as P


def merged(part, axis, combine):
    gathered = jax.tree.map(lambda a: lax.all_gather(a, axis), part)

    def take(source):
        return jax.tree.map(lambda a: lax.dynamic_index_in_dim(a, source, 0, False), gathered)

    return lax.fori_loop(
        1, lax.axis_size(axis), lambda source, state: combine(state, take(source)), take(0)
    )


def join_parts(first, second):
    first_max, first_total, first_sum = first
    second_max, second_total, second_sum = second
    joined = jnp.maximum(first_max, second_max)
    first_scale = jnp.exp(first_max - joined)
    second_scale = jnp.exp(second_max - joined)
    totals = first_total * first_scale + second_total * second_scale
    summed = first_sum * first_scale[:, None] + second_sum * second_scale[:, None]
    return (joined, totals, summed)


def local(tokens, slot_keys, w_in, w_out):
    partial_scores = lax.dot_general(
        slot_keys, tokens, (((0,), (1,)), ((), ())), preferred_element_type=jnp.float32
    )
    logits = lax.psum(partial_scores, "expert")
    top_local = jnp.max(logits, axis=1)
    dispatch = jnp.exp(logits - top_local[:, None]).astype(jnp.bfloat16)
    combine = jax.nn.softmax(logits, axis=0).astype(jnp.bfloat16)
    total_local = jnp.sum(dispatch.astype(jnp.float32), axis=1)
    weighted = jnp.dot(dispatch, tokens, preferred_element_type=jnp.float32)
    top_slot, totals, summed = merged((top_local, total_local, weighted), "seq", join_parts)
    slot_in = (summed / totals[:, None]).astype(jnp.bfloat16)
    owned_slots = lax.all_to_all(slot_in, "expert", split_axis=0, concat_axis=1, tiled=True)
    inner = jnp.einsum("ed,edf->ef", owned_slots, w_in, preferred_element_type=jnp.float32)
    hidden = jax.nn.gelu(inner, approximate=False).astype(jnp.bfloat16)
    partial_out = jnp.einsum("ef,efd->ed", hidden, w_out, preferred_element_type=jnp.float32)
    slot_out = lax.psum(partial_out, "seq")
    returned = lax.all_to_all(slot_out, "expert", split_axis=1, concat_axis=0, tiled=True)
    mixed_out = lax.dot_general(
        combine.astype(jnp.float32),
        returned,
        (((0,), (0,)), ((), ())),
        preferred_element_type=jnp.float32,
    )
    return mixed_out


def solution(mesh):
    return jax.shard_map(
        local,
        mesh=mesh,
        in_specs=(
            P(("clip", "seq"), "expert"),
            P("expert", None),
            P("expert", None, "seq"),
            P("expert", "seq", None),
        ),
        out_specs=P(("clip", "seq"), "expert"),
        check_vma=False,
    )
```

profile of v0, /device:TPU:33, one launch (start us, length us, event | category | flops | bytes accessed | tf_op | source)
XLA Modules:
  0.0 243.8 jit_solution(5370904943834263244)
XLA Ops:
  6.5 1.6 copy-done
  8.1 2.2 fusion.34
  10.4 1.3 dynamic-slice
  12.2 58.3 %all-reduce.5.cloned.1.call-done = f32[32,4096]{1,0:T(8,128)} async-done(((f32[32,4096]{1,0:T(8,128)}), f32[32,4096]{1,0:T(8,128)}) %all-reduce.5.cloned.1.call-update) | async-done | bytes 524304 | tf_op jit(solution)/shard_map/psum | solution.py:33
  70.5 1.2 fusion.32
  71.7 0.2 dynamic-update-slice
  72.0 1.3 convert_reduce_fusion
  73.3 0.2 dynamic-update-slice.1
  73.5 33.4 %all-reduce.2 = (f32[512]{0:T(512)S(1)}, f32[512]{0:T(512)S(1)}) all-reduce(f32[512]{0:T(512)S(1)} %dynamic-update-slice, f32[512]{0:T(512)S(1)} %dynamic-update-slice.1), channel_id=2, replica_groups=mesh['clip'=4,'seq'=16,'expert'=4] {'seq'}, use_global_device_ids=true, to_apply=%add | all-reduce | flops 1024 | bytes 8192
  107.1 1.6 fusion.31
  108.6 16.0 %all-gather.2 = f32[512,256]{1,0:T(8,128)S(1)} all-gather(f32[32,256]{1,0:T(8,128)S(1)} %fusion.31), channel_id=4, replica_groups=mesh['clip'=4,'seq'=16,'expert'=4] {'seq'}, dimensions={0}, use_global_device_ids=true | all-gather | bytes 557056 | tf_op jit(solution)/shard_map/all_gather | solution.py:8
  124.7 1.6 while.19
  124.7 0.1 fusion.43
  124.9 0.1 fusion.43
  125.0 0.1 fusion.43
  125.1 0.1 fusion.43
  125.2 0.1 fusion.43
  125.4 0.1 fusion.43
  126.3 22.0 %all_to_all.38 = bf16[4,8,256]{2,1,0:T(8,128)(2,1)S(1)} all-to-all(bf16[4,8,256]{2,1,0:T(8,128)(2,1)S(1)} %fusion.13), channel_id=1, replica_groups=mesh['clip'=4,'seq'=16,'expert'=4] {'expert'}, dimensions={0} | all-to-all | bytes 32768 | tf_op jit(solution)/shard_map/all_to_all | solution.py:41
  148.3 2.9 %fusion.11 = f32[8,1,256]{2,1,0:T(1,128)S(1)} fusion(bf16[8,1024,256]{2,1,0:T(8,128)(2,1)} %param.8, bf16[8,1024,1]{1,0,2:T(8,128)(2,1)S(1)} %bitcast.86), kind=kOutput, calls=%fused_computation.20 | convolution fusion | flops 4194304 | bytes 4218880 | tf_op jit(solution)/shard_map/ed,edf->ef/dot_general | solution.py:42
  151.3 0.7 fusion.18
  152.0 57.9 %psum.15 = bf16[8,4,256]{2,0,1:T(8,128)(2,1)S(1)} all-reduce(f32[8,4,256]{2,0,1:T(8,128)S(1)} %bitcast.87), channel_id=1, replica_groups=mesh['clip'=4,'seq'=16,'expert'=4] {'seq'}, use_global_device_ids=true, to_apply=%region_7.8 | all-reduce | flops 8192 | bytes 49152 | tf_op jit(solution)/shard_map/psum | solution.py:45
  209.9 24.3 %all_to_all.39 = bf16[8,4,256]{2,0,1:T(8,128)(2,1)S(1)} all-to-all(bf16[8,4,256]{2,0,1:T(8,128)(2,1)S(1)} %psum.15), channel_id=1, replica_groups=mesh['clip'=4,'seq'=16,'expert'=4] {'expert'}, dimensions={1} | all-to-all | bytes 32768 | tf_op jit(solution)/shard_map/all_to_all | solution.py:46
  234.1 2.8 %fusion.7 = f32[4096,256]{1,0:T(8,128)} fusion(f32[32,4096]{1,0:T(8,128)S(1)} %copy-done.1, f32[4096]{0:T(1024)S(1)} %get-tuple-element.185, f32[4096]{0:T(1024)S(1)} %get-tuple-element.187, bf16[8,4,256]{2,0,1:T(8,128)(2,1)S(1)} %all_to_all.39), kind=kOutput, calls=%fused_computation.16 | convolution fusion | flops 67502080 | bytes 4767744 | tf_op jit(solution)/shard_map/dot_general | solution.py:47
  (41 shorter events, 1.4 us)
Async XLA Ops:
  6.5 1.6 copy-start
  6.5 64.0 %all-reduce.5.cloned.1.call-start = ((), (), s32[]{:S(2)}) async-start(), calls=%async_computation.2 | async-start | bytes 1048576 | tf_op jit(solution)/shard_map/psum | solution.py:33
  126.2 25.1 %copy-start.2 = (bf16[8,256,1024]{2,1,0:T(8,128)(2,1)S(1)}, bf16[8,256,1024]{2,1,0:T(8,128)(2,1)}, u32[]{:S(2)}) copy-start(bf16[8,256,1024]{2,1,0:T(8,128)(2,1)} %param.9) | copy-start | bytes 12582916
  148.3 85.8 %copy-start.1 = (f32[32,4096]{1,0:T(8,128)S(1)}, f32[32,4096]{1,0:T(8,128)}, u32[]{:S(2)}) copy-start(f32[32,4096]{1,0:T(8,128)} %all-reduce.5.cloned.1.call-done) | copy-start | bytes 1572868
Sparse Core Ops, SparseCore 0:
  10.5 59.9 all-reduce.4
where the time goes:
time: 246 us; the launch traced here: 244 us
  blocking collectives  154 us (63%)
  waiting for transfers between devices  58.3 us (24%)
  between operations  14 us (6%)
  matrix products  10.1 us (4%)
  other arithmetic  4.19 us (2%)
  local copies, waits for them, and re-layouts  3.51 us (1%)
    psum x1, waiting for transfers between devices, local(): logits = lax.psum(partial_scores, 'expert')  58.3 us
    psum x1, blocking collectives, local(): slot_out = lax.psum(partial_out, 'seq')  57.9 us
    unnamed x1, blocking collectives  33.4 us
    all_to_all x1, blocking collectives, local(): lax.all_to_all(slot_out, 'expert', split_axis=1, concat_axis=0, tiled=True)  24.3 us
    all_to_all x1, blocking collectives, local(): lax.all_to_all(slot_in, 'expert', split_axis=0, concat_axis=1, tiled=True)  22 us
    all_gather x1, blocking collectives, merged(): gathered = jax.tree.map(lambda a: lax.all_gather(a, axis), part)  16 us
  transfers between devices with their start and end apart: 1, of which 1 were waited for; matrix products, arithmetic and copies ran while one was open for 1% of the time, Pallas kernels for 0%

commit v1 on v0

v1 whole, which is shorter than its diff:
```python
import jax
import jax.numpy as jnp
from jax import lax
from jax.sharding import PartitionSpec as P

BF16 = jnp.bfloat16
F32 = jnp.float32


def swap(value, z_step, core_step):
    pairs = [
        (z * 2 + c, (z ^ z_step) * 2 + (c ^ core_step)) for z in range(2) for c in range(2)
    ]
    return lax.ppermute(value, "expert", pairs)


def full_logits(tokens, slot_keys):
    count = tokens.shape[0]
    half = count // 2
    core = lax.axis_index("expert") % 2
    partial = lax.dot_general(
        slot_keys, tokens, (((0,), (1,)), ((), ())), preferred_element_type=F32
    )
    theirs = jnp.where(core == 0, partial[:, half:], partial[:, :half])
    mine = jnp.where(core == 0, partial[:, :half], partial[:, half:])
    mine = mine + swap(theirs, 0, 1)
    mine = mine + swap(mine, 1, 0)
    other = swap(mine, 0, 1)
    return jnp.concatenate(
        [jnp.where(core == 0, mine, other), jnp.where(core == 0, other, mine)], axis=1
    )


def spread(value):
    first = lax.reduce_precision(value, 8, 7)
    second = lax.reduce_precision(value - first, 8, 7)
    third = value - first - second
    return jnp.stack([first, second, third], axis=-1).astype(BF16)


def local(tokens, slot_keys, w_in, w_out):
    seq = lax.axis_size("seq")
    expert = lax.axis_size("expert")
    group = ("seq", "expert")
    slots = slot_keys.shape[1]
    width = tokens.shape[1]
    own = slots // expert

    logits = full_logits(tokens, slot_keys)
    top = jnp.max(logits, axis=1)
    dispatch = jnp.exp(logits - top[:, None]).astype(BF16)
    combine = jax.nn.softmax(logits, axis=0).astype(BF16)
    totals = jnp.sum(dispatch.astype(F32), axis=1)
    weighted = jnp.dot(dispatch, tokens, preferred_element_type=F32)
    mean = (weighted / totals[:, None]).astype(BF16)
    weight = spread(top + jnp.log(totals))
    weight = jnp.pad(weight, ((0, 0), (0, 125)))
    send = jnp.concatenate([mean, weight], axis=1).reshape(1, expert, own, width + 128)
    send = jnp.broadcast_to(send, (seq, expert, own, width + 128))
    got = lax.all_to_all(send.reshape(seq * expert, own, width + 128), group, 0, 0)
    got = got.reshape(seq, expert, own, width + 128).astype(F32)
    weight = jnp.sum(got[..., width : width + 3], axis=-1, keepdims=True)
    scale = jax.nn.softmax(weight, axis=0)
    slot_in = jnp.sum(got[..., :width] * scale, axis=0).astype(BF16)
    slot_in = slot_in.transpose(1, 0, 2).reshape(own, expert * width)

    inner = jnp.einsum("ed,edf->ef", slot_in, w_in, preferred_element_type=F32)
    hidden = jax.nn.gelu(inner, approximate=False).astype(BF16)
    partial_out = jnp.einsum("ef,efd->ed", hidden, w_out, preferred_element_type=F32)
    back = partial_out.astype(BF16).reshape(own, expert, width).transpose(1, 0, 2)
    back = jnp.broadcast_to(back[None], (seq, expert, own, width))
    back = lax.all_to_all(back.reshape(seq * expert, own, width), group, 0, 0)
    back = back.reshape(seq, slots, width).astype(F32)
    returned = jnp.sum(back, axis=0).astype(BF16)
    return lax.dot_general(
        combine, returned, (((0,), (0,)), ((), ())), preferred_element_type=F32
    )


def solution(mesh):
    return jax.shard_map(
        local,
        mesh=mesh,
        in_specs=(
            P(("clip", "seq"), "expert"),
            P("expert", None),
            P("expert", None, "seq"),
            P("expert", "seq", None),
        ),
        out_specs=P(("clip", "seq"), "expert"),
        check_vma=False,
    )
```

time: 246 us -> 83.4 us (0.34)
  blocking collectives: 154 us -> 48.5 us
  waiting for transfers between devices: 58.3 us -> 14.3 us
  between operations: 14 us -> 0.1 us
  starting transfers between devices: 0.01 us -> 7.92 us
  other arithmetic: 4.19 us -> 1.4 us
    psum x1 -> x0, waiting for transfers between devices: 58.3 us -> none  [local(): logits = lax.psum(partial_scores, 'expert')]
    psum x1 -> x0, blocking collectives: 57.9 us -> none  [local(): slot_out = lax.psum(partial_out, 'seq')]
    unnamed x1 -> x0, blocking collectives: 33.4 us -> none
    all_gather x1 -> x0, blocking collectives: 16 us -> none  [merged(): gathered = jax.tree.map(lambda a: lax.all_gather(a, axis), part)]
    ppermute x0 -> x3, waiting for transfers between devices: none -> 14.3 us  [swap(): return lax.ppermute(value, 'expert', pairs)]
    ppermute x0 -> x3, starting transfers between devices: none -> 7.92 us  [swap(): return lax.ppermute(value, 'expert', pairs)]
  transfers between devices with their start and end apart: 1 -> 3, of which waited for: 1 -> 3; matrix products, arithmetic and copies ran while one was open for 1% -> 0% of each run, Pallas kernels for 0% -> 0%
where the time goes in v1:
time: 83.4 us; the launch traced here: 82.7 us
  blocking collectives  48.5 us (58%)
  waiting for transfers between devices  14.3 us (17%)
  matrix products  8.3 us (10%)
  starting transfers between devices  7.92 us (9%)
  local copies, waits for them, and re-layouts  2.19 us (3%)
  other arithmetic  1.4 us (2%)
    all_to_all x1, blocking collectives, local(): lax.all_to_all(send.reshape(seq * expert, own, width + 128), group, 0, 0)  30.5 us
    all_to_all x1, blocking collectives, local(): back = lax.all_to_all(back.reshape(seq * expert, own, width), group, 0, 0)  18 us
    ppermute x3, waiting for transfers between devices, swap(): return lax.ppermute(value, 'expert', pairs)  14.3 us
    ppermute x3, starting transfers between devices, swap(): return lax.ppermute(value, 'expert', pairs)  7.92 us
    dot_general x1, matrix products, local(): inner = jnp.einsum('ed,edf->ef', slot_in, w_in, preferred_element_type=F32)  2.99 us
    dot_general x1, matrix products, local(): lax.dot_general(combine, returned, (((0,), (0,)), ((), ())), preferred_el...  2.78 us
    unnamed x5, local copies, waits for them, and re-layouts  1.94 us
  transfers between devices with their start and end apart: 3, of which 3 were waited for; matrix products, arithmetic and copies ran while one was open for 0% of the time, Pallas kernels for 0%

profile of v1, /device:TPU:33, one launch (start us, length us, event | category | flops | bytes accessed | tf_op | source)
XLA Modules:
  0.0 82.7 jit_solution(14587924808903861926)
XLA Ops:
  0.0 1.6 %copy-done = bf16[4096,256]{1,0:T(8,128)(2,1)S(1)} copy-done((bf16[4096,256]{1,0:T(8,128)(2,1)S(1)}, bf16[4096,256]{1,0:T(8,128)(2,1)}, u32[]{:S(2)}) %copy-start) | copy-done | bytes 2097176
  1.6 1.4 %fusion.35 = f32[32,4096]{1,0:T(8,128)S(1)} fusion(bf16[256,32]{0,1:T(8,128)(2,1)} %param.5, bf16[4096,256]{1,0:T(8,128)(2,1)S(1)} %copy-done), kind=kOutput, calls=%fused_computation.67 | convolution fusion | flops 67108864 | bytes 2637824 | tf_op jit(solution)/shard_map/dot_general | solution.py:21
  3.1 0.8 collective-permute-start
  3.8 1.2 %collective-permute-done = f32[32,2048]{1,0:T(8,128)S(1)} collective-permute-done((f32[32,2048]{1,0:T(8,128)S(1)}, f32[32,2048]{1,0:T(8,128)S(1)}, u32[]{:S(2)}, u32[]{:S(2)}) %collective-permute-start) | collective-permute-done | bytes 262176 | tf_op jit(solution)/shard_map/ppermute | solution.py:14
  5.0 6.1 %collective-permute-start.1 = (f32[32,2048]{1,0:T(8,128)S(1)}, f32[32,2048]{1,0:T(8,128)S(1)}, u32[]{:S(2)}, u32[]{:S(2)}) collective-permute-start(f32[32,2048]{1,0:T(8,128)S(1)} %select_add_fusion), channel_id=1, source_target_pairs={{0,2},{1,3},{2,0},{3,1},{4,6},{5,7},{6,4},{7,5},{8,10},{9,11},{10,... | collective-permute-start | bytes 786440 | tf_op jit(solution)/shard_map/ppermute | solution.py:14
  11.1 12.0 %collective-permute-done.1 = f32[32,2048]{1,0:T(8,128)S(1)} collective-permute-done((f32[32,2048]{1,0:T(8,128)S(1)}, f32[32,2048]{1,0:T(8,128)S(1)}, u32[]{:S(2)}, u32[]{:S(2)}) %collective-permute-start.1) | collective-permute-done | bytes 262176 | tf_op jit(solution)/shard_map/ppermute | solution.py:14
  23.2 1.1 %collective-permute-start.2 = (f32[32,2048]{1,0:T(8,128)S(1)}, f32[32,2048]{1,0:T(8,128)S(1)}, u32[]{:S(2)}, u32[]{:S(2)}) collective-permute-start(f32[32,2048]{1,0:T(8,128)S(1)} %add.35), channel_id=1, source_target_pairs={{0,1},{1,0},{2,3},{3,2},{4,5},{5,4},{6,7},{7,6},{8,9},{9,8},{10,11... | collective-permute-start | bytes 786440 | tf_op jit(solution)/shard_map/ppermute | solution.py:14
  24.2 1.2 %collective-permute-done.2 = f32[32,2048]{1,0:T(8,128)S(1)} collective-permute-done((f32[32,2048]{1,0:T(8,128)S(1)}, f32[32,2048]{1,0:T(8,128)S(1)}, u32[]{:S(2)}, u32[]{:S(2)}) %collective-permute-start.2) | collective-permute-done | bytes 262176 | tf_op jit(solution)/shard_map/ppermute | solution.py:14
  25.4 0.2 fusion.33
  25.6 0.3 convert_reduce_fusion
  25.9 0.5 fusion
  26.4 0.1 copy.8
  26.6 30.5 %all_to_all.10 = bf16[64,8,384]{2,1,0:T(8,128)(2,1)S(1)} all-to-all(bf16[64,8,384]{2,1,0:T(8,128)(2,1)S(1)} %bitcast.76), channel_id=1, replica_groups=mesh['clip'=4,'seq'=16,'expert'=4] {'seq','expert'}, dimensions={0} | all-to-all | bytes 786432 | tf_op jit(solution)/shard_map/all_to_all | solution.py:60
  57.1 0.2 slice_reduce_fusion
  57.3 0.1 copy.15
  57.4 0.2 fusion.13
  57.6 0.1 fusion.12
  57.7 0.1 copy.10
  57.8 0.1 fusion.1
  57.9 3.0 %fusion.8 = f32[8,1,256]{2,1,0:T(1,128)S(1)} fusion(bf16[8,1024,256]{2,1,0:T(8,128)(2,1)} %param.6, bf16[8,1024,1]{1,0,2:T(8,128)(2,1)S(1)} %bitcast.79), kind=kOutput, calls=%fused_computation.23 | convolution fusion | flops 4194304 | bytes 4218880 | tf_op jit(solution)/shard_map/ed,edf->ef/dot_general | solution.py:67
  60.9 0.3 copy-done.1
  61.2 0.7 fusion.18
  61.9 18.0 %all_to_all.11 = bf16[64,8,256]{2,1,0:T(8,128)(2,1)S(1)} all-to-all(bf16[64,8,256]{2,1,0:T(8,128)(2,1)S(1)} %bitcast.77), channel_id=1, replica_groups=mesh['clip'=4,'seq'=16,'expert'=4] {'seq','expert'}, dimensions={0} | all-to-all | bytes 524288 | tf_op jit(solution)/shard_map/all_to_all | solution.py:72
  79.9 2.8 %fusion.3 = f32[4096,256]{1,0:T(8,128)} fusion(bf16[32,256]{1,0:T(8,128)(2,1)S(1)} %bitcast_reduce_fusion, f32[4096]{0:T(1024)S(1)} %get-tuple-element.11, f32[4096]{0:T(1024)S(1)} %fusion.6, f32[32,2048]{1,0:T(8,128)S(1)} %get-tuple-element.8, f32[32,2048]{1,0:T(8,128)S(1)} %get-tuple-element.13), kind=kOutput, calls=%fused_computation.10 | convolution fusion | flops 67633152 | bytes 4767744 | tf_op jit(solution)/shard_map/dot_general | solution.py:75
  (17 shorter events, 0.5 us)
Async XLA Ops:
  0.0 1.6 %copy-start = (bf16[4096,256]{1,0:T(8,128)(2,1)S(1)}, bf16[4096,256]{1,0:T(8,128)(2,1)}, u32[]{:S(2)}) copy-start(bf16[4096,256]{1,0:T(8,128)(2,1)} %param.4) | copy-start | bytes 6291460
  3.1 1.9 %collective-permute-start = (f32[32,2048]{1,0:T(8,128)S(1)}, f32[32,2048]{1,0:T(8,128)S(1)}, u32[]{:S(2)}, u32[]{:S(2)}) collective-permute-start(f32[32,2048]{1,0:T(8,128)S(1)} %slice_select_fusion), channel_id=1, source_target_pairs={{0,1},{1,0},{2,3},{3,2},{4,5},{5,4},{6,7},{7,6},{8,9},{9,8},{10,11... | collective-permute-start | bytes 786440 | tf_op jit(solution)/shard_map/ppermute | solution.py:14
  5.0 18.1 %collective-permute-start.1 = (f32[32,2048]{1,0:T(8,128)S(1)}, f32[32,2048]{1,0:T(8,128)S(1)}, u32[]{:S(2)}, u32[]{:S(2)}) collective-permute-start(f32[32,2048]{1,0:T(8,128)S(1)} %select_add_fusion), channel_id=1, source_target_pairs={{0,2},{1,3},{2,0},{3,1},{4,6},{5,7},{6,4},{7,5},{8,10},{9,11},{10,... | collective-permute-start | bytes 786440 | tf_op jit(solution)/shard_map/ppermute | solution.py:14
  23.2 2.2 %collective-permute-start.2 = (f32[32,2048]{1,0:T(8,128)S(1)}, f32[32,2048]{1,0:T(8,128)S(1)}, u32[]{:S(2)}, u32[]{:S(2)}) collective-permute-start(f32[32,2048]{1,0:T(8,128)S(1)} %add.35), channel_id=1, source_target_pairs={{0,1},{1,0},{2,3},{3,2},{4,5},{5,4},{6,7},{7,6},{8,9},{9,8},{10,11... | collective-permute-start | bytes 786440 | tf_op jit(solution)/shard_map/ppermute | solution.py:14
  57.8 3.5 %copy-start.1 = (bf16[8,256,1024]{2,1,0:T(8,128)(2,1)S(1)}, bf16[8,256,1024]{2,1,0:T(8,128)(2,1)}, u32[]{:S(2)}) copy-start(bf16[8,256,1024]{2,1,0:T(8,128)(2,1)} %param.7) | copy-start | bytes 12582916

commit v2 on v1

v2 whole, which is shorter than its diff:
```python
import jax
import jax.numpy as jnp
from jax import lax
from jax.experimental import pallas as pl
from jax.experimental.pallas import tpu as pltpu
from jax.sharding import PartitionSpec as P

BF16 = jnp.bfloat16
F32 = jnp.float32
LANES = 128
REACH = 125.0
BLOCK = 512


def swap(value, z_step, core_step):
    pairs = [
        (z * 2 + c, (z ^ z_step) * 2 + (c ^ core_step)) for z in range(2) for c in range(2)
    ]
    return lax.ppermute(value, "expert", pairs)


def spread(value):
    first = lax.reduce_precision(value, 8, 7)
    second = lax.reduce_precision(value - first, 8, 7)
    return [first, second, value - first - second]


def exchanged(scores):
    high = jnp.max(scores, axis=1)
    low = jnp.min(scores, axis=1)
    center = 0.5 * (high + low)
    span = jnp.maximum(high - low, 1e-30)
    code = jnp.exp2((scores - center[:, None]) * (2 * REACH / span)[:, None])
    side = jnp.stack(spread(center) + spread(span), axis=1)
    side = jnp.pad(side, ((0, 0), (0, LANES - side.shape[1])))
    sent = jnp.concatenate([code, side], axis=1).astype(BF16)
    got = swap(sent, 1, 0).astype(F32)
    count = scores.shape[1]
    center = jnp.sum(got[:, count : count + 3], axis=1, keepdims=True)
    span = jnp.sum(got[:, count + 3 : count + 6], axis=1, keepdims=True)
    return jnp.log2(got[:, :count]) * (span / (2 * REACH)) + center


def full_logits(tokens, slot_keys):
    count = tokens.shape[0]
    half = count // 2
    core = lax.axis_index("expert") % 2
    partial = lax.dot_general(
        slot_keys, tokens, (((0,), (1,)), ((), ())), preferred_element_type=F32
    )
    theirs = jnp.where(core == 0, partial[:, half:], partial[:, :half])
    mine = jnp.where(core == 0, partial[:, :half], partial[:, half:])
    mine = mine + swap(theirs, 0, 1)
    mine = mine + exchanged(mine)
    other = swap(mine, 0, 1)
    return jnp.concatenate(
        [jnp.where(core == 0, mine, other), jnp.where(core == 0, other, mine)], axis=1
    )


def experts(got, w_in, w_out, seq, expert):
    own, width = w_in.shape[0], w_in.shape[1] // expert
    hidden_width = w_in.shape[2]

    def kernel(got_ref, w_in_ref, w_out_ref, out_ref):
        weight = jnp.sum(got_ref[:, :, width:].astype(F32), axis=-1, keepdims=True)
        weight = weight.reshape(seq, expert, own, 1)
        scale = jnp.exp(weight - jnp.max(weight, axis=0, keepdims=True))
        scale = scale / jnp.sum(scale, axis=0, keepdims=True)
        pieces = []
        for e in range(expert):
            total = jnp.zeros((own, width), F32)
            for s in range(seq):
                total += got_ref[s * expert + e, :, :width].astype(F32) * scale[s, e]
            pieces.append(total.astype(BF16))
        rows = lax.broadcasted_iota(jnp.int32, (own, hidden_width), 0)
        inner = jnp.zeros((own, hidden_width), F32)
        for i in range(own):
            total = jnp.zeros((own, hidden_width), F32)
            for e in range(expert):
                total += jnp.dot(
                    pieces[e],
                    w_in_ref[i, e * width : (e + 1) * width, :],
                    preferred_element_type=F32,
                )
            inner = jnp.where(rows == i, total, inner)
        hidden = 0.5 * inner * (1.0 + lax.erf(inner * (0.5**0.5)))
        hidden = hidden.astype(BF16)
        for e in range(expert):
            rows = lax.broadcasted_iota(jnp.int32, (own, width), 0)
            result = jnp.zeros((own, width), F32)
            for i in range(own):
                part = jnp.dot(
                    hidden,
                    w_out_ref[i, :, e * width : (e + 1) * width],
                    preferred_element_type=F32,
                )
                result = jnp.where(rows == i, part, result)
            result = result.astype(BF16)
            for s in range(seq):
                out_ref[s * expert + e] = result

    whole = pl.BlockSpec(memory_space=pltpu.VMEM)
    return pl.pallas_call(
        kernel,
        out_shape=jax.ShapeDtypeStruct((seq * expert, own, width), BF16),
        in_specs=[whole, whole, whole],
        out_specs=whole,
        compiler_params=pltpu.CompilerParams(vmem_limit_bytes=24 * 2**20),
        cost_estimate=pl.CostEstimate(
            flops=4 * own * width * expert * hidden_width * own,
            bytes_accessed=2 * (w_in.size + w_out.size),
            transcendentals=own * hidden_width,
        ),
        name="experts",
    )(
        got,
        pltpu.with_memory_space_constraint(w_in, pltpu.VMEM),
        pltpu.with_memory_space_constraint(w_out, pltpu.VMEM),
    )


def mix(combine, back, seq, expert):
    slots, count = combine.shape
    width = back.shape[2]
    own = slots // expert

    def kernel(combine_ref, back_ref, out_ref, table):
        @pl.when(pl.program_id(0) == 0)
        def _():
            parts = []
            for e in range(expert):
                total = jnp.zeros((own, width), F32)
                for s in range(seq):
                    total += back_ref[s * expert + e].astype(F32)
                parts.append(total)
            table[...] = jnp.concatenate(parts, axis=0).astype(BF16)

        out_ref[...] = lax.dot_general(
            combine_ref[...],
            table[...],
            (((0,), (0,)), ((), ())),
            preferred_element_type=F32,
        )

    return pl.pallas_call(
        kernel,
        grid=(count // BLOCK,),
        out_shape=jax.ShapeDtypeStruct((count, width), F32),
        in_specs=[
            pl.BlockSpec((slots, BLOCK), lambda i: (0, i)),
            pl.BlockSpec(back.shape, lambda i: (0, 0, 0)),
        ],
        out_specs=pl.BlockSpec((BLOCK, width), lambda i: (i, 0)),
        scratch_shapes=[pltpu.VMEM((slots, width), BF16)],
        compiler_params=pltpu.CompilerParams(vmem_limit_bytes=16 * 2**20),
        cost_estimate=pl.CostEstimate(
            flops=2 * slots * count * width, bytes_accessed=4 * count * width, transcendentals=0
        ),
        name="mix",
    )(combine, back)


def local(tokens, slot_keys, w_in, w_out):
    seq = lax.axis_size("seq")
    expert = lax.axis_size("expert")
    group = ("seq", "expert")
    slots = slot_keys.shape[1]
    width = tokens.shape[1]
    own = slots // expert

    logits = full_logits(tokens, slot_keys)
    top = jnp.max(logits, axis=1)
    dispatch = jnp.exp(logits - top[:, None]).astype(BF16)
    combine = jax.nn.softmax(logits, axis=0).astype(BF16)
    totals = jnp.sum(dispatch.astype(F32), axis=1)
    weighted = jnp.dot(dispatch, tokens, preferred_element_type=F32)
    mean = (weighted / totals[:, None]).astype(BF16)
    weight = jnp.stack(spread(top + jnp.log(totals)), axis=1).astype(BF16)
    weight = jnp.pad(weight, ((0, 0), (0, LANES - weight.shape[1])))
    send = jnp.concatenate([mean, weight], axis=1).reshape(1, expert, own, width + LANES)
    send = jnp.broadcast_to(send, (seq, expert, own, width + LANES))
    got = lax.all_to_all(send.reshape(seq * expert, own, width + LANES), group, 0, 0)

    back = experts(got, w_in, w_out, seq, expert)
    back = lax.all_to_all(back, group, 0, 0)
    return mix(combine, back, seq, expert)


def solution(mesh):
    return jax.shard_map(
        local,
        mesh=mesh,
        in_specs=(
            P(("clip", "seq"), "expert"),
            P("expert", None),
            P("expert", None, "seq"),
            P("expert", "seq", None),
        ),
        out_specs=P(("clip", "seq"), "expert"),
        check_vma=False,
    )
```

time: 83.4 us -> 81.9 us (0.982)
  matrix products: 8.3 us -> 1.88 us
  Pallas kernels: 0 us -> 5.91 us
  waiting for transfers between devices: 14.3 us -> 9.05 us
  local copies, waits for them, and re-layouts: 2.19 us -> 6.24 us
    dot_general x3 -> x0, matrix products: 6.41 us -> none  [the longest x1 2.99 us: local(): inner = jnp.einsum('ed,edf->ef', slot_in, w_in, preferred_element_type=F32)]
    pallas_call x0 -> x2, Pallas kernels: none -> 5.91 us  [the longest x1 4.49 us: mix(): pl.pallas_call(kernel, grid=(count // BLOCK,), out_shape=jax.ShapeDtypeSt...]
    ppermute x3, waiting for transfers between devices: 14.3 us -> 9.05 us  [swap(): return lax.ppermute(value, 'expert', pairs)]
    unnamed x5 -> x6, local copies, waits for them, and re-layouts: 1.94 us -> 5.97 us
where the time goes in v2:
time: 81.9 us; the launch traced here: 81.6 us
  blocking collectives  49.2 us (60%)
  waiting for transfers between devices  9.05 us (11%)
  starting transfers between devices  7.88 us (10%)
  local copies, waits for them, and re-layouts  6.24 us (8%)
  Pallas kernels  5.91 us (7%)
  matrix products  1.88 us (2%)
  other arithmetic  1.33 us (2%)
    all_to_all x1, blocking collectives, local(): lax.all_to_all(send.reshape(seq * expert, own, width + LANES), group, 0, 0)  31.2 us
    all_to_all x1, blocking collectives, local(): back = lax.all_to_all(back, group, 0, 0)  18 us
    ppermute x3, waiting for transfers between devices, swap(): return lax.ppermute(value, 'expert', pairs)  9.05 us
    ppermute x3, starting transfers between devices, swap(): return lax.ppermute(value, 'expert', pairs)  7.88 us
    unnamed x6, local copies, waits for them, and re-layouts  5.97 us
    pallas_call x1, Pallas kernels, mix(): pl.pallas_call(kernel, grid=(count // BLOCK,), out_shape=jax.ShapeDtypeSt...  4.49 us
  transfers between devices with their start and end apart: 3, of which 3 were waited for; matrix products, arithmetic and copies ran while one was open for 0% of the time, Pallas kernels for 0%

profile of v2, /device:TPU:33, one launch (start us, length us, event | category | flops | bytes accessed | tf_op | source)
XLA Modules:
  0.0 81.6 jit_solution(10962540264176856490)
XLA Ops:
  0.0 1.6 %copy-done = bf16[4096,256]{1,0:T(8,128)(2,1)S(1)} copy-done((bf16[4096,256]{1,0:T(8,128)(2,1)S(1)}, bf16[4096,256]{1,0:T(8,128)(2,1)}, u32[]{:S(2)}) %copy-start) | copy-done | bytes 2097176
  1.6 1.4 %fusion.17 = f32[32,4096]{1,0:T(8,128)S(1)} fusion(bf16[256,32]{0,1:T(8,128)(2,1)} %param.5, bf16[4096,256]{1,0:T(8,128)(2,1)S(1)} %copy-done), kind=kOutput, calls=%fused_computation.51 | convolution fusion | flops 67108864 | bytes 2637824 | tf_op jit(solution)/shard_map/dot_general | solution.py:48
  3.1 0.8 collective-permute-start
  3.8 1.2 %collective-permute-done = f32[32,2048]{1,0:T(8,128)S(1)} collective-permute-done((f32[32,2048]{1,0:T(8,128)S(1)}, f32[32,2048]{1,0:T(8,128)S(1)}, u32[]{:S(2)}, u32[]{:S(2)}) %collective-permute-start) | collective-permute-done | bytes 262176 | tf_op jit(solution)/shard_map/ppermute | solution.py:19
  5.0 0.2 fusion.14
  5.2 0.1 copy.11
  5.3 0.1 exponential_convert_fusion.1
  5.5 6.1 %collective-permute-start.1 = (bf16[32,2176]{1,0:T(8,128)(2,1)S(1)}, bf16[32,2176]{1,0:T(8,128)(2,1)S(1)}, u32[]{:S(2)}, u32[]{:S(2)}) collective-permute-start(bf16[32,2176]{1,0:T(8,128)(2,1)S(1)} %fusion.7), channel_id=1, source_target_pairs={{0,2},{1,3},{2,0},{3,1},{4,6},{5,7},{6,4},{7,5},{8,10},{9,11},{10,... | collective-permute-start | bytes 417800 | tf_op jit(solution)/shard_map/ppermute | solution.py:19
  11.6 6.7 %collective-permute-done.1 = bf16[32,2176]{1,0:T(8,128)(2,1)S(1)} collective-permute-done((bf16[32,2176]{1,0:T(8,128)(2,1)S(1)}, bf16[32,2176]{1,0:T(8,128)(2,1)S(1)}, u32[]{:S(2)}, u32[]{:S(2)}) %collective-permute-start.1) | collective-permute-done | bytes 139296 | tf_op jit(solution)/shard_map/ppermute | solution.py:19
  18.4 0.2 slice_reduce_fusion.1
  18.5 0.1 fusion.5
  18.7 1.0 %collective-permute-start.2 = (f32[32,2048]{1,0:T(8,128)S(1)}, f32[32,2048]{1,0:T(8,128)S(1)}, u32[]{:S(2)}, u32[]{:S(2)}) collective-permute-start(f32[32,2048]{1,0:T(8,128)S(1)} %fusion.5), channel_id=1, source_target_pairs={{0,1},{1,0},{2,3},{3,2},{4,5},{5,4},{6,7},{7,6},{8,9},{9,8},{10,11... | collective-permute-start | bytes 786440 | tf_op jit(solution)/shard_map/ppermute | solution.py:19
  19.7 1.2 %collective-permute-done.2 = f32[32,2048]{1,0:T(8,128)S(1)} collective-permute-done((f32[32,2048]{1,0:T(8,128)S(1)}, f32[32,2048]{1,0:T(8,128)S(1)}, u32[]{:S(2)}, u32[]{:S(2)}) %collective-permute-start.2) | collective-permute-done | bytes 262176 | tf_op jit(solution)/shard_map/ppermute | solution.py:19
  20.8 0.2 fusion.16
  21.0 0.1 fusion.1
  21.2 0.3 convert_reduce_fusion
  21.5 0.5 fusion
  22.0 0.1 copy.12
  22.1 31.2 %all_to_all.10.got_ref = bf16[64,8,384]{2,1,0:T(8,128)(2,1)S(1)} all-to-all(bf16[64,8,384]{2,1,0:T(8,128)(2,1)S(1)} %bitcast.28), channel_id=1, replica_groups=mesh['clip'=4,'seq'=16,'expert'=4] {'seq','expert'}, dimensions={0} | all-to-all | bytes 786432 | tf_op jit(solution)/shard_map/all_to_all | solution.py:183
  53.3 2.2 %copy-done.1 = bf16[8,1024,256]{2,1,0:T(8,128)(2,1)S(1)} copy-done((bf16[8,1024,256]{2,1,0:T(8,128)(2,1)S(1)}, bf16[8,1024,256]{2,1,0:T(8,128)(2,1)}, u32[]{:S(2)}) %copy-start.1) | copy-done | bytes 4194328
  55.5 2.2 %copy-done.2 = bf16[8,256,1024]{2,1,0:T(8,128)(2,1)S(1)} copy-done((bf16[8,256,1024]{2,1,0:T(8,128)(2,1)S(1)}, bf16[8,256,1024]{2,1,0:T(8,128)(2,1)}, u32[]{:S(2)}) %copy-start.2) | copy-done | bytes 4194328
  57.7 1.4 %experts.1 = bf16[64,8,256]{2,1,0:T(8,128)(2,1)S(1)} custom-call(bf16[64,8,384]{2,1,0:T(8,128)(2,1)S(1)} %all_to_all.10.got_ref, bf16[8,1024,256]{2,1,0:T(8,128)(2,1)S(1)} %copy-done.1, bf16[8,256,1024]{2,1,0:T(8,128)(2,1)S(1)} %copy-done.2), custom_call_target="tpu_custom_call" | custom-call | flops 67108864 | bytes 8388608 | tf_op jit(solution)/shard_map/experts/pallas_call | solution.py:104
  59.1 18.0 %all_to_all.11.back_ref = bf16[64,8,256]{2,1,0:T(8,128)(2,1)S(1)} all-to-all(bf16[64,8,256]{2,1,0:T(8,128)(2,1)S(1)} %experts.1), channel_id=1, replica_groups=mesh['clip'=4,'seq'=16,'expert'=4] {'seq','expert'}, dimensions={0} | all-to-all | bytes 524288 | tf_op jit(solution)/shard_map/all_to_all | solution.py:186
  77.1 4.5 %mix.1 = f32[4096,256]{1,0:T(8,128)} custom-call(bf16[32,4096]{1,0:T(8,128)(2,1)S(1)} %get-tuple-element.20.combine_ref, bf16[64,8,256]{2,1,0:T(8,128)(2,1)S(1)} %all_to_all.11.back_ref), custom_call_target="tpu_custom_call" | custom-call | flops 67108864 | bytes 4194304 | tf_op jit(solution)/shard_map/mix/pallas_call | solution.py:146
  (17 shorter events, 0.3 us)
Async XLA Ops:
  0.0 1.6 %copy-start = (bf16[4096,256]{1,0:T(8,128)(2,1)S(1)}, bf16[4096,256]{1,0:T(8,128)(2,1)}, u32[]{:S(2)}) copy-start(bf16[4096,256]{1,0:T(8,128)(2,1)} %param.4) | copy-start | bytes 6291460
  3.1 1.9 %collective-permute-start = (f32[32,2048]{1,0:T(8,128)S(1)}, f32[32,2048]{1,0:T(8,128)S(1)}, u32[]{:S(2)}, u32[]{:S(2)}) collective-permute-start(f32[32,2048]{1,0:T(8,128)S(1)} %slice_select_fusion), channel_id=1, source_target_pairs={{0,1},{1,0},{2,3},{3,2},{4,5},{5,4},{6,7},{7,6},{8,9},{9,8},{10,11... | collective-permute-start | bytes 786440 | tf_op jit(solution)/shard_map/ppermute | solution.py:19
  5.5 12.8 %collective-permute-start.1 = (bf16[32,2176]{1,0:T(8,128)(2,1)S(1)}, bf16[32,2176]{1,0:T(8,128)(2,1)S(1)}, u32[]{:S(2)}, u32[]{:S(2)}) collective-permute-start(bf16[32,2176]{1,0:T(8,128)(2,1)S(1)} %fusion.7), channel_id=1, source_target_pairs={{0,2},{1,3},{2,0},{3,1},{4,6},{5,7},{6,4},{7,5},{8,10},{9,11},{10,... | collective-permute-start | bytes 417800 | tf_op jit(solution)/shard_map/ppermute | solution.py:19
  18.7 2.2 %collective-permute-start.2 = (f32[32,2048]{1,0:T(8,128)S(1)}, f32[32,2048]{1,0:T(8,128)S(1)}, u32[]{:S(2)}, u32[]{:S(2)}) collective-permute-start(f32[32,2048]{1,0:T(8,128)S(1)} %fusion.5), channel_id=1, source_target_pairs={{0,1},{1,0},{2,3},{3,2},{4,5},{5,4},{6,7},{7,6},{8,9},{9,8},{10,11... | collective-permute-start | bytes 786440 | tf_op jit(solution)/shard_map/ppermute | solution.py:19
  53.3 2.2 %copy-start.1 = (bf16[8,1024,256]{2,1,0:T(8,128)(2,1)S(1)}, bf16[8,1024,256]{2,1,0:T(8,128)(2,1)}, u32[]{:S(2)}) copy-start(bf16[8,1024,256]{2,1,0:T(8,128)(2,1)} %w_in_ref.1) | copy-start | bytes 12582916
  55.5 2.2 %copy-start.2 = (bf16[8,256,1024]{2,1,0:T(8,128)(2,1)S(1)}, bf16[8,256,1024]{2,1,0:T(8,128)(2,1)}, u32[]{:S(2)}) copy-start(bf16[8,256,1024]{2,1,0:T(8,128)(2,1)} %w_out_ref.1) | copy-start | bytes 12582916

commit v3 on v2

--- a/solution.py
+++ b/solution.py
@@ -25,7 +25,7 @@
     return [first, second, value - first - second]
 
 
-def exchanged(scores):
+def exchanged(scores, w_in, w_out):
     high = jnp.max(scores, axis=1)
     low = jnp.min(scores, axis=1)
     center = 0.5 * (high + low)
@@ -34,28 +34,122 @@
     side = jnp.stack(spread(center) + spread(span), axis=1)
     side = jnp.pad(side, ((0, 0), (0, LANES - side.shape[1])))
     sent = jnp.concatenate([code, side], axis=1).astype(BF16)
-    got = swap(sent, 1, 0).astype(F32)
+    sent, w_in, w_out = lax.optimization_barrier((sent, w_in, w_out))
+    got = swap(sent, 1, 0)
+    w_in, w_out = staged(w_in, w_out)
+    got, w_in, w_out = lax.optimization_barrier((got, w_in, w_out))
+    got = got.astype(F32)
     count = scores.shape[1]
     center = jnp.sum(got[:, count : count + 3], axis=1, keepdims=True)
     span = jnp.sum(got[:, count + 3 : count + 6], axis=1, keepdims=True)
-    return jnp.log2(got[:, :count]) * (span / (2 * REACH)) + center
-
-
-def full_logits(tokens, slot_keys):
-    count = tokens.shape[0]
+    return jnp.log2(got[:, :count]) * (span / (2 * REACH)) + center, w_in, w_out
+
+
+def scores(tokens, slot_keys):
+    count, width = tokens.shape
+    slots = slot_keys.shape[1]
     half = count // 2
+    steps = half // BLOCK
+
+    def kernel(keys_hbm, tokens_ref, theirs_ref, mine_ref, held_ref, keys_ref, sems):
+        core = lax.axis_index("expert") % 2
+
+        def rows(step):
+            start = (1 - core) * half if step < steps else core * half
+            return pl.ds(pl.multiple_of(start + (step % steps) * BLOCK, BLOCK), BLOCK)
+
+        def copy(step):
+            return pltpu.make_async_copy(
+                tokens_ref.at[rows(step)], held_ref.at[rows(step)], sems.at[step]
+            )
+
+        keys = pltpu.make_async_copy(keys_hbm, keys_ref, sems.at[2 * steps])
+        keys.start()
+        for step in range(2 * steps):
+            copy(step).start()
+        keys.wait()
+        for step in range(2 * steps):
+            copy(step).wait()
+            part = lax.dot_general(
+                keys_ref[...],
+                held_ref[rows(step)],
+                (((1,), (1,)), ((), ())),
+                preferred_element_type=F32,
+            )
+            target = theirs_ref if step < steps else mine_ref
+            target[:, (step % steps) * BLOCK : (step % steps + 1) * BLOCK] = part
+
+    whole = pl.BlockSpec(memory_space=pltpu.VMEM)
+    return pl.pallas_call(
+        kernel,
+        out_shape=(
+            jax.ShapeDtypeStruct((slots, half), F32),
+            jax.ShapeDtypeStruct((slots, half), F32),
+            pltpu.VMEM((count, width), BF16),
+        ),
+        in_specs=[pl.BlockSpec(memory_space=pltpu.HBM)] * 2,
+        out_specs=(whole, whole, whole),
+        scratch_shapes=[
+            pltpu.VMEM((slots, width), BF16),
+            pltpu.SemaphoreType.DMA((2 * steps + 1,)),
+        ],
+        compiler_params=pltpu.CompilerParams(vmem_limit_bytes=16 * 2**20),
+        cost_estimate=pl.CostEstimate(
+            flops=2 * slots * count * width, bytes_accessed=2 * count * width, transcendentals=0
+        ),
+        name="scores",
+    )(
+        pltpu.with_memory_space_constraint(slot_keys.T, pltpu.HBM),
+        pltpu.with_memory_space_constraint(tokens, pltpu.HBM),
+    )
+
+
+def staged(first, second):
+    pieces = first.shape[0]
+
+    def kernel(first_ref, second_ref, first_out, second_out, sems):
+        copies = []
+        for i in range(pieces):
+            copies.append(
+                pltpu.make_async_copy(first_ref.at[i], first_out.at[i], sems.at[0, i])
+            )
+            copies.append(
+                pltpu.make_async_copy(second_ref.at[i], second_out.at[i], sems.at[1, i])
+            )
+        for item in copies:
+            item.start()
+        for item in copies:
+            item.wait()
+
+    outside = pl.BlockSpec(memory_space=pltpu.HBM)
+    whole = pl.BlockSpec(memory_space=pltpu.VMEM)
+    return pl.pallas_call(
+        kernel,
+        out_shape=(pltpu.VMEM(first.shape, first.dtype), pltpu.VMEM(second.shape, second.dtype)),
+        in_specs=[outside, outside],
+        out_specs=(whole, whole),
+        scratch_shapes=[pltpu.SemaphoreType.DMA((2, pieces))],
+        compiler_params=pltpu.CompilerParams(vmem_limit_bytes=16 * 2**20),
+        cost_estimate=pl.CostEstimate(
+            flops=0, bytes_accessed=4 * (first.size + second.size), transcendentals=0
+        ),
+        name="staged",
+    )(
+        pltpu.with_memory_space_constraint(first, pltpu.HBM),
+        pltpu.with_memory_space_constraint(second, pltpu.HBM),
+    )
+
+
+def full_logits(theirs, mine, w_in, w_out):
     core = lax.axis_index("expert") % 2
-    partial = lax.dot_general(
-        slot_keys, tokens, (((0,), (1,)), ((), ())), preferred_element_type=F32
-    )
-    theirs = jnp.where(core == 0, partial[:, half:], partial[:, :half])
-    mine = jnp.where(core == 0, partial[:, :half], partial[:, half:])
     mine = mine + swap(theirs, 0, 1)
-    mine = mine + exchanged(mine)
+    gained, w_in, w_out = exchanged(mine, w_in, w_out)
+    mine = mine + gained
     other = swap(mine, 0, 1)
-    return jnp.concatenate(
+    logits = jnp.concatenate(
         [jnp.where(core == 0, mine, other), jnp.where(core == 0, other, mine)], axis=1
     )
+    return logits, w_in, w_out
 
 
 def experts(got, w_in, w_out, seq, expert):
@@ -120,47 +214,6 @@
     )
 
 
-def mix(combine, back, seq, expert):
-    slots, count = combine.shape
-    width = back.shape[2]
-    own = slots // expert
-
-    def kernel(combine_ref, back_ref, out_ref, table):
-        @pl.when(pl.program_id(0) == 0)
-        def _():
-            parts = []
-            for e in range(expert):
-                total = jnp.zeros((own, width), F32)
-                for s in range(seq):
-                    total += back_ref[s * expert + e].astype(F32)
-                parts.append(total)
-            table[...] = jnp.concatenate(parts, axis=0).astype(BF16)
-
-        out_ref[...] = lax.dot_general(
-            combine_ref[...],
-            table[...],
-            (((0,), (0,)), ((), ())),
-            preferred_element_type=F32,
-        )
-
-    return pl.pallas_call(
-        kernel,
-        grid=(count // BLOCK,),
-        out_shape=jax.ShapeDtypeStruct((count, width), F32),
-        in_specs=[
-            pl.BlockSpec((slots, BLOCK), lambda i: (0, i)),
-            pl.BlockSpec(back.shape, lambda i: (0, 0, 0)),
-        ],
-        out_specs=pl.BlockSpec((BLOCK, width), lambda i: (i, 0)),
-        scratch_shapes=[pltpu.VMEM((slots, width), BF16)],
-        compiler_params=pltpu.CompilerParams(vmem_limit_bytes=16 * 2**20),
-        cost_estimate=pl.CostEstimate(
-            flops=2 * slots * count * width, bytes_accessed=4 * count * width, transcendentals=0
-        ),
-        name="mix",
-    )(combine, back)
-
-
 def local(tokens, slot_keys, w_in, w_out):
     seq = lax.axis_size("seq")
     expert = lax.axis_size("expert")
@@ -169,7 +222,8 @@
     width = tokens.shape[1]
     own = slots // expert
 
-    logits = full_logits(tokens, slot_keys)
+    theirs, mine, tokens = scores(tokens, slot_keys)
+    logits, w_in, w_out = full_logits(theirs, mine, w_in, w_out)
     top = jnp.max(logits, axis=1)
     dispatch = jnp.exp(logits - top[:, None]).astype(BF16)
     combine = jax.nn.softmax(logits, axis=0).astype(BF16)
@@ -184,7 +238,10 @@
 
     back = experts(got, w_in, w_out, seq, expert)
     back = lax.all_to_all(back, group, 0, 0)
-    return mix(combine, back, seq, expert)
+    returned = jnp.sum(back.reshape(seq, slots, width).astype(F32), axis=0).astype(BF16)
+    return lax.dot_general(
+        combine, returned, (((0,), (0,)), ((), ())), preferred_element_type=F32
+    )
 
 
 def solution(mesh):

time: 81.9 us -> 79.5 us (0.971)
  waiting for transfers between devices: 9.05 us -> 2.33 us
  local copies, waits for them, and re-layouts: 6.24 us -> 8.58 us
  Pallas kernels: 5.91 us -> 7.48 us
  matrix products: 1.88 us -> 3.24 us
    ppermute x3, waiting for transfers between devices: 9.05 us -> 2.33 us  [swap(): return lax.ppermute(value, 'expert', pairs)]
    unnamed x6 -> x8, local copies, waits for them, and re-layouts: 5.97 us -> 8.31 us
    pallas_call x1 -> x2, Pallas kernels: 4.49 us -> 6.07 us  [the longest x1 3.51 us: staged(): pl.pallas_call(kernel, out_shape=(pltpu.VMEM(first.shape, first.dtype), p...]
    dot_general x1, matrix products: 1.42 us -> 2.78 us  [local(): lax.dot_general(combine, returned, (((0,), (0,)), ((), ())), preferred_el...]
  transfers between devices with their start and end apart: 3 -> 3, of which waited for: 3 -> 2; matrix products, arithmetic and copies ran while one was open for 0% -> 0% of each run, Pallas kernels for 0% -> 4%
where the time goes in v3:
time: 79.5 us; the launch traced here: 79.3 us
  blocking collectives  48.8 us (61%)
  local copies, waits for them, and re-layouts  8.58 us (11%)
  starting transfers between devices  7.6 us (10%)
  Pallas kernels  7.48 us (9%)
  matrix products  3.24 us (4%)
  waiting for transfers between devices  2.33 us (3%)
  other arithmetic  1.19 us (1%)
    all_to_all x1, blocking collectives, local(): lax.all_to_all(send.reshape(seq * expert, own, width + LANES), group, 0, 0)  30.8 us
    all_to_all x1, blocking collectives, local(): back = lax.all_to_all(back, group, 0, 0)  18 us
    unnamed x8, local copies, waits for them, and re-layouts  8.31 us
    ppermute x3, starting transfers between devices, swap(): return lax.ppermute(value, 'expert', pairs)  7.6 us
    pallas_call x1, Pallas kernels, staged(): pl.pallas_call(kernel, out_shape=(pltpu.VMEM(first.shape, first.dtype), p...  3.51 us
    dot_general x1, matrix products, local(): lax.dot_general(combine, returned, (((0,), (0,)), ((), ())), preferred_el...  2.78 us
    pallas_call x1, Pallas kernels, scores(): pl.pallas_call(kernel, out_shape=(jax.ShapeDtypeStruct((slots, half), F32...  2.56 us
    ppermute x3, waiting for transfers between devices, swap(): return lax.ppermute(value, 'expert', pairs)  2.33 us
  transfers between devices with their start and end apart: 3, of which 2 were waited for; matrix products, arithmetic and copies ran while one was open for 0% of the time, Pallas kernels for 4%

profile of v3, /device:TPU:33, one launch (start us, length us, event | category | flops | bytes accessed | tf_op | source)
XLA Modules:
  0.0 79.3 jit_solution(7345906235292304426)
XLA Ops:
  0.0 2.6 %scores.1 = (f32[32,2048]{1,0:T(8,128)S(1)}, f32[32,2048]{1,0:T(8,128)S(1)}, bf16[4096,256]{1,0:T(8,128)(2,1)S(1)}) custom-call(bf16[32,256]{1,0:T(8,128)(2,1)} %bitcast.33, bf16[4096,256]{1,0:T(8,128)(2,1)} %tokens_ref.1), custom_call_target="tpu_custom_call" | custom-call | flops 67108864 | bytes 2097152 | tf_op jit(solution)/shard_map/scores/pallas_call | solution.py:83
  2.6 0.8 collective-permute-start
  3.3 1.2 %collective-permute-done = f32[32,2048]{1,0:T(8,128)S(1)} collective-permute-done((f32[32,2048]{1,0:T(8,128)S(1)}, f32[32,2048]{1,0:T(8,128)S(1)}, u32[]{:S(2)}, u32[]{:S(2)}) %collective-permute-start) | collective-permute-done | bytes 262176 | tf_op jit(solution)/shard_map/ppermute | solution.py:19
  4.5 0.2 fusion.18
  4.7 0.1 copy.11
  4.8 0.1 exponential_convert_fusion.1
  5.0 6.1 %collective-permute-start.1 = (bf16[32,2176]{1,0:T(8,128)(2,1)S(1)}, bf16[32,2176]{1,0:T(8,128)(2,1)S(1)}, u32[]{:S(2)}, u32[]{:S(2)}) collective-permute-start(bf16[32,2176]{1,0:T(8,128)(2,1)S(1)} %fusion.10), channel_id=1, source_target_pairs={{0,2},{1,3},{2,0},{3,1},{4,6},{5,7},{6,4},{7,5},{8,10},{9,11},{10,... | collective-permute-start | bytes 417800 | tf_op jit(solution)/shard_map/ppermute | solution.py:19
  11.1 3.5 %staged.1 = (bf16[8,1024,256]{2,1,0:T(8,128)(2,1)S(1)}, bf16[8,256,1024]{2,1,0:T(8,128)(2,1)S(1)}) custom-call(bf16[8,1024,256]{2,1,0:T(8,128)(2,1)} %first_ref, bf16[8,256,1024]{2,1,0:T(8,128)(2,1)} %second_ref), custom_call_target="tpu_custom_call" | custom-call | bytes 16777216 | tf_op jit(solution)/shard_map/staged/pallas_call | solution.py:126
  14.6 2.0 %copy-done = bf16[8,1024,256]{2,1,0:T(8,128)(2,1)} copy-done((bf16[8,1024,256]{2,1,0:T(8,128)(2,1)}, bf16[8,1024,256]{2,1,0:T(8,128)(2,1)S(1)}, u32[]{:S(2)}) %copy-start) | copy-done | bytes 4194328
  16.6 1.9 %copy-done.2 = bf16[8,256,1024]{2,1,0:T(8,128)(2,1)} copy-done((bf16[8,256,1024]{2,1,0:T(8,128)(2,1)}, bf16[8,256,1024]{2,1,0:T(8,128)(2,1)S(1)}, u32[]{:S(2)}) %copy-start.2) | copy-done | bytes 4194328
  18.6 0.2 slice_reduce_fusion.1
  18.8 0.1 fusion.6
  18.9 0.7 collective-permute-start.2
  19.6 1.2 %collective-permute-done.2 = f32[32,2048]{1,0:T(8,128)S(1)} collective-permute-done((f32[32,2048]{1,0:T(8,128)S(1)}, f32[32,2048]{1,0:T(8,128)S(1)}, u32[]{:S(2)}, u32[]{:S(2)}) %collective-permute-start.2) | collective-permute-done | bytes 262176 | tf_op jit(solution)/shard_map/ppermute | solution.py:19
  20.8 0.2 fusion.19
  21.0 0.3 convert_reduce_fusion
  21.3 0.1 copy.12
  21.4 0.5 fusion
  21.9 30.8 %all_to_all.10.got_ref = bf16[64,8,384]{2,1,0:T(8,128)(2,1)S(1)} all-to-all(bf16[64,8,384]{2,1,0:T(8,128)(2,1)S(1)} %bitcast.31), channel_id=1, replica_groups=mesh['clip'=4,'seq'=16,'expert'=4] {'seq','expert'}, dimensions={0} | all-to-all | bytes 786432 | tf_op jit(solution)/shard_map/all_to_all | solution.py:237
  52.7 2.2 %copy-done.1 = bf16[8,1024,256]{2,1,0:T(8,128)(2,1)S(1)} copy-done((bf16[8,1024,256]{2,1,0:T(8,128)(2,1)S(1)}, bf16[8,1024,256]{2,1,0:T(8,128)(2,1)}, u32[]{:S(2)}) %copy-start.1) | copy-done | bytes 4194328
  54.9 2.2 %copy-done.3 = bf16[8,256,1024]{2,1,0:T(8,128)(2,1)S(1)} copy-done((bf16[8,256,1024]{2,1,0:T(8,128)(2,1)S(1)}, bf16[8,256,1024]{2,1,0:T(8,128)(2,1)}, u32[]{:S(2)}) %copy-start.3) | copy-done | bytes 4194328
  57.1 1.4 %experts.1 = bf16[64,8,256]{2,1,0:T(8,128)(2,1)S(1)} custom-call(bf16[64,8,384]{2,1,0:T(8,128)(2,1)S(1)} %all_to_all.10.got_ref, bf16[8,1024,256]{2,1,0:T(8,128)(2,1)S(1)} %copy-done.1, bf16[8,256,1024]{2,1,0:T(8,128)(2,1)S(1)} %copy-done.3), custom_call_target="tpu_custom_call" | custom-call | flops 67108864 | bytes 8388608 | tf_op jit(solution)/shard_map/experts/pallas_call | solution.py:198
  58.5 18.0 %all_to_all.11 = bf16[64,8,256]{2,1,0:T(8,128)(2,1)S(1)} all-to-all(bf16[64,8,256]{2,1,0:T(8,128)(2,1)S(1)} %experts.1), channel_id=1, replica_groups=mesh['clip'=4,'seq'=16,'expert'=4] {'seq','expert'}, dimensions={0} | all-to-all | bytes 524288 | tf_op jit(solution)/shard_map/all_to_all | solution.py:240
  76.5 2.8 %fusion.3 = f32[4096,256]{1,0:T(8,128)} fusion(bf16[32,256]{1,0:T(8,128)(2,1)S(1)} %bitcast_reduce_fusion, f32[4096]{0:T(1024)S(1)} %get-tuple-element.42, f32[4096]{0:T(1024)S(1)} %fusion.9, f32[32,2048]{1,0:T(8,128)S(1)} %get-tuple-element.34, f32[32,2048]{1,0:T(8,128)S(1)} %get-tuple-element.44), kind=kOutput, calls=%fused_computation.10 | convolution fusion | flops 67633152 | bytes 4767744 | tf_op jit(solution)/shard_map/dot_general | solution.py:242
  (19 shorter events, 0.3 us)
Async XLA Ops:
  2.6 1.9 %collective-permute-start = (f32[32,2048]{1,0:T(8,128)S(1)}, f32[32,2048]{1,0:T(8,128)S(1)}, u32[]{:S(2)}, u32[]{:S(2)}) collective-permute-start(f32[32,2048]{1,0:T(8,128)S(1)} %get-tuple-element.17), channel_id=1, source_target_pairs={{0,1},{1,0},{2,3},{3,2},{4,5},{5,4},{6,7},{7,6},{8,9},{9,8},{10,11... | collective-permute-start | bytes 786440 | tf_op jit(solution)/shard_map/ppermute | solution.py:19
  5.0 13.6 %collective-permute-start.1 = (bf16[32,2176]{1,0:T(8,128)(2,1)S(1)}, bf16[32,2176]{1,0:T(8,128)(2,1)S(1)}, u32[]{:S(2)}, u32[]{:S(2)}) collective-permute-start(bf16[32,2176]{1,0:T(8,128)(2,1)S(1)} %fusion.10), channel_id=1, source_target_pairs={{0,2},{1,3},{2,0},{3,1},{4,6},{5,7},{6,4},{7,5},{8,10},{9,11},{10,... | collective-permute-start | bytes 417800 | tf_op jit(solution)/shard_map/ppermute | solution.py:19
  14.6 2.0 %copy-start = (bf16[8,1024,256]{2,1,0:T(8,128)(2,1)}, bf16[8,1024,256]{2,1,0:T(8,128)(2,1)S(1)}, u32[]{:S(2)}) copy-start(bf16[8,1024,256]{2,1,0:T(8,128)(2,1)S(1)} %get-tuple-element.25.w_in_ref) | copy-start | bytes 12582916
  16.6 1.9 %copy-start.2 = (bf16[8,256,1024]{2,1,0:T(8,128)(2,1)}, bf16[8,256,1024]{2,1,0:T(8,128)(2,1)S(1)}, u32[]{:S(2)}) copy-start(bf16[8,256,1024]{2,1,0:T(8,128)(2,1)S(1)} %get-tuple-element.26.w_out_ref) | copy-start | bytes 12582916
  18.9 1.9 %collective-permute-start.2 = (f32[32,2048]{1,0:T(8,128)S(1)}, f32[32,2048]{1,0:T(8,128)S(1)}, u32[]{:S(2)}, u32[]{:S(2)}) collective-permute-start(f32[32,2048]{1,0:T(8,128)S(1)} %fusion.6), channel_id=1, source_target_pairs={{0,1},{1,0},{2,3},{3,2},{4,5},{5,4},{6,7},{7,6},{8,9},{9,8},{10,11... | collective-permute-start | bytes 786440 | tf_op jit(solution)/shard_map/ppermute | solution.py:19
  52.7 2.2 %copy-start.1 = (bf16[8,1024,256]{2,1,0:T(8,128)(2,1)S(1)}, bf16[8,1024,256]{2,1,0:T(8,128)(2,1)}, u32[]{:S(2)}) copy-start(bf16[8,1024,256]{2,1,0:T(8,128)(2,1)} %copy-done) | copy-start | bytes 12582916
  54.9 2.2 %copy-start.3 = (bf16[8,256,1024]{2,1,0:T(8,128)(2,1)S(1)}, bf16[8,256,1024]{2,1,0:T(8,128)(2,1)}, u32[]{:S(2)}) copy-start(bf16[8,256,1024]{2,1,0:T(8,128)(2,1)} %copy-done.2) | copy-start | bytes 12582916

commit v4 on v3

--- a/solution.py
+++ b/solution.py
@@ -10,6 +10,7 @@
 LANES = 128
 REACH = 125.0
 BLOCK = 512
+LIMIT = 16 * 2**20
 
 
 def swap(value, z_step, core_step):
@@ -19,30 +20,112 @@
     return lax.ppermute(value, "expert", pairs)
 
 
-def spread(value):
-    first = lax.reduce_precision(value, 8, 7)
-    second = lax.reduce_precision(value - first, 8, 7)
-    return [first, second, value - first - second]
-
-
-def exchanged(scores, w_in, w_out):
-    high = jnp.max(scores, axis=1)
-    low = jnp.min(scores, axis=1)
-    center = 0.5 * (high + low)
-    span = jnp.maximum(high - low, 1e-30)
-    code = jnp.exp2((scores - center[:, None]) * (2 * REACH / span)[:, None])
-    side = jnp.stack(spread(center) + spread(span), axis=1)
-    side = jnp.pad(side, ((0, 0), (0, LANES - side.shape[1])))
-    sent = jnp.concatenate([code, side], axis=1).astype(BF16)
-    sent, w_in, w_out = lax.optimization_barrier((sent, w_in, w_out))
-    got = swap(sent, 1, 0)
-    w_in, w_out = staged(w_in, w_out)
-    got, w_in, w_out = lax.optimization_barrier((got, w_in, w_out))
-    got = got.astype(F32)
-    count = scores.shape[1]
-    center = jnp.sum(got[:, count : count + 3], axis=1, keepdims=True)
-    span = jnp.sum(got[:, count + 3 : count + 6], axis=1, keepdims=True)
-    return jnp.log2(got[:, :count]) * (span / (2 * REACH)) + center, w_in, w_out
+def spread(value, lane, first):
+    high = value.astype(BF16).astype(F32)
+    middle = (value - high).astype(BF16).astype(F32)
+    low = value - high - middle
+    parts = jnp.where(lane == first, high, 0.0)
+    parts = jnp.where(lane == first + 1, middle, parts)
+    return jnp.where(lane == first + 2, low, parts)
+
+
+def call(kernel, name, out_shape, inputs, flops=0, scratch=()):
+    whole = pl.BlockSpec(memory_space=pltpu.VMEM)
+    moved = sum(a.size * a.dtype.itemsize for a in inputs)
+    return pl.pallas_call(
+        kernel,
+        out_shape=out_shape,
+        in_specs=[whole] * len(inputs),
+        out_specs=jax.tree.map(lambda _: whole, out_shape),
+        scratch_shapes=scratch,
+        compiler_params=pltpu.CompilerParams(vmem_limit_bytes=LIMIT),
+        cost_estimate=pl.CostEstimate(flops=flops, bytes_accessed=moved, transcendentals=0),
+        name=name,
+    )(*inputs)
+
+
+def encode(mine, gained):
+    slots, count = mine.shape
+
+    def kernel(mine_ref, gained_ref, total_ref, code_ref):
+        total = mine_ref[...] + gained_ref[...]
+        total_ref[...] = total
+        high = jnp.max(total, axis=1, keepdims=True)
+        low = jnp.min(total, axis=1, keepdims=True)
+        center = 0.5 * (high + low)
+        span = jnp.maximum(high - low, 1e-30)
+        code = jnp.exp2((total - center) * (2 * REACH / span))
+        code_ref[:, :count] = code.astype(BF16)
+        lane = lax.broadcasted_iota(jnp.int32, (slots, LANES), 1)
+        side = spread(center, lane, 0) + spread(span, lane, 3)
+        code_ref[:, count:] = side.astype(BF16)
+
+    return call(
+        kernel,
+        "encode",
+        (
+            jax.ShapeDtypeStruct((slots, count), F32),
+            jax.ShapeDtypeStruct((slots, count + LANES), BF16),
+        ),
+        (mine, gained),
+    )
+
+
+def decode(total, code):
+    slots, count = total.shape
+
+    def kernel(total_ref, code_ref, out_ref):
+        side = code_ref[:, count:].astype(F32)
+        lane = lax.broadcasted_iota(jnp.int32, (slots, LANES), 1)
+        center = jnp.sum(jnp.where(lane < 3, side, 0.0), axis=1, keepdims=True)
+        span = jnp.sum(jnp.where(lane < 3, 0.0, side), axis=1, keepdims=True)
+        power = jnp.log2(code_ref[:, :count].astype(F32))
+        out_ref[...] = total_ref[...] + (power * (span / (2 * REACH)) + center)
+
+    return call(
+        kernel, "decode", jax.ShapeDtypeStruct((slots, count), F32), (total, code)
+    )
+
+
+def weigh(mine, other, tokens, seq, expert):
+    slots, half = mine.shape
+    width = tokens.shape[1]
+    own = slots // expert
+
+    def kernel(mine_ref, other_ref, tokens_ref, send_ref, combine_ref):
+        core = lax.axis_index("expert") % 2
+        places = [
+            pl.ds(pl.multiple_of(start, half), half) for start in (core * half, (1 - core) * half)
+        ]
+        parts = [mine_ref[...], other_ref[...]]
+        top = jnp.max(jnp.maximum(parts[0], parts[1]), axis=1, keepdims=True)
+        totals = jnp.zeros((slots, 1), F32)
+        weighted = jnp.zeros((slots, width), F32)
+        for part, place in zip(parts, places):
+            dispatch = jnp.exp(part - top).astype(BF16)
+            totals += jnp.sum(dispatch.astype(F32), axis=1, keepdims=True)
+            weighted += jnp.dot(dispatch, tokens_ref[place, :], preferred_element_type=F32)
+            shifted = jnp.exp(part - jnp.max(part, axis=0, keepdims=True))
+            share = shifted / jnp.sum(shifted, axis=0, keepdims=True)
+            combine_ref[:, place] = share.astype(BF16)
+        lane = lax.broadcasted_iota(jnp.int32, (slots, LANES), 1)
+        weight = spread(top + jnp.log(totals), lane, 0)
+        block = jnp.concatenate([weighted / totals, weight], axis=1)
+        for e in range(expert):
+            piece = block[e * own : (e + 1) * own].astype(BF16)
+            for s in range(seq):
+                send_ref[s * expert + e] = piece
+
+    return call(
+        kernel,
+        "weigh",
+        (
+            jax.ShapeDtypeStruct((seq * expert, own, width + LANES), BF16),
+            jax.ShapeDtypeStruct((slots, 2 * half), BF16),
+        ),
+        (mine, other, tokens),
+        flops=4 * slots * half * width,
+    )
 
 
 def scores(tokens, slot_keys):
@@ -93,7 +176,7 @@
             pltpu.VMEM((slots, width), BF16),
             pltpu.SemaphoreType.DMA((2 * steps + 1,)),
         ],
-        compiler_params=pltpu.CompilerParams(vmem_limit_bytes=16 * 2**20),
+        compiler_params=pltpu.CompilerParams(vmem_limit_bytes=LIMIT),
         cost_estimate=pl.CostEstimate(
             flops=2 * slots * count * width, bytes_accessed=2 * count * width, transcendentals=0
         ),
@@ -129,7 +212,7 @@
         in_specs=[outside, outside],
         out_specs=(whole, whole),
         scratch_shapes=[pltpu.SemaphoreType.DMA((2, pieces))],
-        compiler_params=pltpu.CompilerParams(vmem_limit_bytes=16 * 2**20),
+        compiler_params=pltpu.CompilerParams(vmem_limit_bytes=LIMIT),
         cost_estimate=pl.CostEstimate(
             flops=0, bytes_accessed=4 * (first.size + second.size), transcendentals=0
         ),
@@ -138,18 +221,6 @@
         pltpu.with_memory_space_constraint(first, pltpu.HBM),
         pltpu.with_memory_space_constraint(second, pltpu.HBM),
     )
-
-
-def full_logits(theirs, mine, w_in, w_out):
-    core = lax.axis_index("expert") % 2
-    mine = mine + swap(theirs, 0, 1)
-    gained, w_in, w_out = exchanged(mine, w_in, w_out)
-    mine = mine + gained
-    other = swap(mine, 0, 1)
-    logits = jnp.concatenate(
-        [jnp.where(core == 0, mine, other), jnp.where(core == 0, other, mine)], axis=1
-    )
-    return logits, w_in, w_out
 
 
 def experts(got, w_in, w_out, seq, expert):
@@ -200,7 +271,7 @@
         out_shape=jax.ShapeDtypeStruct((seq * expert, own, width), BF16),
         in_specs=[whole, whole, whole],
         out_specs=whole,
-        compiler_params=pltpu.CompilerParams(vmem_limit_bytes=24 * 2**20),
+        compiler_params=pltpu.CompilerParams(vmem_limit_bytes=LIMIT),
         cost_estimate=pl.CostEstimate(
             flops=4 * own * width * expert * hidden_width * own,
             bytes_accessed=2 * (w_in.size + w_out.size),
@@ -220,22 +291,16 @@
     group = ("seq", "expert")
     slots = slot_keys.shape[1]
     width = tokens.shape[1]
-    own = slots // expert
 
     theirs, mine, tokens = scores(tokens, slot_keys)
-    logits, w_in, w_out = full_logits(theirs, mine, w_in, w_out)
-    top = jnp.max(logits, axis=1)
-    dispatch = jnp.exp(logits - top[:, None]).astype(BF16)
-    combine = jax.nn.softmax(logits, axis=0).astype(BF16)
-    totals = jnp.sum(dispatch.astype(F32), axis=1)
-    weighted = jnp.dot(dispatch, tokens, preferred_element_type=F32)
-    mean = (weighted / totals[:, None]).astype(BF16)
-    weight = jnp.stack(spread(top + jnp.log(totals)), axis=1).astype(BF16)
-    weight = jnp.pad(weight, ((0, 0), (0, LANES - weight.shape[1])))
-    send = jnp.concatenate([mean, weight], axis=1).reshape(1, expert, own, width + LANES)
-    send = jnp.broadcast_to(send, (seq, expert, own, width + LANES))
-    got = lax.all_to_all(send.reshape(seq * expert, own, width + LANES), group, 0, 0)
-
+    mine, sent = encode(mine, swap(theirs, 0, 1))
+    sent, w_in, w_out = lax.optimization_barrier((sent, w_in, w_out))
+    got = swap(sent, 1, 0)
+    w_in, w_out = staged(w_in, w_out)
+    got, w_in, w_out = lax.optimization_barrier((got, w_in, w_out))
+    mine = decode(mine, got)
+    send, combine = weigh(mine, swap(mine, 0, 1), tokens, seq, expert)
+    got = lax.all_to_all(send, group, 0, 0)
     back = experts(got, w_in, w_out, seq, expert)
     back = lax.all_to_all(back, group, 0, 0)
     returned = jnp.sum(back.reshape(seq, slots, width).astype(F32), axis=0).astype(BF16)

time: 79.5 us -> 74.1 us (0.932)
  local copies, waits for them, and re-layouts: 8.58 us -> 0 us
  waiting for transfers between devices: 2.33 us -> 5.54 us
  other arithmetic: 1.19 us -> 0.04 us
  Pallas kernels: 7.48 us -> 8.44 us
    unnamed x8 -> x0, local copies, waits for them, and re-layouts: 8.31 us -> none
    ppermute x3, waiting for transfers between devices: 2.33 us -> 5.54 us  [swap(): return lax.ppermute(value, 'expert', pairs)]
    pallas_call x0 -> x3, Pallas kernels: none -> 0.96 us  [call(): pl.pallas_call(kernel, out_shape=out_shape, in_specs=[whole] * len(inputs...]
  transfers between devices with their start and end apart: 3 -> 3, of which waited for: 2 -> 3; matrix products, arithmetic and copies ran while one was open for 0% -> 0% of each run, Pallas kernels for 4% -> 5%
where the time goes in v4:
time: 74.1 us; the launch traced here: 73.9 us
  blocking collectives  49.2 us (66%)
  Pallas kernels  8.44 us (11%)
  starting transfers between devices  7.88 us (11%)
  waiting for transfers between devices  5.54 us (7%)
  matrix products  2.77 us (4%)
    all_to_all x1, blocking collectives, local(): got = lax.all_to_all(send, group, 0, 0)  31.2 us
    all_to_all x1, blocking collectives, local(): back = lax.all_to_all(back, group, 0, 0)  18 us
    ppermute x3, starting transfers between devices, swap(): return lax.ppermute(value, 'expert', pairs)  7.88 us
    ppermute x3, waiting for transfers between devices, swap(): return lax.ppermute(value, 'expert', pairs)  5.54 us
    pallas_call x1, Pallas kernels, staged(): pl.pallas_call(kernel, out_shape=(pltpu.VMEM(first.shape, first.dtype), p...  3.51 us
    dot_general x1, matrix products, local(): lax.dot_general(combine, returned, (((0,), (0,)), ((), ())), preferred_el...  2.77 us
    pallas_call x1, Pallas kernels, scores(): pl.pallas_call(kernel, out_shape=(jax.ShapeDtypeStruct((slots, half), F32...  2.56 us
  transfers between devices with their start and end apart: 3, of which 3 were waited for; matrix products, arithmetic and copies ran while one was open for 0% of the time, Pallas kernels for 5%

profile of v4, /device:TPU:33, one launch (start us, length us, event | category | flops | bytes accessed | tf_op | source)
XLA Modules:
  0.0 73.9 jit_solution(8009414225567857170)
XLA Ops:
  0.0 2.6 %scores.1 = (f32[32,2048]{1,0:T(8,128)S(1)}, f32[32,2048]{1,0:T(8,128)S(1)}, bf16[4096,256]{1,0:T(8,128)(2,1)S(1)}) custom-call(bf16[32,256]{1,0:T(8,128)(2,1)} %bitcast.7, bf16[4096,256]{1,0:T(8,128)(2,1)} %tokens_ref.1), custom_call_target="tpu_custom_call" | custom-call | flops 67108864 | bytes 2097152 | tf_op jit(solution)/shard_map/scores/pallas_call | solution.py:166
  2.6 0.8 %collective-permute-start = (f32[32,2048]{1,0:T(8,128)S(1)}, f32[32,2048]{1,0:T(8,128)S(1)}, u32[]{:S(2)}, u32[]{:S(2)}) collective-permute-start(f32[32,2048]{1,0:T(8,128)S(1)} %get-tuple-element.21), channel_id=1, source_target_pairs={{0,1},{1,0},{2,3},{3,2},{4,5},{5,4},{6,7},{7,6},{8,9},{9,8},{10,11... | collective-permute-start | bytes 786440 | tf_op jit(solution)/shard_map/ppermute | solution.py:20
  3.3 1.2 %collective-permute-done.gained_ref = f32[32,2048]{1,0:T(8,128)S(1)} collective-permute-done((f32[32,2048]{1,0:T(8,128)S(1)}, f32[32,2048]{1,0:T(8,128)S(1)}, u32[]{:S(2)}, u32[]{:S(2)}) %collective-permute-start) | collective-permute-done | bytes 262176 | tf_op jit(solution)/shard_map/ppermute | solution.py:20
  4.5 0.2 encode.1
  4.7 6.1 %collective-permute-start.1 = (bf16[32,2176]{1,0:T(8,128)(2,1)S(1)}, bf16[32,2176]{1,0:T(8,128)(2,1)S(1)}, u32[]{:S(2)}, u32[]{:S(2)}) collective-permute-start(bf16[32,2176]{1,0:T(8,128)(2,1)S(1)} %get-tuple-element.24), channel_id=1, source_target_pairs={{0,2},{1,3},{2,0},{3,1},{4,6},{5,7},{6,4},{7,5},{8,10},{9,11},{10,... | collective-permute-start | bytes 417800 | tf_op jit(solution)/shard_map/ppermute | solution.py:20
  10.8 3.5 %staged.1 = (bf16[8,1024,256]{2,1,0:T(8,128)(2,1)S(1)}, bf16[8,256,1024]{2,1,0:T(8,128)(2,1)S(1)}) custom-call(bf16[8,1024,256]{2,1,0:T(8,128)(2,1)} %first_ref, bf16[8,256,1024]{2,1,0:T(8,128)(2,1)} %second_ref), custom_call_target="tpu_custom_call" | custom-call | bytes 16777216 | tf_op jit(solution)/shard_map/staged/pallas_call | solution.py:209
  14.3 3.2 %collective-permute-done.1.code_ref = bf16[32,2176]{1,0:T(8,128)(2,1)S(1)} collective-permute-done((bf16[32,2176]{1,0:T(8,128)(2,1)S(1)}, bf16[32,2176]{1,0:T(8,128)(2,1)S(1)}, u32[]{:S(2)}, u32[]{:S(2)}) %collective-permute-start.1) | collective-permute-done | bytes 139296 | tf_op jit(solution)/shard_map/ppermute | solution.py:20
  17.5 0.1 decode.1.mine_ref
  17.6 1.0 %collective-permute-start.2 = (f32[32,2048]{1,0:T(8,128)S(1)}, f32[32,2048]{1,0:T(8,128)S(1)}, u32[]{:S(2)}, u32[]{:S(2)}) collective-permute-start(f32[32,2048]{1,0:T(8,128)S(1)} %decode.1.mine_ref), channel_id=1, source_target_pairs={{0,1},{1,0},{2,3},{3,2},{4,5},{5,4},{6,7},{7,6},{8,9},{9,8},{10,11... | collective-permute-start | bytes 786440 | tf_op jit(solution)/shard_map/ppermute | solution.py:20
  18.6 1.2 %collective-permute-done.2.other_ref = f32[32,2048]{1,0:T(8,128)S(1)} collective-permute-done((f32[32,2048]{1,0:T(8,128)S(1)}, f32[32,2048]{1,0:T(8,128)S(1)}, u32[]{:S(2)}, u32[]{:S(2)}) %collective-permute-start.2) | collective-permute-done | bytes 262176 | tf_op jit(solution)/shard_map/ppermute | solution.py:20
  19.8 0.7 weigh.1
  20.5 31.2 %all_to_all.10.got_ref = bf16[64,8,384]{2,1,0:T(8,128)(2,1)S(1)} all-to-all(bf16[64,8,384]{2,1,0:T(8,128)(2,1)S(1)} %get-tuple-element.32), channel_id=1, replica_groups=mesh['clip'=4,'seq'=16,'expert'=4] {'seq','expert'}, dimensions={0} | all-to-all | bytes 786432 | tf_op jit(solution)/shard_map/all_to_all | solution.py:303
  51.7 1.4 %experts.1 = bf16[64,8,256]{2,1,0:T(8,128)(2,1)S(1)} custom-call(bf16[64,8,384]{2,1,0:T(8,128)(2,1)S(1)} %all_to_all.10.got_ref, bf16[8,1024,256]{2,1,0:T(8,128)(2,1)S(1)} %get-tuple-element.33.w_in_ref, bf16[8,256,1024]{2,1,0:T(8,128)(2,1)S(1)} %get-tuple-element.34.w_out_ref), custom_call_target="tpu_custom_call" | custom-call | flops 67108864 | bytes 8388608 | tf_op jit(solution)/shard_map/experts/pallas_call | solution.py:269
  53.1 18.0 %all_to_all.11 = bf16[64,8,256]{2,1,0:T(8,128)(2,1)S(1)} all-to-all(bf16[64,8,256]{2,1,0:T(8,128)(2,1)S(1)} %experts.1), channel_id=1, replica_groups=mesh['clip'=4,'seq'=16,'expert'=4] {'seq','expert'}, dimensions={0} | all-to-all | bytes 524288 | tf_op jit(solution)/shard_map/all_to_all | solution.py:305
  71.1 2.8 %fusion = f32[4096,256]{1,0:T(8,128)} fusion(bf16[32,4096]{1,0:T(8,128)(2,1)S(1)} %get-tuple-element.31, bf16[32,256]{1,0:T(8,128)(2,1)S(1)} %bitcast_reduce_fusion), kind=kOutput, calls=%fused_computation.1 | convolution fusion | flops 67108864 | bytes 4472832 | tf_op jit(solution)/shard_map/dot_general | solution.py:307
  (1 shorter events, 0.0 us)
Async XLA Ops:
  2.6 1.9 %collective-permute-start = (f32[32,2048]{1,0:T(8,128)S(1)}, f32[32,2048]{1,0:T(8,128)S(1)}, u32[]{:S(2)}, u32[]{:S(2)}) collective-permute-start(f32[32,2048]{1,0:T(8,128)S(1)} %get-tuple-element.21), channel_id=1, source_target_pairs={{0,1},{1,0},{2,3},{3,2},{4,5},{5,4},{6,7},{7,6},{8,9},{9,8},{10,11... | collective-permute-start | bytes 786440 | tf_op jit(solution)/shard_map/ppermute | solution.py:20
  4.7 12.8 %collective-permute-start.1 = (bf16[32,2176]{1,0:T(8,128)(2,1)S(1)}, bf16[32,2176]{1,0:T(8,128)(2,1)S(1)}, u32[]{:S(2)}, u32[]{:S(2)}) collective-permute-start(bf16[32,2176]{1,0:T(8,128)(2,1)S(1)} %get-tuple-element.24), channel_id=1, source_target_pairs={{0,2},{1,3},{2,0},{3,1},{4,6},{5,7},{6,4},{7,5},{8,10},{9,11},{10,... | collective-permute-start | bytes 417800 | tf_op jit(solution)/shard_map/ppermute | solution.py:20
  17.6 2.2 %collective-permute-start.2 = (f32[32,2048]{1,0:T(8,128)S(1)}, f32[32,2048]{1,0:T(8,128)S(1)}, u32[]{:S(2)}, u32[]{:S(2)}) collective-permute-start(f32[32,2048]{1,0:T(8,128)S(1)} %decode.1.mine_ref), channel_id=1, source_target_pairs={{0,1},{1,0},{2,3},{3,2},{4,5},{5,4},{6,7},{7,6},{8,9},{9,8},{10,11... | collective-permute-start | bytes 786440 | tf_op jit(solution)/shard_map/ppermute | solution.py:20

commit v5 on v4

--- a/solution.py
+++ b/solution.py
@@ -10,6 +10,7 @@
 LANES = 128
 REACH = 125.0
 BLOCK = 512
+MIX = 512
 LIMIT = 16 * 2**20
 
 
@@ -71,48 +72,46 @@
     )
 
 
-def decode(total, code):
-    slots, count = total.shape
-
-    def kernel(total_ref, code_ref, out_ref):
-        side = code_ref[:, count:].astype(F32)
-        lane = lax.broadcasted_iota(jnp.int32, (slots, LANES), 1)
-        center = jnp.sum(jnp.where(lane < 3, side, 0.0), axis=1, keepdims=True)
-        span = jnp.sum(jnp.where(lane < 3, 0.0, side), axis=1, keepdims=True)
-        power = jnp.log2(code_ref[:, :count].astype(F32))
-        out_ref[...] = total_ref[...] + (power * (span / (2 * REACH)) + center)
-
-    return call(
-        kernel, "decode", jax.ShapeDtypeStruct((slots, count), F32), (total, code)
-    )
-
-
-def weigh(mine, other, tokens, seq, expert):
-    slots, half = mine.shape
-    width = tokens.shape[1]
+def decoded(total, code):
+    count = total.shape[1]
+    side = code[:, count:].astype(F32)
+    lane = lax.broadcasted_iota(jnp.int32, side.shape, 1)
+    center = jnp.sum(jnp.where(lane < 3, side, 0.0), axis=1, keepdims=True)
+    span = jnp.sum(jnp.where(lane < 3, 0.0, side), axis=1, keepdims=True)
+    power = jnp.log2(code[:, :count].astype(F32))
+    return total + (power * (span / (2 * REACH)) + center)
+
+
+def weigh(totals_of, codes, held, seq, expert):
+    slots, half = totals_of[0].shape
+    width = held[0].shape[1]
     own = slots // expert
 
-    def kernel(mine_ref, other_ref, tokens_ref, send_ref, combine_ref):
+    def kernel(mine_ref, other_ref, code_ref, sent_ref, near_ref, far_ref, send_ref, combine_ref):
         core = lax.axis_index("expert") % 2
         places = [
             pl.ds(pl.multiple_of(start, half), half) for start in (core * half, (1 - core) * half)
         ]
-        parts = [mine_ref[...], other_ref[...]]
+        parts = [decoded(mine_ref[...], code_ref[...]), decoded(other_ref[...], sent_ref[...])]
         top = jnp.max(jnp.maximum(parts[0], parts[1]), axis=1, keepdims=True)
         totals = jnp.zeros((slots, 1), F32)
         weighted = jnp.zeros((slots, width), F32)
-        for part, place in zip(parts, places):
+        for part, place, held_ref in zip(parts, places, (near_ref, far_ref)):
             dispatch = jnp.exp(part - top).astype(BF16)
             totals += jnp.sum(dispatch.astype(F32), axis=1, keepdims=True)
-            weighted += jnp.dot(dispatch, tokens_ref[place, :], preferred_element_type=F32)
+            weighted += jnp.dot(dispatch, held_ref[...], preferred_element_type=F32)
             shifted = jnp.exp(part - jnp.max(part, axis=0, keepdims=True))
             share = shifted / jnp.sum(shifted, axis=0, keepdims=True)
             combine_ref[:, place] = share.astype(BF16)
         lane = lax.broadcasted_iota(jnp.int32, (slots, LANES), 1)
-        weight = spread(top + jnp.log(totals), lane, 0)
-        block = jnp.concatenate([weighted / totals, weight], axis=1)
+        weight = top + jnp.log(totals)
+        first, second = spread(weight, lane, 0), spread(weight, lane, 3)
+        mean = weighted / totals
         for e in range(expert):
-            piece = block[e * own : (e + 1) * own].astype(BF16)
+            near = slice(e * own, e * own + own // 2)
+            far = slice(e * own + own // 2, (e + 1) * own)
+            piece = [mean[near], mean[far], first[near] + second[far]]
+            piece = jnp.concatenate(piece, axis=1).astype(BF16)
             for s in range(seq):
                 send_ref[s * expert + e] = piece
 
@@ -120,67 +119,65 @@
         kernel,
         "weigh",
         (
-            jax.ShapeDtypeStruct((seq * expert, own, width + LANES), BF16),
+            jax.ShapeDtypeStruct((seq * expert, own // 2, 2 * width + LANES), BF16),
             jax.ShapeDtypeStruct((slots, 2 * half), BF16),
         ),
-        (mine, other, tokens),
+        (*totals_of, *codes, *held),
         flops=4 * slots * half * width,
     )
 
 
-def scores(tokens, slot_keys):
+def scores(tokens, slot_keys, mine):
     count, width = tokens.shape
     slots = slot_keys.shape[1]
     half = count // 2
     steps = half // BLOCK
 
-    def kernel(keys_hbm, tokens_ref, theirs_ref, mine_ref, held_ref, keys_ref, sems):
+    def kernel(keys_hbm, tokens_ref, part_ref, held_ref, keys_ref, sems):
         core = lax.axis_index("expert") % 2
-
-        def rows(step):
-            start = (1 - core) * half if step < steps else core * half
-            return pl.ds(pl.multiple_of(start + (step % steps) * BLOCK, BLOCK), BLOCK)
-
-        def copy(step):
-            return pltpu.make_async_copy(
-                tokens_ref.at[rows(step)], held_ref.at[rows(step)], sems.at[step]
-            )
-
-        keys = pltpu.make_async_copy(keys_hbm, keys_ref, sems.at[2 * steps])
+        start = (core if mine else 1 - core) * half
+        copies = []
+        for step in range(steps):
+            source = pl.ds(pl.multiple_of(start + step * BLOCK, BLOCK), BLOCK)
+            target = pl.ds(step * BLOCK, BLOCK)
+            copies.append(
+                pltpu.make_async_copy(
+                    tokens_ref.at[source], held_ref.at[target], sems.at[step]
+                )
+            )
+        keys = pltpu.make_async_copy(keys_hbm, keys_ref, sems.at[steps])
         keys.start()
-        for step in range(2 * steps):
-            copy(step).start()
+        for copy in copies:
+            copy.start()
         keys.wait()
-        for step in range(2 * steps):
-            copy(step).wait()
-            part = lax.dot_general(
+        for step in range(steps):
+            copies[step].wait()
+            target = pl.ds(step * BLOCK, BLOCK)
+            part_ref[:, target] = lax.dot_general(
                 keys_ref[...],
-                held_ref[rows(step)],
+                held_ref[target],
                 (((1,), (1,)), ((), ())),
                 preferred_element_type=F32,
             )
-            target = theirs_ref if step < steps else mine_ref
-            target[:, (step % steps) * BLOCK : (step % steps + 1) * BLOCK] = part
 
     whole = pl.BlockSpec(memory_space=pltpu.VMEM)
     return pl.pallas_call(
         kernel,
         out_shape=(
             jax.ShapeDtypeStruct((slots, half), F32),
-            jax.ShapeDtypeStruct((slots, half), F32),
-            pltpu.VMEM((count, width), BF16),
+            pltpu.VMEM((half, width), BF16),
         ),
         in_specs=[pl.BlockSpec(memory_space=pltpu.HBM)] * 2,
-        out_specs=(whole, whole, whole),
+        out_specs=(whole, whole),
         scratch_shapes=[
             pltpu.VMEM((slots, width), BF16),
-            pltpu.SemaphoreType.DMA((2 * steps + 1,)),
+            pltpu.SemaphoreType.DMA((steps + 1,)),
         ],
         compiler_params=pltpu.CompilerParams(vmem_limit_bytes=LIMIT),
         cost_estimate=pl.CostEstimate(
-            flops=2 * slots * count * width, bytes_accessed=2 * count * width, transcendentals=0
-        ),
-        name="scores",
+            flops=2 * slots * half * width, bytes_accessed=4 * half * width, transcendentals=0
+        ),
+        name="scores_mine" if mine else "scores_theirs",
     )(
         pltpu.with_memory_space_constraint(slot_keys.T, pltpu.HBM),
         pltpu.with_memory_space_constraint(tokens, pltpu.HBM),
@@ -228,16 +225,24 @@
     hidden_width = w_in.shape[2]
 
     def kernel(got_ref, w_in_ref, w_out_ref, out_ref):
-        weight = jnp.sum(got_ref[:, :, width:].astype(F32), axis=-1, keepdims=True)
-        weight = weight.reshape(seq, expert, own, 1)
-        scale = jnp.exp(weight - jnp.max(weight, axis=0, keepdims=True))
-        scale = scale / jnp.sum(scale, axis=0, keepdims=True)
+        side = got_ref[:, :, 2 * width :].astype(F32)
+        lane = lax.broadcasted_iota(jnp.int32, side.shape, 2)
+        scales = []
+        for wanted in (lane < 3, lane >= 3):
+            weight = jnp.sum(jnp.where(wanted, side, 0.0), axis=-1, keepdims=True)
+            weight = weight.reshape(seq, expert, own // 2, 1)
+            scale = jnp.exp(weight - jnp.max(weight, axis=0, keepdims=True))
+            scales.append(scale / jnp.sum(scale, axis=0, keepdims=True))
         pieces = []
         for e in range(expert):
-            total = jnp.zeros((own, width), F32)
-            for s in range(seq):
-                total += got_ref[s * expert + e, :, :width].astype(F32) * scale[s, e]
-            pieces.append(total.astype(BF16))
+            halves = []
+            for k in range(2):
+                total = jnp.zeros((own // 2, width), F32)
+                for s in range(seq):
+                    part = got_ref[s * expert + e, :, k * width : (k + 1) * width]
+                    total += part.astype(F32) * scales[k][s, e]
+                halves.append(total)
+            pieces.append(jnp.concatenate(halves, axis=0).astype(BF16))
         rows = lax.broadcasted_iota(jnp.int32, (own, hidden_width), 0)
         inner = jnp.zeros((own, hidden_width), F32)
         for i in range(own):
@@ -285,6 +290,49 @@
     )
 
 
+def mix(combine, back, seq, expert):
+    slots, count = combine.shape
+    own, width = back.shape[1:]
+    steps = count // MIX
+
+    def kernel(combine_ref, back_ref, out_ref, held_ref, sems):
+        parts = []
+        for e in range(expert):
+            total = jnp.zeros((own, width), F32)
+            for s in range(seq):
+                total += back_ref[s * expert + e].astype(F32)
+            parts.append(total)
+        table = jnp.concatenate(parts, axis=0).astype(BF16)
+        copies = []
+        for step in range(steps):
+            rows = pl.ds(step * MIX, MIX)
+            held_ref[rows, :] = lax.dot_general(
+                combine_ref[:, rows], table, (((0,), (0,)), ((), ())), preferred_element_type=F32
+            )
+            copy = pltpu.make_async_copy(held_ref.at[rows], out_ref.at[rows], sems.at[step])
+            copy.start()
+            copies.append(copy)
+        for copy in copies:
+            copy.wait()
+
+    whole = pl.BlockSpec(memory_space=pltpu.VMEM)
+    return pl.pallas_call(
+        kernel,
+        out_shape=jax.ShapeDtypeStruct((count, width), F32),
+        in_specs=[whole, whole],
+        out_specs=pl.BlockSpec(memory_space=pltpu.HBM),
+        scratch_shapes=[
+            pltpu.VMEM((count, width), F32),
+            pltpu.SemaphoreType.DMA((steps,)),
+        ],
+        compiler_params=pltpu.CompilerParams(vmem_limit_bytes=LIMIT),
+        cost_estimate=pl.CostEstimate(
+            flops=2 * slots * count * width, bytes_accessed=4 * count * width, transcendentals=0
+        ),
+        name="mix",
+    )(combine, back)
+
+
 def local(tokens, slot_keys, w_in, w_out):
     seq = lax.axis_size("seq")
     expert = lax.axis_size("expert")
@@ -292,21 +340,24 @@
     slots = slot_keys.shape[1]
     width = tokens.shape[1]
 
-    theirs, mine, tokens = scores(tokens, slot_keys)
-    mine, sent = encode(mine, swap(theirs, 0, 1))
-    sent, w_in, w_out = lax.optimization_barrier((sent, w_in, w_out))
-    got = swap(sent, 1, 0)
+    theirs, tokens_other = scores(tokens, slot_keys, False)
+    theirs, tokens = lax.optimization_barrier((theirs, tokens))
+    gained = swap(theirs, 0, 1)
+    mine, tokens_mine = scores(tokens, slot_keys, True)
+    gained, mine = lax.optimization_barrier((gained, mine))
+    mine, sent = encode(mine, gained)
+    sent, mine, w_in, w_out = lax.optimization_barrier((sent, mine, w_in, w_out))
+    code = swap(sent, 1, 0)
+    other = swap(mine, 0, 1)
     w_in, w_out = staged(w_in, w_out)
-    got, w_in, w_out = lax.optimization_barrier((got, w_in, w_out))
-    mine = decode(mine, got)
-    send, combine = weigh(mine, swap(mine, 0, 1), tokens, seq, expert)
+    code, other, w_in, w_out = lax.optimization_barrier((code, other, w_in, w_out))
+    codes = (code, swap(code, 0, 1))
+    held = (tokens_mine, tokens_other)
+    send, combine = weigh((mine, other), codes, held, seq, expert)
     got = lax.all_to_all(send, group, 0, 0)
     back = experts(got, w_in, w_out, seq, expert)
     back = lax.all_to_all(back, group, 0, 0)
-    returned = jnp.sum(back.reshape(seq, slots, width).astype(F32), axis=0).astype(BF16)
-    return lax.dot_general(
-        combine, returned, (((0,), (0,)), ((), ())), preferred_element_type=F32
-    )
+    return mix(combine, back, seq, expert)
 
 
 def solution(mesh):

time: 74.1 us -> 72.2 us (0.974)
  Pallas kernels: 8.44 us -> 11.9 us
  matrix products: 2.77 us -> 0 us
  blocking collectives: 49.2 us -> 47.8 us
  waiting for transfers between devices: 5.54 us -> 4.18 us
    dot_general x1 -> x0, matrix products: 2.77 us -> none  [local(): lax.dot_general(combine, returned, (((0,), (0,)), ((), ())), preferred_el...]
    pallas_call x0 -> x1, Pallas kernels: none -> 2.41 us  [mix(): pl.pallas_call(kernel, out_shape=jax.ShapeDtypeStruct((count, width), F32...]
    all_to_all x1, blocking collectives: 31.2 us -> 29.8 us  [local(): got = lax.all_to_all(send, group, 0, 0)]
    ppermute x3 -> x4, waiting for transfers between devices: 5.54 us -> 4.18 us  [swap(): return lax.ppermute(value, 'expert', pairs)]
    pallas_call x1 -> x2, Pallas kernels: 2.56 us -> 3.53 us  [scores(): pl.pallas_call(kernel, out_shape=(jax.ShapeDtypeStruct((slots, half), F32...]
    ppermute x3 -> x4, starting transfers between devices: 7.88 us -> 7.93 us  [swap(): return lax.ppermute(value, 'expert', pairs)]
  transfers between devices with their start and end apart: 3 -> 4, of which waited for: 3 -> 2; matrix products, arithmetic and copies ran while one was open for 0% -> 0% of each run, Pallas kernels for 5% -> 7%
where the time goes in v5:
time: 72.2 us; the launch traced here: 71.9 us
  blocking collectives  47.8 us (66%)
  Pallas kernels  11.9 us (16%)
  starting transfers between devices  7.93 us (11%)
  waiting for transfers between devices  4.18 us (6%)
    all_to_all x1, blocking collectives, local(): got = lax.all_to_all(send, group, 0, 0)  29.8 us
    all_to_all x1, blocking collectives, local(): back = lax.all_to_all(back, group, 0, 0)  18 us
    ppermute x4, starting transfers between devices, swap(): return lax.ppermute(value, 'expert', pairs)  7.93 us
    ppermute x4, waiting for transfers between devices, swap(): return lax.ppermute(value, 'expert', pairs)  4.18 us
    pallas_call x2, Pallas kernels, scores(): pl.pallas_call(kernel, out_shape=(jax.ShapeDtypeStruct((slots, half), F32...  3.53 us
    pallas_call x1, Pallas kernels, staged(): pl.pallas_call(kernel, out_shape=(pltpu.VMEM(first.shape, first.dtype), p...  3.51 us
    pallas_call x1, Pallas kernels, mix(): pl.pallas_call(kernel, out_shape=jax.ShapeDtypeStruct((count, width), F32...  2.41 us
    pallas_call x1, Pallas kernels, experts(): pl.pallas_call(kernel, out_shape=jax.ShapeDtypeStruct((seq * expert, own,...  1.5 us
  transfers between devices with their start and end apart: 4, of which 2 were waited for; matrix products, arithmetic and copies ran while one was open for 0% of the time, Pallas kernels for 7%

profile of v5, /device:TPU:33, one launch (start us, length us, event | category | flops | bytes accessed | tf_op | source)
XLA Modules:
  0.0 71.9 jit_solution(854074658128454504)
XLA Ops:
  0.0 1.8 %scores_theirs.1 = (f32[32,2048]{1,0:T(8,128)S(1)}, bf16[2048,256]{1,0:T(8,128)(2,1)S(1)}) custom-call(bf16[32,256]{1,0:T(8,128)(2,1)} %bitcast.1, bf16[4096,256]{1,0:T(8,128)(2,1)} %tokens_ref.2), custom_call_target="tpu_custom_call" | custom-call | flops 33554432 | bytes 2097152 | tf_op jit(solution)/shard_map/scores_theirs/pallas_call | solution.py:164
  1.8 0.8 %collective-permute-start = (f32[32,2048]{1,0:T(8,128)S(1)}, f32[32,2048]{1,0:T(8,128)S(1)}, u32[]{:S(2)}, u32[]{:S(2)}) collective-permute-start(f32[32,2048]{1,0:T(8,128)S(1)} %get-tuple-element.28), channel_id=1, source_target_pairs={{0,1},{1,0},{2,3},{3,2},{4,5},{5,4},{6,7},{7,6},{8,9},{9,8},{10,11... | collective-permute-start | bytes 786440 | tf_op jit(solution)/shard_map/ppermute | solution.py:21
  2.5 1.8 %scores_mine.1 = (f32[32,2048]{1,0:T(8,128)S(1)}, bf16[2048,256]{1,0:T(8,128)(2,1)S(1)}) custom-call(bf16[32,256]{1,0:T(8,128)(2,1)} %bitcast.2, bf16[4096,256]{1,0:T(8,128)(2,1)} %tokens_ref.2), custom_call_target="tpu_custom_call" | custom-call | flops 33554432 | bytes 2097152 | tf_op jit(solution)/shard_map/scores_mine/pallas_call | solution.py:164
  4.3 0.0 collective-permute-done.gained_ref
  4.3 0.2 encode.1
  4.5 0.1 collective-permute-start.2
  4.6 6.1 %collective-permute-start.1 = (bf16[32,2176]{1,0:T(8,128)(2,1)S(1)}, bf16[32,2176]{1,0:T(8,128)(2,1)S(1)}, u32[]{:S(2)}, u32[]{:S(2)}) collective-permute-start(bf16[32,2176]{1,0:T(8,128)(2,1)S(1)} %get-tuple-element.36), channel_id=1, source_target_pairs={{0,2},{1,3},{2,0},{3,1},{4,6},{5,7},{6,4},{7,5},{8,10},{9,11},{10,... | collective-permute-start | bytes 417800 | tf_op jit(solution)/shard_map/ppermute | solution.py:21
  10.7 3.5 %staged.1 = (bf16[8,1024,256]{2,1,0:T(8,128)(2,1)S(1)}, bf16[8,256,1024]{2,1,0:T(8,128)(2,1)S(1)}) custom-call(bf16[8,1024,256]{2,1,0:T(8,128)(2,1)} %first_ref, bf16[8,256,1024]{2,1,0:T(8,128)(2,1)} %second_ref), custom_call_target="tpu_custom_call" | custom-call | bytes 16777216 | tf_op jit(solution)/shard_map/staged/pallas_call | solution.py:206
  14.2 3.2 %collective-permute-done.1.code_ref = bf16[32,2176]{1,0:T(8,128)(2,1)S(1)} collective-permute-done((bf16[32,2176]{1,0:T(8,128)(2,1)S(1)}, bf16[32,2176]{1,0:T(8,128)(2,1)S(1)}, u32[]{:S(2)}, u32[]{:S(2)}) %collective-permute-start.1) | collective-permute-done | bytes 139296 | tf_op jit(solution)/shard_map/ppermute | solution.py:21
  17.4 0.0 collective-permute-done.2.other_ref
  17.4 1.0 %collective-permute-start.3 = (bf16[32,2176]{1,0:T(8,128)(2,1)S(1)}, bf16[32,2176]{1,0:T(8,128)(2,1)S(1)}, u32[]{:S(2)}, u32[]{:S(2)}) collective-permute-start(bf16[32,2176]{1,0:T(8,128)(2,1)S(1)} %collective-permute-done.1.code_ref), channel_id=1, source_target_pairs={{0,1},{1,0},{2,3},{3,2},{4,5},{5,4},{6,7},{7,6},{8,9},{9,8},{10,11... | collective-permute-start | bytes 417800 | tf_op jit(solution)/shard_map/ppermute | solution.py:21
  18.4 1.0 %collective-permute-done.3.sent_ref = bf16[32,2176]{1,0:T(8,128)(2,1)S(1)} collective-permute-done((bf16[32,2176]{1,0:T(8,128)(2,1)S(1)}, bf16[32,2176]{1,0:T(8,128)(2,1)S(1)}, u32[]{:S(2)}, u32[]{:S(2)}) %collective-permute-start.3) | collective-permute-done | bytes 139296 | tf_op jit(solution)/shard_map/ppermute | solution.py:21
  19.4 0.8 %weigh.1 = (bf16[64,4,640]{2,1,0:T(4,128)(2,1)S(1)}, bf16[32,4096]{1,0:T(8,128)(2,1)S(1)}) custom-call(f32[32,2048]{1,0:T(8,128)S(1)} %get-tuple-element.35.mine_ref, f32[32,2048]{1,0:T(8,128)S(1)} %collective-permute-done.2.other_ref, bf16[32,2176]{1,0:T(8,128)(2,1)S(1)} %collective-permute-done.1.code_ref, ...), custom_call_target="tpu_custom_call" | custom-call | flops 67108864 | bytes 2899968 | tf_op jit(solution)/shard_map/weigh/pallas_call | solution.py:36
  20.2 29.8 %all_to_all.10.got_ref = bf16[64,4,640]{2,1,0:T(4,128)(2,1)S(1)} all-to-all(bf16[64,4,640]{2,1,0:T(4,128)(2,1)S(1)} %get-tuple-element.46), channel_id=1, replica_groups=mesh['clip'=4,'seq'=16,'expert'=4] {'seq','expert'}, dimensions={0} | all-to-all | bytes 655360 | tf_op jit(solution)/shard_map/all_to_all | solution.py:357
  50.0 1.5 %experts.1 = bf16[64,8,256]{2,1,0:T(8,128)(2,1)S(1)} custom-call(bf16[64,4,640]{2,1,0:T(4,128)(2,1)S(1)} %all_to_all.10.got_ref, bf16[8,1024,256]{2,1,0:T(8,128)(2,1)S(1)} %get-tuple-element.47.w_in_ref, bf16[8,256,1024]{2,1,0:T(8,128)(2,1)S(1)} %get-tuple-element.48.w_out_ref), custom_call_target="tpu_custom_call" | custom-call | flops 67108864 | bytes 8388608 | tf_op jit(solution)/shard_map/experts/pallas_call | solution.py:274
  51.5 18.0 %all_to_all.11.back_ref = bf16[64,8,256]{2,1,0:T(8,128)(2,1)S(1)} all-to-all(bf16[64,8,256]{2,1,0:T(8,128)(2,1)S(1)} %experts.1), channel_id=1, replica_groups=mesh['clip'=4,'seq'=16,'expert'=4] {'seq','expert'}, dimensions={0} | all-to-all | bytes 524288 | tf_op jit(solution)/shard_map/all_to_all | solution.py:359
  69.5 2.4 %mix.1 = f32[4096,256]{1,0:T(8,128)} custom-call(bf16[32,4096]{1,0:T(8,128)(2,1)S(1)} %get-tuple-element.45.combine_ref, bf16[64,8,256]{2,1,0:T(8,128)(2,1)S(1)} %all_to_all.11.back_ref), custom_call_target="tpu_custom_call" | custom-call | flops 67108864 | bytes 4194304 | tf_op jit(solution)/shard_map/mix/pallas_call | solution.py:319
Async XLA Ops:
  1.8 2.5 %collective-permute-start = (f32[32,2048]{1,0:T(8,128)S(1)}, f32[32,2048]{1,0:T(8,128)S(1)}, u32[]{:S(2)}, u32[]{:S(2)}) collective-permute-start(f32[32,2048]{1,0:T(8,128)S(1)} %get-tuple-element.28), channel_id=1, source_target_pairs={{0,1},{1,0},{2,3},{3,2},{4,5},{5,4},{6,7},{7,6},{8,9},{9,8},{10,11... | collective-permute-start | bytes 786440 | tf_op jit(solution)/shard_map/ppermute | solution.py:21
  4.5 12.9 %collective-permute-start.2 = (f32[32,2048]{1,0:T(8,128)S(1)}, f32[32,2048]{1,0:T(8,128)S(1)}, u32[]{:S(2)}, u32[]{:S(2)}) collective-permute-start(f32[32,2048]{1,0:T(8,128)S(1)} %get-tuple-element.35.mine_ref), channel_id=1, source_target_pairs={{0,1},{1,0},{2,3},{3,2},{4,5},{5,4},{6,7},{7,6},{8,9},{9,8},{10,11... | collective-permute-start | bytes 786440 | tf_op jit(solution)/shard_map/ppermute | solution.py:21
  4.6 12.8 %collective-permute-start.1 = (bf16[32,2176]{1,0:T(8,128)(2,1)S(1)}, bf16[32,2176]{1,0:T(8,128)(2,1)S(1)}, u32[]{:S(2)}, u32[]{:S(2)}) collective-permute-start(bf16[32,2176]{1,0:T(8,128)(2,1)S(1)} %get-tuple-element.36), channel_id=1, source_target_pairs={{0,2},{1,3},{2,0},{3,1},{4,6},{5,7},{6,4},{7,5},{8,10},{9,11},{10,... | collective-permute-start | bytes 417800 | tf_op jit(solution)/shard_map/ppermute | solution.py:21
  17.4 2.0 %collective-permute-start.3 = (bf16[32,2176]{1,0:T(8,128)(2,1)S(1)}, bf16[32,2176]{1,0:T(8,128)(2,1)S(1)}, u32[]{:S(2)}, u32[]{:S(2)}) collective-permute-start(bf16[32,2176]{1,0:T(8,128)(2,1)S(1)} %collective-permute-done.1.code_ref), channel_id=1, source_target_pairs={{0,1},{1,0},{2,3},{3,2},{4,5},{5,4},{6,7},{7,6},{8,9},{9,8},{10,11... | collective-permute-start | bytes 417800 | tf_op jit(solution)/shard_map/ppermute | solution.py:21

commit v6 on v5

--- a/solution.py
+++ b/solution.py
@@ -9,16 +9,13 @@
 F32 = jnp.float32
 LANES = 128
 REACH = 125.0
-BLOCK = 512
+BLOCK = 1024
 MIX = 512
 LIMIT = 16 * 2**20
 
 
-def swap(value, z_step, core_step):
-    pairs = [
-        (z * 2 + c, (z ^ z_step) * 2 + (c ^ core_step)) for z in range(2) for c in range(2)
-    ]
-    return lax.ppermute(value, "expert", pairs)
+def swap(value, axis):
+    return lax.ppermute(value, axis, [(0, 1), (1, 0)])
 
 
 def spread(value, lane, first):
@@ -82,48 +79,60 @@
     return total + (power * (span / (2 * REACH)) + center)
 
 
-def weigh(totals_of, codes, held, seq, expert):
+def weigh(totals_of, codes, held, seq, planes):
     slots, half = totals_of[0].shape
     width = held[0].shape[1]
-    own = slots // expert
-
-    def kernel(mine_ref, other_ref, code_ref, sent_ref, near_ref, far_ref, send_ref, combine_ref):
-        core = lax.axis_index("expert") % 2
+    own = slots // planes // 2
+
+    def kernel(mine_ref, other_ref, code_ref, sent_ref, *refs):
+        near, far, near_next, far_next, send_ref, combine_ref = refs
+        core = lax.axis_index("core")
         places = [
             pl.ds(pl.multiple_of(start, half), half) for start in (core * half, (1 - core) * half)
         ]
         parts = [decoded(mine_ref[...], code_ref[...]), decoded(other_ref[...], sent_ref[...])]
-        top = jnp.max(jnp.maximum(parts[0], parts[1]), axis=1, keepdims=True)
-        totals = jnp.zeros((slots, 1), F32)
-        weighted = jnp.zeros((slots, width), F32)
-        for part, place, held_ref in zip(parts, places, (near_ref, far_ref)):
-            dispatch = jnp.exp(part - top).astype(BF16)
-            totals += jnp.sum(dispatch.astype(F32), axis=1, keepdims=True)
-            weighted += jnp.dot(dispatch, held_ref[...], preferred_element_type=F32)
+        first, second = [], []
+        for part, place in zip(parts, places):
             shifted = jnp.exp(part - jnp.max(part, axis=0, keepdims=True))
             share = shifted / jnp.sum(shifted, axis=0, keepdims=True)
             combine_ref[:, place] = share.astype(BF16)
-        lane = lax.broadcasted_iota(jnp.int32, (slots, LANES), 1)
+            rows = [part[k * own : (k + 1) * own] for k in range(2 * planes)]
+            first += [jnp.where(core == 0, rows[2 * z], rows[2 * z + 1]) for z in range(planes)]
+        parts = [jnp.concatenate(first[k * planes : (k + 1) * planes], axis=0) for k in range(2)]
+        top = jnp.max(jnp.maximum(parts[0], parts[1]), axis=1, keepdims=True)
+        dispatch = [jnp.exp(part - top).astype(BF16) for part in parts]
+        totals = sum(jnp.sum(d.astype(F32), axis=1, keepdims=True) for d in dispatch)
+
+        def gathered(a, b):
+            return (
+                jnp.dot(dispatch[0], a[...], preferred_element_type=F32)
+                + jnp.dot(dispatch[1], b[...], preferred_element_type=F32)
+            ) / totals
+
+        ours, next_ours = gathered(near, far), gathered(near_next, far_next)
+        mean = jnp.concatenate(
+            [jnp.where(core == 0, ours, next_ours), jnp.where(core == 0, next_ours, ours)], axis=1
+        )
+        lane = lax.broadcasted_iota(jnp.int32, (planes * own, LANES), 1)
         weight = top + jnp.log(totals)
         first, second = spread(weight, lane, 0), spread(weight, lane, 3)
-        mean = weighted / totals
-        for e in range(expert):
-            near = slice(e * own, e * own + own // 2)
-            far = slice(e * own + own // 2, (e + 1) * own)
-            piece = [mean[near], mean[far], first[near] + second[far]]
+        for z in range(planes):
+            near_rows = slice(z * own, z * own + own // 2)
+            far_rows = slice(z * own + own // 2, (z + 1) * own)
+            piece = [mean[near_rows], mean[far_rows], first[near_rows] + second[far_rows]]
             piece = jnp.concatenate(piece, axis=1).astype(BF16)
             for s in range(seq):
-                send_ref[s * expert + e] = piece
+                send_ref[s * planes + z] = piece
 
     return call(
         kernel,
         "weigh",
         (
-            jax.ShapeDtypeStruct((seq * expert, own // 2, 2 * width + LANES), BF16),
+            jax.ShapeDtypeStruct((seq * planes, own // 2, 4 * width + LANES), BF16),
             jax.ShapeDtypeStruct((slots, 2 * half), BF16),
         ),
         (*totals_of, *codes, *held),
-        flops=4 * slots * half * width,
+        flops=8 * planes * own * half * width,
     )
 
 
@@ -134,7 +143,7 @@
     steps = half // BLOCK
 
     def kernel(keys_hbm, tokens_ref, part_ref, held_ref, keys_ref, sems):
-        core = lax.axis_index("expert") % 2
+        core = lax.axis_index("core")
         start = (core if mine else 1 - core) * half
         copies = []
         for step in range(steps):
@@ -220,29 +229,80 @@
     )
 
 
+def projected(hidden, w_out_ref, core, planes, width):
+    own = hidden.shape[0]
+    rows = lax.broadcasted_iota(jnp.int32, (own, width), 0)
+    results = []
+    for z in range(planes):
+        start = pl.multiple_of((2 * z + core) * width, width)
+        result = jnp.zeros((own, width), F32)
+        for i in range(own):
+            part = jnp.dot(
+                hidden, w_out_ref[i, :, pl.ds(start, width)], preferred_element_type=F32
+            )
+            result = jnp.where(rows == i, part, result)
+        results.append(result.astype(BF16))
+    return jnp.stack(results)
+
+
+def kept(hidden, w_out, planes):
+    own, width = w_out.shape[0], w_out.shape[2] // planes // 2
+
+    def kernel(hidden_ref, w_out_ref, out_ref):
+        core = lax.axis_index("core")
+        out_ref[...] = projected(hidden_ref[...], w_out_ref, core, planes, width)
+
+    return call(
+        kernel,
+        "kept",
+        jax.ShapeDtypeStruct((planes, own, width), BF16),
+        (hidden, pltpu.with_memory_space_constraint(w_out, pltpu.VMEM)),
+        flops=16 * w_out.size,
+    )
+
+
+def packed(keep, taken, seq):
+    planes, own, width = keep.shape
+
+    def kernel(keep_ref, taken_ref, out_ref):
+        for z in range(planes):
+            pair = jnp.concatenate([keep_ref[z], taken_ref[z]], axis=0)
+            for s in range(seq):
+                out_ref[s * planes + z] = pair
+
+    return call(
+        kernel,
+        "packed",
+        jax.ShapeDtypeStruct((seq * planes, 2 * own, width), BF16),
+        (keep, taken),
+    )
+
+
 def experts(got, w_in, w_out, seq, expert):
     own, width = w_in.shape[0], w_in.shape[1] // expert
+    planes = expert // 2
     hidden_width = w_in.shape[2]
 
-    def kernel(got_ref, w_in_ref, w_out_ref, out_ref):
-        side = got_ref[:, :, 2 * width :].astype(F32)
+    def kernel(got_ref, w_in_ref, w_out_ref, hidden_ref, give_ref):
+        side = got_ref[:, :, 4 * width :].astype(F32)
         lane = lax.broadcasted_iota(jnp.int32, side.shape, 2)
         scales = []
         for wanted in (lane < 3, lane >= 3):
             weight = jnp.sum(jnp.where(wanted, side, 0.0), axis=-1, keepdims=True)
-            weight = weight.reshape(seq, expert, own // 2, 1)
+            weight = weight.reshape(seq, planes, own // 2, 1)
             scale = jnp.exp(weight - jnp.max(weight, axis=0, keepdims=True))
             scales.append(scale / jnp.sum(scale, axis=0, keepdims=True))
         pieces = []
-        for e in range(expert):
+        for z in range(planes):
             halves = []
             for k in range(2):
-                total = jnp.zeros((own // 2, width), F32)
+                total = jnp.zeros((own // 2, 2 * width), F32)
                 for s in range(seq):
-                    part = got_ref[s * expert + e, :, k * width : (k + 1) * width]
-                    total += part.astype(F32) * scales[k][s, e]
+                    part = got_ref[s * planes + z, :, 2 * k * width : 2 * (k + 1) * width]
+                    total += part.astype(F32) * scales[k][s, z]
                 halves.append(total)
-            pieces.append(jnp.concatenate(halves, axis=0).astype(BF16))
+            both = jnp.concatenate(halves, axis=0).astype(BF16)
+            pieces += [both[:, :width], both[:, width:]]
         rows = lax.broadcasted_iota(jnp.int32, (own, hidden_width), 0)
         inner = jnp.zeros((own, hidden_width), F32)
         for i in range(own):
@@ -256,26 +316,19 @@
             inner = jnp.where(rows == i, total, inner)
         hidden = 0.5 * inner * (1.0 + lax.erf(inner * (0.5**0.5)))
         hidden = hidden.astype(BF16)
-        for e in range(expert):
-            rows = lax.broadcasted_iota(jnp.int32, (own, width), 0)
-            result = jnp.zeros((own, width), F32)
-            for i in range(own):
-                part = jnp.dot(
-                    hidden,
-                    w_out_ref[i, :, e * width : (e + 1) * width],
-                    preferred_element_type=F32,
-                )
-                result = jnp.where(rows == i, part, result)
-            result = result.astype(BF16)
-            for s in range(seq):
-                out_ref[s * expert + e] = result
+        hidden_ref[...] = hidden
+        core = lax.axis_index("core")
+        give_ref[...] = projected(hidden, w_out_ref, 1 - core, planes, width)
 
     whole = pl.BlockSpec(memory_space=pltpu.VMEM)
     return pl.pallas_call(
         kernel,
-        out_shape=jax.ShapeDtypeStruct((seq * expert, own, width), BF16),
+        out_shape=[
+            jax.ShapeDtypeStruct((own, hidden_width), BF16),
+            jax.ShapeDtypeStruct((planes, own, width), BF16),
+        ],
         in_specs=[whole, whole, whole],
-        out_specs=whole,
+        out_specs=[whole, whole],
         compiler_params=pltpu.CompilerParams(vmem_limit_bytes=LIMIT),
         cost_estimate=pl.CostEstimate(
             flops=4 * own * width * expert * hidden_width * own,
@@ -290,18 +343,21 @@
     )
 
 
-def mix(combine, back, seq, expert):
+def mix(combine, back, seq, planes):
     slots, count = combine.shape
-    own, width = back.shape[1:]
+    pair, width = back.shape[1:]
+    own = pair // 2
     steps = count // MIX
 
     def kernel(combine_ref, back_ref, out_ref, held_ref, sems):
+        core = lax.axis_index("core")
         parts = []
-        for e in range(expert):
-            total = jnp.zeros((own, width), F32)
+        for z in range(planes):
+            total = jnp.zeros((pair, width), F32)
             for s in range(seq):
-                total += back_ref[s * expert + e].astype(F32)
-            parts.append(total)
+                total += back_ref[s * planes + z].astype(F32)
+            near, far = total[:own], total[own:]
+            parts += [jnp.where(core == 0, near, far), jnp.where(core == 0, far, near)]
         table = jnp.concatenate(parts, axis=0).astype(BF16)
         copies = []
         for step in range(steps):
@@ -335,41 +391,49 @@
 
 def local(tokens, slot_keys, w_in, w_out):
     seq = lax.axis_size("seq")
-    expert = lax.axis_size("expert")
-    group = ("seq", "expert")
-    slots = slot_keys.shape[1]
-    width = tokens.shape[1]
-
-    theirs, tokens_other = scores(tokens, slot_keys, False)
+    planes = lax.axis_size("plane")
+    expert = 2 * planes
+
+    theirs, far = scores(tokens, slot_keys, False)
     theirs, tokens = lax.optimization_barrier((theirs, tokens))
-    gained = swap(theirs, 0, 1)
-    mine, tokens_mine = scores(tokens, slot_keys, True)
+    gained = swap(theirs, "core")
+    mine, near = scores(tokens, slot_keys, True)
     gained, mine = lax.optimization_barrier((gained, mine))
     mine, sent = encode(mine, gained)
-    sent, mine, w_in, w_out = lax.optimization_barrier((sent, mine, w_in, w_out))
-    code = swap(sent, 1, 0)
-    other = swap(mine, 0, 1)
+    sent, mine, near, far, w_in, w_out = lax.optimization_barrier(
+        (sent, mine, near, far, w_in, w_out)
+    )
+    code = swap(sent, "plane")
+    other = swap(mine, "core")
+    near_next, far_next = swap(far, "core"), swap(near, "core")
     w_in, w_out = staged(w_in, w_out)
-    code, other, w_in, w_out = lax.optimization_barrier((code, other, w_in, w_out))
-    codes = (code, swap(code, 0, 1))
-    held = (tokens_mine, tokens_other)
-    send, combine = weigh((mine, other), codes, held, seq, expert)
-    got = lax.all_to_all(send, group, 0, 0)
-    back = experts(got, w_in, w_out, seq, expert)
-    back = lax.all_to_all(back, group, 0, 0)
-    return mix(combine, back, seq, expert)
+    code, w_in, w_out = lax.optimization_barrier((code, w_in, w_out))
+    codes = (code, swap(code, "core"))
+    held = (near, far, near_next, far_next)
+    send, combine = weigh((mine, other), codes, held, seq, planes)
+    got = lax.all_to_all(send, ("seq", "plane"), 0, 0)
+    hidden, give = experts(got, w_in, w_out, seq, expert)
+    taken = swap(give, "core")
+    back = packed(kept(hidden, w_out, planes), taken, seq)
+    back = lax.all_to_all(back, ("seq", "plane"), 0, 0)
+    return mix(combine, back, seq, planes)
 
 
 def solution(mesh):
+    clips, seq, expert = mesh.devices.shape
+    split = jax.sharding.Mesh(
+        mesh.devices.reshape(clips, seq, expert // 2, 2), ("clip", "seq", "plane", "core")
+    )
+    expert = ("plane", "core")
     return jax.shard_map(
         local,
-        mesh=mesh,
+        mesh=split,
         in_specs=(
-            P(("clip", "seq"), "expert"),
-            P("expert", None),
-            P("expert", None, "seq"),
-            P("expert", "seq", None),
-        ),
-        out_specs=P(("clip", "seq"), "expert"),
+            P(("clip", "seq"), expert),
+            P(expert, None),
+            P(expert, None, "seq"),
+            P(expert, "seq", None),
+        ),
+        out_specs=P(("clip", "seq"), expert),
         check_vma=False,
     )

time: 72.2 us -> 70.8 us (0.981); the launches traced: 71.9 us -> 69.5 us
  blocking collectives: 47.8 us -> 43.8 us
  starting transfers between devices: 7.93 us -> 9.3 us
    all_to_all x2, blocking collectives: 47.8 us -> 43.8 us  [the longest x1 27.9 us: local(): got = lax.all_to_all(send, ('seq', 'plane'), 0, 0)]
    ppermute x4 -> x7, starting transfers between devices: 7.93 us -> 9.3 us  [swap(): return lax.ppermute(value, axis, [(0, 1), (1, 0)])]
    pallas_call x2 -> x4, Pallas kernels: 1 us -> 1.58 us  [call(): pl.pallas_call(kernel, out_shape=out_shape, in_specs=[whole] * len(inputs...]
    ppermute x4 -> x7, waiting for transfers between devices: 4.18 us -> 4.47 us  [swap(): return lax.ppermute(value, axis, [(0, 1), (1, 0)])]
  transfers between devices with their start and end apart: 4 -> 7, of which waited for: 2 -> 3; matrix products, arithmetic and copies ran while one was open for 0% -> 0% of each run, Pallas kernels for 7% -> 8%
where the time goes in v6:
time: 70.8 us; the launch traced here: 69.5 us
  blocking collectives  43.8 us (62%)
  Pallas kernels  11.9 us (17%)
  starting transfers between devices  9.3 us (13%)
  waiting for transfers between devices  4.47 us (6%)
    all_to_all x1, blocking collectives, local(): got = lax.all_to_all(send, ('seq', 'plane'), 0, 0)  27.9 us
    all_to_all x1, blocking collectives, local(): back = lax.all_to_all(back, ('seq', 'plane'), 0, 0)  15.9 us
    ppermute x7, starting transfers between devices, swap(): return lax.ppermute(value, axis, [(0, 1), (1, 0)])  9.3 us
    ppermute x7, waiting for transfers between devices, swap(): return lax.ppermute(value, axis, [(0, 1), (1, 0)])  4.47 us
    pallas_call x1, Pallas kernels, staged(): pl.pallas_call(kernel, out_shape=(pltpu.VMEM(first.shape, first.dtype), p...  3.51 us
    pallas_call x2, Pallas kernels, scores(): pl.pallas_call(kernel, out_shape=(jax.ShapeDtypeStruct((slots, half), F32...  3.23 us
    pallas_call x1, Pallas kernels, mix(): pl.pallas_call(kernel, out_shape=jax.ShapeDtypeStruct((count, width), F32...  2.39 us
    pallas_call x4, Pallas kernels, call(): pl.pallas_call(kernel, out_shape=out_shape, in_specs=[whole] * len(inputs...  1.58 us
  transfers between devices with their start and end apart: 7, of which 3 were waited for; matrix products, arithmetic and copies ran while one was open for 0% of the time, Pallas kernels for 8%

profile of v6, /device:TPU:33, one launch (start us, length us, event | category | flops | bytes accessed | tf_op | source)
XLA Modules:
  0.0 69.5 jit_solution(7547372848770928722)
XLA Ops:
  0.0 1.6 %scores_theirs.1 = (f32[32,2048]{1,0:T(8,128)S(1)}, bf16[2048,256]{1,0:T(8,128)(2,1)S(1)}) custom-call(bf16[32,256]{1,0:T(8,128)(2,1)} %bitcast.1, bf16[4096,256]{1,0:T(8,128)(2,1)} %tokens_ref.2), custom_call_target="tpu_custom_call" | custom-call | flops 33554432 | bytes 2097152 | tf_op jit(solution)/shard_map/scores_theirs/pallas_call | solution.py:173
  1.6 0.8 %collective-permute-start = (f32[32,2048]{1,0:T(8,128)S(1)}, f32[32,2048]{1,0:T(8,128)S(1)}, u32[]{:S(2)}, u32[]{:S(2)}) collective-permute-start(f32[32,2048]{1,0:T(8,128)S(1)} %get-tuple-element.31), channel_id=1, source_target_pairs={{0,1},{1,0},{2,3},{3,2},{4,5},{5,4},{6,7},{7,6},{8,9},{9,8},{10,11... | collective-permute-start | bytes 786440 | tf_op jit(solution)/shard_map/ppermute | solution.py:18
  2.4 1.6 %scores_mine.1 = (f32[32,2048]{1,0:T(8,128)S(1)}, bf16[2048,256]{1,0:T(8,128)(2,1)S(1)}) custom-call(bf16[32,256]{1,0:T(8,128)(2,1)} %bitcast.2, bf16[4096,256]{1,0:T(8,128)(2,1)} %tokens_ref.2), custom_call_target="tpu_custom_call" | custom-call | flops 33554432 | bytes 2097152 | tf_op jit(solution)/shard_map/scores_mine/pallas_call | solution.py:173
  4.0 0.0 collective-permute-done.gained_ref
  4.0 0.2 encode.1
  4.2 0.1 collective-permute-start.5
  4.3 0.5 collective-permute-start.4
  4.8 6.0 %collective-permute-start.2 = (bf16[32,2176]{1,0:T(8,128)(2,1)S(1)}, bf16[32,2176]{1,0:T(8,128)(2,1)S(1)}, u32[]{:S(2)}, u32[]{:S(2)}) collective-permute-start(bf16[32,2176]{1,0:T(8,128)(2,1)S(1)} %get-tuple-element.41), channel_id=1, source_target_pairs={{0,2},{2,0},{1,3},{3,1},{4,6},{6,4},{5,7},{7,5},{8,10},{10,8},{9,1... | collective-permute-start | bytes 417800 | tf_op jit(solution)/shard_map/ppermute | solution.py:18
  10.8 0.4 collective-permute-start.1
  11.2 3.5 %staged.1 = (bf16[8,1024,256]{2,1,0:T(8,128)(2,1)S(1)}, bf16[8,256,1024]{2,1,0:T(8,128)(2,1)S(1)}) custom-call(bf16[8,1024,256]{2,1,0:T(8,128)(2,1)} %first_ref, bf16[8,256,1024]{2,1,0:T(8,128)(2,1)} %second_ref), custom_call_target="tpu_custom_call" | custom-call | bytes 16777216 | tf_op jit(solution)/shard_map/staged/pallas_call | solution.py:215
  14.7 3.0 %collective-permute-done.2.code_ref = bf16[32,2176]{1,0:T(8,128)(2,1)S(1)} collective-permute-done((bf16[32,2176]{1,0:T(8,128)(2,1)S(1)}, bf16[32,2176]{1,0:T(8,128)(2,1)S(1)}, u32[]{:S(2)}, u32[]{:S(2)}) %collective-permute-start.2) | collective-permute-done | bytes 139296 | tf_op jit(solution)/shard_map/ppermute | solution.py:18
  17.7 0.7 %collective-permute-start.3 = (bf16[32,2176]{1,0:T(8,128)(2,1)S(1)}, bf16[32,2176]{1,0:T(8,128)(2,1)S(1)}, u32[]{:S(2)}, u32[]{:S(2)}) collective-permute-start(bf16[32,2176]{1,0:T(8,128)(2,1)S(1)} %collective-permute-done.2.code_ref), channel_id=1, source_target_pairs={{0,1},{1,0},{2,3},{3,2},{4,5},{5,4},{6,7},{7,6},{8,9},{9,8},{10,11... | collective-permute-start | bytes 417800 | tf_op jit(solution)/shard_map/ppermute | solution.py:18
  18.5 0.0 collective-permute-done.1.other_ref
  18.5 1.0 %collective-permute-done.3.sent_ref = bf16[32,2176]{1,0:T(8,128)(2,1)S(1)} collective-permute-done((bf16[32,2176]{1,0:T(8,128)(2,1)S(1)}, bf16[32,2176]{1,0:T(8,128)(2,1)S(1)}, u32[]{:S(2)}, u32[]{:S(2)}) %collective-permute-start.3) | collective-permute-done | bytes 139296 | tf_op jit(solution)/shard_map/ppermute | solution.py:18
  19.5 0.0 collective-permute-done.5.refs_3_
  19.5 0.0 collective-permute-done.4.refs_2_
  19.5 1.0 %weigh.1 = (bf16[32,4,1152]{2,1,0:T(4,128)(2,1)S(1)}, bf16[32,4096]{1,0:T(8,128)(2,1)S(1)}) custom-call(f32[32,2048]{1,0:T(8,128)S(1)} %get-tuple-element.40.mine_ref, f32[32,2048]{1,0:T(8,128)S(1)} %collective-permute-done.1.other_ref, bf16[32,2176]{1,0:T(8,128)(2,1)S(1)} %collective-permute-done.2.code_ref, ...), custom_call_target="tpu_custom_call" | custom-call | flops 67108864 | bytes 4997120 | tf_op jit(solution)/shard_map/weigh/pallas_call | solution.py:33
  20.5 27.9 %all_to_all.10.got_ref = bf16[32,4,1152]{2,1,0:T(4,128)(2,1)S(1)} all-to-all(bf16[32,4,1152]{2,1,0:T(4,128)(2,1)S(1)} %get-tuple-element.50), channel_id=1, replica_groups=mesh['clip'=4,'seq'=16,'plane'=2,'core'=2] {'seq','plane'}, dimensions={0} | all-to-all | bytes 589824 | tf_op jit(solution)/shard_map/all_to_all | solution.py:414
  48.4 1.2 %experts.1 = (bf16[8,256]{1,0:T(8,128)(2,1)S(1)}, bf16[2,8,256]{2,1,0:T(8,128)(2,1)S(1)}) custom-call(bf16[32,4,1152]{2,1,0:T(4,128)(2,1)S(1)} %all_to_all.10.got_ref, bf16[8,1024,256]{2,1,0:T(8,128)(2,1)S(1)} %get-tuple-element.51.w_in_ref, bf16[8,256,1024]{2,1,0:T(8,128)(2,1)S(1)} %get-tuple-element.52.w_out_ref), custom_call_target="tpu_custom_call" | custom-call | flops 67108864 | bytes 8388608 | tf_op jit(solution)/shard_map/experts/pallas_call | solution.py:324
  49.6 0.8 %collective-permute-start.6 = (bf16[2,8,256]{2,1,0:T(8,128)(2,1)S(1)}, bf16[2,8,256]{2,1,0:T(8,128)(2,1)S(1)}, u32[]{:S(2)}, u32[]{:S(2)}) collective-permute-start(bf16[2,8,256]{2,1,0:T(8,128)(2,1)S(1)} %get-tuple-element.54), channel_id=1, source_target_pairs={{0,1},{1,0},{2,3},{3,2},{4,5},{5,4},{6,7},{7,6},{8,9},{9,8},{10,11... | collective-permute-start | bytes 24584 | tf_op jit(solution)/shard_map/ppermute | solution.py:18
  50.4 0.4 kept.1.keep_ref
  50.8 0.4 collective-permute-done.6.taken_ref
  51.2 15.9 %all_to_all.11.back_ref = bf16[32,16,256]{2,1,0:T(8,128)(2,1)S(1)} all-to-all(bf16[32,16,256]{2,1,0:T(8,128)(2,1)S(1)} %packed.1), channel_id=1, replica_groups=mesh['clip'=4,'seq'=16,'plane'=2,'core'=2] {'seq','plane'}, dimensions={0} | all-to-all | bytes 524288 | tf_op jit(solution)/shard_map/all_to_all | solution.py:418
  67.1 2.4 %mix.1 = f32[4096,256]{1,0:T(8,128)} custom-call(bf16[32,4096]{1,0:T(8,128)(2,1)S(1)} %get-tuple-element.49.combine_ref, bf16[32,16,256]{2,1,0:T(8,128)(2,1)S(1)} %all_to_all.11.back_ref), custom_call_target="tpu_custom_call" | custom-call | flops 67108864 | bytes 4194304 | tf_op jit(solution)/shard_map/mix/pallas_call | solution.py:375
  (1 shorter events, 0.0 us)
Async XLA Ops:
  1.6 2.4 %collective-permute-start = (f32[32,2048]{1,0:T(8,128)S(1)}, f32[32,2048]{1,0:T(8,128)S(1)}, u32[]{:S(2)}, u32[]{:S(2)}) collective-permute-start(f32[32,2048]{1,0:T(8,128)S(1)} %get-tuple-element.31), channel_id=1, source_target_pairs={{0,1},{1,0},{2,3},{3,2},{4,5},{5,4},{6,7},{7,6},{8,9},{9,8},{10,11... | collective-permute-start | bytes 786440 | tf_op jit(solution)/shard_map/ppermute | solution.py:18
  4.2 15.3 %collective-permute-start.5 = (bf16[2048,256]{1,0:T(8,128)(2,1)S(1)}, bf16[2048,256]{1,0:T(8,128)(2,1)S(1)}, u32[]{:S(2)}, u32[]{:S(2)}) collective-permute-start(bf16[2048,256]{1,0:T(8,128)(2,1)S(1)} %get-tuple-element.47.refs_0_), channel_id=1, source_target_pairs={{0,1},{1,0},{2,3},{3,2},{4,5},{5,4},{6,7},{7,6},{8,9},{9,8},{10,11... | collective-permute-start | bytes 3145736 | tf_op jit(solution)/shard_map/ppermute | solution.py:18
  4.3 15.2 %collective-permute-start.4 = (bf16[2048,256]{1,0:T(8,128)(2,1)S(1)}, bf16[2048,256]{1,0:T(8,128)(2,1)S(1)}, u32[]{:S(2)}, u32[]{:S(2)}) collective-permute-start(bf16[2048,256]{1,0:T(8,128)(2,1)S(1)} %get-tuple-element.48.refs_1_), channel_id=1, source_target_pairs={{0,1},{1,0},{2,3},{3,2},{4,5},{5,4},{6,7},{7,6},{8,9},{9,8},{10,11... | collective-permute-start | bytes 3145736 | tf_op jit(solution)/shard_map/ppermute | solution.py:18
  4.8 12.9 %collective-permute-start.2 = (bf16[32,2176]{1,0:T(8,128)(2,1)S(1)}, bf16[32,2176]{1,0:T(8,128)(2,1)S(1)}, u32[]{:S(2)}, u32[]{:S(2)}) collective-permute-start(bf16[32,2176]{1,0:T(8,128)(2,1)S(1)} %get-tuple-element.41), channel_id=1, source_target_pairs={{0,2},{2,0},{1,3},{3,1},{4,6},{6,4},{5,7},{7,5},{8,10},{10,8},{9,1... | collective-permute-start | bytes 417800 | tf_op jit(solution)/shard_map/ppermute | solution.py:18
  10.8 7.6 %collective-permute-start.1 = (f32[32,2048]{1,0:T(8,128)S(1)}, f32[32,2048]{1,0:T(8,128)S(1)}, u32[]{:S(2)}, u32[]{:S(2)}) collective-permute-start(f32[32,2048]{1,0:T(8,128)S(1)} %get-tuple-element.40.mine_ref), channel_id=1, source_target_pairs={{0,1},{1,0},{2,3},{3,2},{4,5},{5,4},{6,7},{7,6},{8,9},{9,8},{10,11... | collective-permute-start | bytes 786440 | tf_op jit(solution)/shard_map/ppermute | solution.py:18
  17.7 1.7 %collective-permute-start.3 = (bf16[32,2176]{1,0:T(8,128)(2,1)S(1)}, bf16[32,2176]{1,0:T(8,128)(2,1)S(1)}, u32[]{:S(2)}, u32[]{:S(2)}) collective-permute-start(bf16[32,2176]{1,0:T(8,128)(2,1)S(1)} %collective-permute-done.2.code_ref), channel_id=1, source_target_pairs={{0,1},{1,0},{2,3},{3,2},{4,5},{5,4},{6,7},{7,6},{8,9},{9,8},{10,11... | collective-permute-start | bytes 417800 | tf_op jit(solution)/shard_map/ppermute | solution.py:18
  49.6 1.7 %collective-permute-start.6 = (bf16[2,8,256]{2,1,0:T(8,128)(2,1)S(1)}, bf16[2,8,256]{2,1,0:T(8,128)(2,1)S(1)}, u32[]{:S(2)}, u32[]{:S(2)}) collective-permute-start(bf16[2,8,256]{2,1,0:T(8,128)(2,1)S(1)} %get-tuple-element.54), channel_id=1, source_target_pairs={{0,1},{1,0},{2,3},{3,2},{4,5},{5,4},{6,7},{7,6},{8,9},{9,8},{10,11... | collective-permute-start | bytes 24584 | tf_op jit(solution)/shard_map/ppermute | solution.py:18

commit v7 on v6

--- a/solution.py
+++ b/solution.py
@@ -8,7 +8,7 @@
 BF16 = jnp.bfloat16
 F32 = jnp.float32
 LANES = 128
-REACH = 125.0
+REACH = 124.0
 BLOCK = 1024
 MIX = 512
 LIMIT = 16 * 2**20
@@ -51,7 +51,7 @@
         high = jnp.max(total, axis=1, keepdims=True)
         low = jnp.min(total, axis=1, keepdims=True)
         center = 0.5 * (high + low)
-        span = jnp.maximum(high - low, 1e-30)
+        span = jnp.maximum(high - low, jnp.maximum(jnp.abs(center) * 2.0**-16, 1e-30))
         code = jnp.exp2((total - center) * (2 * REACH / span))
         code_ref[:, :count] = code.astype(BF16)
         lane = lax.broadcasted_iota(jnp.int32, (slots, LANES), 1)
@@ -85,7 +85,7 @@
     own = slots // planes // 2
 
     def kernel(mine_ref, other_ref, code_ref, sent_ref, *refs):
-        near, far, near_next, far_next, send_ref, combine_ref = refs
+        held_ref, next_ref, send_ref, combine_ref = refs
         core = lax.axis_index("core")
         places = [
             pl.ds(pl.multiple_of(start, half), half) for start in (core * half, (1 - core) * half)
@@ -105,11 +105,13 @@
 
         def gathered(a, b):
             return (
-                jnp.dot(dispatch[0], a[...], preferred_element_type=F32)
-                + jnp.dot(dispatch[1], b[...], preferred_element_type=F32)
+                jnp.dot(dispatch[0], a, preferred_element_type=F32)
+                + jnp.dot(dispatch[1], b, preferred_element_type=F32)
             ) / totals
 
-        ours, next_ours = gathered(near, far), gathered(near_next, far_next)
+        near, far = pl.ds(0, half), pl.ds(half, half)
+        ours = gathered(held_ref[near], held_ref[far])
+        next_ours = gathered(next_ref[far], next_ref[near])
         mean = jnp.concatenate(
             [jnp.where(core == 0, ours, next_ours), jnp.where(core == 0, next_ours, ours)], axis=1
         )
@@ -136,19 +138,21 @@
     )
 
 
-def scores(tokens, slot_keys, mine):
+def scores(tokens, slot_keys, held=None):
     count, width = tokens.shape
     slots = slot_keys.shape[1]
     half = count // 2
     steps = half // BLOCK
-
-    def kernel(keys_hbm, tokens_ref, part_ref, held_ref, keys_ref, sems):
+    mine = held is not None
+
+    def kernel(keys_hbm, tokens_ref, *refs):
+        part_ref, held_ref, keys_ref, sems = refs[-4:]
         core = lax.axis_index("core")
         start = (core if mine else 1 - core) * half
         copies = []
         for step in range(steps):
             source = pl.ds(pl.multiple_of(start + step * BLOCK, BLOCK), BLOCK)
-            target = pl.ds(step * BLOCK, BLOCK)
+            target = pl.ds((0 if mine else half) + step * BLOCK, BLOCK)
             copies.append(
                 pltpu.make_async_copy(
                     tokens_ref.at[source], held_ref.at[target], sems.at[step]
@@ -161,10 +165,9 @@
         keys.wait()
         for step in range(steps):
             copies[step].wait()
-            target = pl.ds(step * BLOCK, BLOCK)
-            part_ref[:, target] = lax.dot_general(
+            part_ref[:, pl.ds(step * BLOCK, BLOCK)] = lax.dot_general(
                 keys_ref[...],
-                held_ref[target],
+                held_ref[pl.ds((0 if mine else half) + step * BLOCK, BLOCK)],
                 (((1,), (1,)), ((), ())),
                 preferred_element_type=F32,
             )
@@ -174,9 +177,10 @@
         kernel,
         out_shape=(
             jax.ShapeDtypeStruct((slots, half), F32),
-            pltpu.VMEM((half, width), BF16),
-        ),
-        in_specs=[pl.BlockSpec(memory_space=pltpu.HBM)] * 2,
+            pltpu.VMEM((count, width), BF16),
+        ),
+        in_specs=[pl.BlockSpec(memory_space=pltpu.HBM)] * 2 + [whole] * mine,
+        input_output_aliases={2: 1} if mine else {},
         out_specs=(whole, whole),
         scratch_shapes=[
             pltpu.VMEM((slots, width), BF16),
@@ -190,6 +194,7 @@
     )(
         pltpu.with_memory_space_constraint(slot_keys.T, pltpu.HBM),
         pltpu.with_memory_space_constraint(tokens, pltpu.HBM),
+        *([held] if mine else []),
     )
 
 
@@ -394,22 +399,19 @@
     planes = lax.axis_size("plane")
     expert = 2 * planes
 
-    theirs, far = scores(tokens, slot_keys, False)
+    theirs, held = scores(tokens, slot_keys)
     theirs, tokens = lax.optimization_barrier((theirs, tokens))
     gained = swap(theirs, "core")
-    mine, near = scores(tokens, slot_keys, True)
+    mine, held = scores(tokens, slot_keys, held)
     gained, mine = lax.optimization_barrier((gained, mine))
     mine, sent = encode(mine, gained)
-    sent, mine, near, far, w_in, w_out = lax.optimization_barrier(
-        (sent, mine, near, far, w_in, w_out)
-    )
+    sent, mine, held, w_in, w_out = lax.optimization_barrier((sent, mine, held, w_in, w_out))
     code = swap(sent, "plane")
     other = swap(mine, "core")
-    near_next, far_next = swap(far, "core"), swap(near, "core")
+    held = (held, swap(held, "core"))
     w_in, w_out = staged(w_in, w_out)
     code, w_in, w_out = lax.optimization_barrier((code, w_in, w_out))
     codes = (code, swap(code, "core"))
-    held = (near, far, near_next, far_next)
     send, combine = weigh((mine, other), codes, held, seq, planes)
     got = lax.all_to_all(send, ("seq", "plane"), 0, 0)
     hidden, give = experts(got, w_in, w_out, seq, expert)

time: 70.8 us -> 70.3 us (level)
    ppermute x7 -> x6, waiting for transfers between devices: 4.47 us -> 3.92 us  [swap(): return lax.ppermute(value, axis, [(0, 1), (1, 0)])]
    ppermute x7 -> x6, starting transfers between devices: 9.3 us -> 9.44 us  [swap(): return lax.ppermute(value, axis, [(0, 1), (1, 0)])]
  transfers between devices with their start and end apart: 7 -> 6, of which waited for: 3 -> 3; matrix products, arithmetic and copies ran while one was open for 0% -> 0% of each run, Pallas kernels for 8% -> 8%
where the time goes in v7:
time: 70.3 us; the launch traced here: 69.1 us
  blocking collectives  43.8 us (62%)
  Pallas kernels  11.9 us (17%)
  starting transfers between devices  9.44 us (13%)
  waiting for transfers between devices  3.92 us (6%)
    all_to_all x1, blocking collectives, local(): got = lax.all_to_all(send, ('seq', 'plane'), 0, 0)  27.9 us
    all_to_all x1, blocking collectives, local(): back = lax.all_to_all(back, ('seq', 'plane'), 0, 0)  15.9 us
    ppermute x6, starting transfers between devices, swap(): return lax.ppermute(value, axis, [(0, 1), (1, 0)])  9.44 us
    ppermute x6, waiting for transfers between devices, swap(): return lax.ppermute(value, axis, [(0, 1), (1, 0)])  3.92 us
    pallas_call x1, Pallas kernels, staged(): pl.pallas_call(kernel, out_shape=(pltpu.VMEM(first.shape, first.dtype), p...  3.51 us
    pallas_call x2, Pallas kernels, scores(): pl.pallas_call(kernel, out_shape=(jax.ShapeDtypeStruct((slots, half), F32...  3.23 us
    pallas_call x1, Pallas kernels, mix(): pl.pallas_call(kernel, out_shape=jax.ShapeDtypeStruct((count, width), F32...  2.4 us
    pallas_call x4, Pallas kernels, call(): pl.pallas_call(kernel, out_shape=out_shape, in_specs=[whole] * len(inputs...  1.59 us
  transfers between devices with their start and end apart: 6, of which 3 were waited for; matrix products, arithmetic and copies ran while one was open for 0% of the time, Pallas kernels for 8%

profile of v7, /device:TPU:33, one launch (start us, length us, event | category | flops | bytes accessed | tf_op | source)
XLA Modules:
  0.0 69.1 jit_solution(13531799211004532970)
XLA Ops:
  0.0 1.6 %scores_theirs.1 = (f32[32,2048]{1,0:T(8,128)S(1)}, bf16[4096,256]{1,0:T(8,128)(2,1)S(1)}) custom-call(bf16[32,256]{1,0:T(8,128)(2,1)} %bitcast.1, bf16[4096,256]{1,0:T(8,128)(2,1)} %tokens_ref.2), custom_call_target="tpu_custom_call" | custom-call | flops 33554432 | bytes 2097152 | tf_op jit(solution)/shard_map/scores_theirs/pallas_call | solution.py:176
  1.6 0.8 %collective-permute-start = (f32[32,2048]{1,0:T(8,128)S(1)}, f32[32,2048]{1,0:T(8,128)S(1)}, u32[]{:S(2)}, u32[]{:S(2)}) collective-permute-start(f32[32,2048]{1,0:T(8,128)S(1)} %get-tuple-element.30), channel_id=1, source_target_pairs={{0,1},{1,0},{2,3},{3,2},{4,5},{5,4},{6,7},{7,6},{8,9},{9,8},{10,11... | collective-permute-start | bytes 786440 | tf_op jit(solution)/shard_map/ppermute | solution.py:18
  2.4 1.6 %scores_mine.1 = (f32[32,2048]{1,0:T(8,128)S(1)}, bf16[4096,256]{1,0:T(8,128)(2,1)S(1)}) custom-call(bf16[32,256]{1,0:T(8,128)(2,1)} %bitcast.2, bf16[4096,256]{1,0:T(8,128)(2,1)} %tokens_ref.2, bf16[4096,256]{1,0:T(8,128)(2,1)S(1)} %get-tuple-element.32.refs_0_), custom_call_target="tpu_custom_call", output_to_operand_aliasing={{1}: (2, {})} | custom-call | flops 33554432 | bytes 2097152 | tf_op jit(solution)/shard_map/scores_mine/pallas_call | solution.py:176
  4.0 0.0 collective-permute-done.gained_ref
  4.0 0.2 encode.1
  4.2 0.1 collective-permute-start.4
  4.3 6.1 %collective-permute-start.2 = (bf16[32,2176]{1,0:T(8,128)(2,1)S(1)}, bf16[32,2176]{1,0:T(8,128)(2,1)S(1)}, u32[]{:S(2)}, u32[]{:S(2)}) collective-permute-start(bf16[32,2176]{1,0:T(8,128)(2,1)S(1)} %get-tuple-element.40), channel_id=1, source_target_pairs={{0,2},{2,0},{1,3},{3,1},{4,6},{6,4},{5,7},{7,5},{8,10},{10,8},{9,1... | collective-permute-start | bytes 417800 | tf_op jit(solution)/shard_map/ppermute | solution.py:18
  10.4 0.7 collective-permute-start.1
  11.1 3.5 %staged.1 = (bf16[8,1024,256]{2,1,0:T(8,128)(2,1)S(1)}, bf16[8,256,1024]{2,1,0:T(8,128)(2,1)S(1)}) custom-call(bf16[8,1024,256]{2,1,0:T(8,128)(2,1)} %first_ref, bf16[8,256,1024]{2,1,0:T(8,128)(2,1)} %second_ref), custom_call_target="tpu_custom_call" | custom-call | bytes 16777216 | tf_op jit(solution)/shard_map/staged/pallas_call | solution.py:220
  14.6 2.5 %collective-permute-done.2.code_ref = bf16[32,2176]{1,0:T(8,128)(2,1)S(1)} collective-permute-done((bf16[32,2176]{1,0:T(8,128)(2,1)S(1)}, bf16[32,2176]{1,0:T(8,128)(2,1)S(1)}, u32[]{:S(2)}, u32[]{:S(2)}) %collective-permute-start.2) | collective-permute-done | bytes 139296 | tf_op jit(solution)/shard_map/ppermute | solution.py:18
  17.1 1.0 %collective-permute-start.3 = (bf16[32,2176]{1,0:T(8,128)(2,1)S(1)}, bf16[32,2176]{1,0:T(8,128)(2,1)S(1)}, u32[]{:S(2)}, u32[]{:S(2)}) collective-permute-start(bf16[32,2176]{1,0:T(8,128)(2,1)S(1)} %collective-permute-done.2.code_ref), channel_id=1, source_target_pairs={{0,1},{1,0},{2,3},{3,2},{4,5},{5,4},{6,7},{7,6},{8,9},{9,8},{10,11... | collective-permute-start | bytes 417800 | tf_op jit(solution)/shard_map/ppermute | solution.py:18
  18.1 0.0 collective-permute-done.1.other_ref
  18.1 1.0 %collective-permute-done.3.sent_ref = bf16[32,2176]{1,0:T(8,128)(2,1)S(1)} collective-permute-done((bf16[32,2176]{1,0:T(8,128)(2,1)S(1)}, bf16[32,2176]{1,0:T(8,128)(2,1)S(1)}, u32[]{:S(2)}, u32[]{:S(2)}) %collective-permute-start.3) | collective-permute-done | bytes 139296 | tf_op jit(solution)/shard_map/ppermute | solution.py:18
  19.1 0.0 collective-permute-done.4.refs_1_
  19.1 1.0 %weigh.1 = (bf16[32,4,1152]{2,1,0:T(4,128)(2,1)S(1)}, bf16[32,4096]{1,0:T(8,128)(2,1)S(1)}) custom-call(f32[32,2048]{1,0:T(8,128)S(1)} %get-tuple-element.39.mine_ref, f32[32,2048]{1,0:T(8,128)S(1)} %collective-permute-done.1.other_ref, bf16[32,2176]{1,0:T(8,128)(2,1)S(1)} %collective-permute-done.2.code_ref, ...), custom_call_target="tpu_custom_call" | custom-call | flops 67108864 | bytes 4997120 | tf_op jit(solution)/shard_map/weigh/pallas_call | solution.py:33
  20.1 27.9 %all_to_all.10.got_ref = bf16[32,4,1152]{2,1,0:T(4,128)(2,1)S(1)} all-to-all(bf16[32,4,1152]{2,1,0:T(4,128)(2,1)S(1)} %get-tuple-element.48), channel_id=1, replica_groups=mesh['clip'=4,'seq'=16,'plane'=2,'core'=2] {'seq','plane'}, dimensions={0} | all-to-all | bytes 589824 | tf_op jit(solution)/shard_map/all_to_all | solution.py:416
  47.9 1.2 %experts.1 = (bf16[8,256]{1,0:T(8,128)(2,1)S(1)}, bf16[2,8,256]{2,1,0:T(8,128)(2,1)S(1)}) custom-call(bf16[32,4,1152]{2,1,0:T(4,128)(2,1)S(1)} %all_to_all.10.got_ref, bf16[8,1024,256]{2,1,0:T(8,128)(2,1)S(1)} %get-tuple-element.49.w_in_ref, bf16[8,256,1024]{2,1,0:T(8,128)(2,1)S(1)} %get-tuple-element.50.w_out_ref), custom_call_target="tpu_custom_call" | custom-call | flops 67108864 | bytes 8388608 | tf_op jit(solution)/shard_map/experts/pallas_call | solution.py:329
  49.1 0.8 %collective-permute-start.5 = (bf16[2,8,256]{2,1,0:T(8,128)(2,1)S(1)}, bf16[2,8,256]{2,1,0:T(8,128)(2,1)S(1)}, u32[]{:S(2)}, u32[]{:S(2)}) collective-permute-start(bf16[2,8,256]{2,1,0:T(8,128)(2,1)S(1)} %get-tuple-element.52), channel_id=1, source_target_pairs={{0,1},{1,0},{2,3},{3,2},{4,5},{5,4},{6,7},{7,6},{8,9},{9,8},{10,11... | collective-permute-start | bytes 24584 | tf_op jit(solution)/shard_map/ppermute | solution.py:18
  49.9 0.4 kept.1.keep_ref
  50.3 0.4 collective-permute-done.5.taken_ref
  50.8 15.9 %all_to_all.11.back_ref = bf16[32,16,256]{2,1,0:T(8,128)(2,1)S(1)} all-to-all(bf16[32,16,256]{2,1,0:T(8,128)(2,1)S(1)} %packed.1), channel_id=1, replica_groups=mesh['clip'=4,'seq'=16,'plane'=2,'core'=2] {'seq','plane'}, dimensions={0} | all-to-all | bytes 524288 | tf_op jit(solution)/shard_map/all_to_all | solution.py:420
  66.7 2.4 %mix.1 = f32[4096,256]{1,0:T(8,128)} custom-call(bf16[32,4096]{1,0:T(8,128)(2,1)S(1)} %get-tuple-element.47.combine_ref, bf16[32,16,256]{2,1,0:T(8,128)(2,1)S(1)} %all_to_all.11.back_ref), custom_call_target="tpu_custom_call" | custom-call | flops 67108864 | bytes 4194304 | tf_op jit(solution)/shard_map/mix/pallas_call | solution.py:380
  (1 shorter events, 0.0 us)
Async XLA Ops:
  1.6 2.4 %collective-permute-start = (f32[32,2048]{1,0:T(8,128)S(1)}, f32[32,2048]{1,0:T(8,128)S(1)}, u32[]{:S(2)}, u32[]{:S(2)}) collective-permute-start(f32[32,2048]{1,0:T(8,128)S(1)} %get-tuple-element.30), channel_id=1, source_target_pairs={{0,1},{1,0},{2,3},{3,2},{4,5},{5,4},{6,7},{7,6},{8,9},{9,8},{10,11... | collective-permute-start | bytes 786440 | tf_op jit(solution)/shard_map/ppermute | solution.py:18
  4.2 14.9 %collective-permute-start.4 = (bf16[4096,256]{1,0:T(8,128)(2,1)S(1)}, bf16[4096,256]{1,0:T(8,128)(2,1)S(1)}, u32[]{:S(2)}, u32[]{:S(2)}) collective-permute-start(bf16[4096,256]{1,0:T(8,128)(2,1)S(1)} %get-tuple-element.46.refs_0_), channel_id=1, source_target_pairs={{0,1},{1,0},{2,3},{3,2},{4,5},{5,4},{6,7},{7,6},{8,9},{9,8},{10,11... | collective-permute-start | bytes 6291464 | tf_op jit(solution)/shard_map/ppermute | solution.py:18
  4.3 12.8 %collective-permute-start.2 = (bf16[32,2176]{1,0:T(8,128)(2,1)S(1)}, bf16[32,2176]{1,0:T(8,128)(2,1)S(1)}, u32[]{:S(2)}, u32[]{:S(2)}) collective-permute-start(bf16[32,2176]{1,0:T(8,128)(2,1)S(1)} %get-tuple-element.40), channel_id=1, source_target_pairs={{0,2},{2,0},{1,3},{3,1},{4,6},{6,4},{5,7},{7,5},{8,10},{10,8},{9,1... | collective-permute-start | bytes 417800 | tf_op jit(solution)/shard_map/ppermute | solution.py:18
  10.4 7.7 %collective-permute-start.1 = (f32[32,2048]{1,0:T(8,128)S(1)}, f32[32,2048]{1,0:T(8,128)S(1)}, u32[]{:S(2)}, u32[]{:S(2)}) collective-permute-start(f32[32,2048]{1,0:T(8,128)S(1)} %get-tuple-element.39.mine_ref), channel_id=1, source_target_pairs={{0,1},{1,0},{2,3},{3,2},{4,5},{5,4},{6,7},{7,6},{8,9},{9,8},{10,11... | collective-permute-start | bytes 786440 | tf_op jit(solution)/shard_map/ppermute | solution.py:18
  17.1 2.0 %collective-permute-start.3 = (bf16[32,2176]{1,0:T(8,128)(2,1)S(1)}, bf16[32,2176]{1,0:T(8,128)(2,1)S(1)}, u32[]{:S(2)}, u32[]{:S(2)}) collective-permute-start(bf16[32,2176]{1,0:T(8,128)(2,1)S(1)} %collective-permute-done.2.code_ref), channel_id=1, source_target_pairs={{0,1},{1,0},{2,3},{3,2},{4,5},{5,4},{6,7},{7,6},{8,9},{9,8},{10,11... | collective-permute-start | bytes 417800 | tf_op jit(solution)/shard_map/ppermute | solution.py:18
  49.1 1.7 %collective-permute-start.5 = (bf16[2,8,256]{2,1,0:T(8,128)(2,1)S(1)}, bf16[2,8,256]{2,1,0:T(8,128)(2,1)S(1)}, u32[]{:S(2)}, u32[]{:S(2)}) collective-permute-start(bf16[2,8,256]{2,1,0:T(8,128)(2,1)S(1)} %get-tuple-element.52), channel_id=1, source_target_pairs={{0,1},{1,0},{2,3},{3,2},{4,5},{5,4},{6,7},{7,6},{8,9},{9,8},{10,11... | collective-permute-start | bytes 24584 | tf_op jit(solution)/shard_map/ppermute | solution.py:18

commit v8 on v7

--- a/solution.py
+++ b/solution.py
@@ -85,7 +85,7 @@
     own = slots // planes // 2
 
     def kernel(mine_ref, other_ref, code_ref, sent_ref, *refs):
-        held_ref, next_ref, send_ref, combine_ref = refs
+        held_ref, next_ref, send_ref, logits_ref = refs
         core = lax.axis_index("core")
         places = [
             pl.ds(pl.multiple_of(start, half), half) for start in (core * half, (1 - core) * half)
@@ -93,9 +93,7 @@
         parts = [decoded(mine_ref[...], code_ref[...]), decoded(other_ref[...], sent_ref[...])]
         first, second = [], []
         for part, place in zip(parts, places):
-            shifted = jnp.exp(part - jnp.max(part, axis=0, keepdims=True))
-            share = shifted / jnp.sum(shifted, axis=0, keepdims=True)
-            combine_ref[:, place] = share.astype(BF16)
+            logits_ref[:, place] = part
             rows = [part[k * own : (k + 1) * own] for k in range(2 * planes)]
             first += [jnp.where(core == 0, rows[2 * z], rows[2 * z + 1]) for z in range(planes)]
         parts = [jnp.concatenate(first[k * planes : (k + 1) * planes], axis=0) for k in range(2)]
@@ -131,7 +129,7 @@
         "weigh",
         (
             jax.ShapeDtypeStruct((seq * planes, own // 2, 4 * width + LANES), BF16),
-            jax.ShapeDtypeStruct((slots, 2 * half), BF16),
+            jax.ShapeDtypeStruct((slots, 2 * half), F32),
         ),
         (*totals_of, *codes, *held),
         flops=8 * planes * own * half * width,
@@ -250,18 +248,27 @@
     return jnp.stack(results)
 
 
-def kept(hidden, w_out, planes):
+def kept(hidden, w_out, logits, planes):
     own, width = w_out.shape[0], w_out.shape[2] // planes // 2
-
-    def kernel(hidden_ref, w_out_ref, out_ref):
+    slots, count = logits.shape
+
+    def kernel(hidden_ref, w_out_ref, logits_ref, out_ref, combine_ref):
         core = lax.axis_index("core")
         out_ref[...] = projected(hidden_ref[...], w_out_ref, core, planes, width)
+        for start in range(0, count, BLOCK):
+            part = logits_ref[:, start : start + BLOCK]
+            shifted = jnp.exp(part - jnp.max(part, axis=0, keepdims=True))
+            share = shifted / jnp.sum(shifted, axis=0, keepdims=True)
+            combine_ref[:, start : start + BLOCK] = share.astype(BF16)
 
     return call(
         kernel,
         "kept",
-        jax.ShapeDtypeStruct((planes, own, width), BF16),
-        (hidden, pltpu.with_memory_space_constraint(w_out, pltpu.VMEM)),
+        (
+            jax.ShapeDtypeStruct((planes, own, width), BF16),
+            jax.ShapeDtypeStruct((slots, count), BF16),
+        ),
+        (hidden, pltpu.with_memory_space_constraint(w_out, pltpu.VMEM), logits),
         flops=16 * w_out.size,
     )
 
@@ -412,11 +419,12 @@
     w_in, w_out = staged(w_in, w_out)
     code, w_in, w_out = lax.optimization_barrier((code, w_in, w_out))
     codes = (code, swap(code, "core"))
-    send, combine = weigh((mine, other), codes, held, seq, planes)
+    send, logits = weigh((mine, other), codes, held, seq, planes)
     got = lax.all_to_all(send, ("seq", "plane"), 0, 0)
     hidden, give = experts(got, w_in, w_out, seq, expert)
     taken = swap(give, "core")
-    back = packed(kept(hidden, w_out, planes), taken, seq)
+    keep, combine = kept(hidden, w_out, logits, planes)
+    back = packed(keep, taken, seq)
     back = lax.all_to_all(back, ("seq", "plane"), 0, 0)
     return mix(combine, back, seq, planes)
 

time: 70.3 us -> 70.3 us (level)
  no operation moved by 1% of the time
where the time goes in v8:
time: 70.3 us; the launch traced here: 69 us
  blocking collectives  43.8 us (62%)
  Pallas kernels  11.9 us (17%)
  starting transfers between devices  9.44 us (13%)
  waiting for transfers between devices  3.83 us (5%)
    all_to_all x1, blocking collectives, local(): got = lax.all_to_all(send, ('seq', 'plane'), 0, 0)  27.9 us
    all_to_all x1, blocking collectives, local(): back = lax.all_to_all(back, ('seq', 'plane'), 0, 0)  15.9 us
    ppermute x6, starting transfers between devices, swap(): return lax.ppermute(value, axis, [(0, 1), (1, 0)])  9.44 us
    ppermute x6, waiting for transfers between devices, swap(): return lax.ppermute(value, axis, [(0, 1), (1, 0)])  3.83 us
    pallas_call x1, Pallas kernels, staged(): pl.pallas_call(kernel, out_shape=(pltpu.VMEM(first.shape, first.dtype), p...  3.51 us
    pallas_call x2, Pallas kernels, scores(): pl.pallas_call(kernel, out_shape=(jax.ShapeDtypeStruct((slots, half), F32...  3.23 us
    pallas_call x1, Pallas kernels, mix(): pl.pallas_call(kernel, out_shape=jax.ShapeDtypeStruct((count, width), F32...  2.4 us
    pallas_call x4, Pallas kernels, call(): pl.pallas_call(kernel, out_shape=out_shape, in_specs=[whole] * len(inputs...  1.58 us
  transfers between devices with their start and end apart: 6, of which 3 were waited for; matrix products, arithmetic and copies ran while one was open for 0% of the time, Pallas kernels for 8%

profile of v8, /device:TPU:33, one launch (start us, length us, event | category | flops | bytes accessed | tf_op | source)
XLA Modules:
  0.0 69.0 jit_solution(14441259501236891459)
XLA Ops:
  0.0 1.6 %scores_theirs.1 = (f32[32,2048]{1,0:T(8,128)S(1)}, bf16[4096,256]{1,0:T(8,128)(2,1)S(1)}) custom-call(bf16[32,256]{1,0:T(8,128)(2,1)} %bitcast.1, bf16[4096,256]{1,0:T(8,128)(2,1)} %tokens_ref.2), custom_call_target="tpu_custom_call" | custom-call | flops 33554432 | bytes 2097152 | tf_op jit(solution)/shard_map/scores_theirs/pallas_call | solution.py:174
  1.6 0.8 %collective-permute-start = (f32[32,2048]{1,0:T(8,128)S(1)}, f32[32,2048]{1,0:T(8,128)S(1)}, u32[]{:S(2)}, u32[]{:S(2)}) collective-permute-start(f32[32,2048]{1,0:T(8,128)S(1)} %get-tuple-element.32), channel_id=1, source_target_pairs={{0,1},{1,0},{2,3},{3,2},{4,5},{5,4},{6,7},{7,6},{8,9},{9,8},{10,11... | collective-permute-start | bytes 786440 | tf_op jit(solution)/shard_map/ppermute | solution.py:18
  2.4 1.6 %scores_mine.1 = (f32[32,2048]{1,0:T(8,128)S(1)}, bf16[4096,256]{1,0:T(8,128)(2,1)S(1)}) custom-call(bf16[32,256]{1,0:T(8,128)(2,1)} %bitcast.2, bf16[4096,256]{1,0:T(8,128)(2,1)} %tokens_ref.2, bf16[4096,256]{1,0:T(8,128)(2,1)S(1)} %get-tuple-element.34.refs_0_), custom_call_target="tpu_custom_call", output_to_operand_aliasing={{1}: (2, {})} | custom-call | flops 33554432 | bytes 2097152 | tf_op jit(solution)/shard_map/scores_mine/pallas_call | solution.py:174
  4.0 0.0 collective-permute-done.gained_ref
  4.0 0.2 encode.1
  4.2 0.1 collective-permute-start.4
  4.3 6.1 %collective-permute-start.2 = (bf16[32,2176]{1,0:T(8,128)(2,1)S(1)}, bf16[32,2176]{1,0:T(8,128)(2,1)S(1)}, u32[]{:S(2)}, u32[]{:S(2)}) collective-permute-start(bf16[32,2176]{1,0:T(8,128)(2,1)S(1)} %get-tuple-element.42), channel_id=1, source_target_pairs={{0,2},{2,0},{1,3},{3,1},{4,6},{6,4},{5,7},{7,5},{8,10},{10,8},{9,1... | collective-permute-start | bytes 417800 | tf_op jit(solution)/shard_map/ppermute | solution.py:18
  10.4 0.7 collective-permute-start.1
  11.1 3.5 %staged.1 = (bf16[8,1024,256]{2,1,0:T(8,128)(2,1)S(1)}, bf16[8,256,1024]{2,1,0:T(8,128)(2,1)S(1)}) custom-call(bf16[8,1024,256]{2,1,0:T(8,128)(2,1)} %first_ref, bf16[8,256,1024]{2,1,0:T(8,128)(2,1)} %second_ref), custom_call_target="tpu_custom_call" | custom-call | bytes 16777216 | tf_op jit(solution)/shard_map/staged/pallas_call | solution.py:218
  14.6 2.5 %collective-permute-done.2.code_ref = bf16[32,2176]{1,0:T(8,128)(2,1)S(1)} collective-permute-done((bf16[32,2176]{1,0:T(8,128)(2,1)S(1)}, bf16[32,2176]{1,0:T(8,128)(2,1)S(1)}, u32[]{:S(2)}, u32[]{:S(2)}) %collective-permute-start.2) | collective-permute-done | bytes 139296 | tf_op jit(solution)/shard_map/ppermute | solution.py:18
  17.1 1.0 %collective-permute-start.3 = (bf16[32,2176]{1,0:T(8,128)(2,1)S(1)}, bf16[32,2176]{1,0:T(8,128)(2,1)S(1)}, u32[]{:S(2)}, u32[]{:S(2)}) collective-permute-start(bf16[32,2176]{1,0:T(8,128)(2,1)S(1)} %collective-permute-done.2.code_ref), channel_id=1, source_target_pairs={{0,1},{1,0},{2,3},{3,2},{4,5},{5,4},{6,7},{7,6},{8,9},{9,8},{10,11... | collective-permute-start | bytes 417800 | tf_op jit(solution)/shard_map/ppermute | solution.py:18
  18.1 0.0 collective-permute-done.1.other_ref
  18.1 1.0 %collective-permute-done.3.sent_ref = bf16[32,2176]{1,0:T(8,128)(2,1)S(1)} collective-permute-done((bf16[32,2176]{1,0:T(8,128)(2,1)S(1)}, bf16[32,2176]{1,0:T(8,128)(2,1)S(1)}, u32[]{:S(2)}, u32[]{:S(2)}) %collective-permute-start.3) | collective-permute-done | bytes 139296 | tf_op jit(solution)/shard_map/ppermute | solution.py:18
  19.1 0.0 collective-permute-done.4.refs_1_
  19.1 0.9 %weigh.1 = (bf16[32,4,1152]{2,1,0:T(4,128)(2,1)S(1)}, f32[32,4096]{1,0:T(8,128)S(1)}) custom-call(f32[32,2048]{1,0:T(8,128)S(1)} %get-tuple-element.41.mine_ref, f32[32,2048]{1,0:T(8,128)S(1)} %collective-permute-done.1.other_ref, bf16[32,2176]{1,0:T(8,128)(2,1)S(1)} %collective-permute-done.2.code_ref, ...), custom_call_target="tpu_custom_call" | custom-call | flops 67108864 | bytes 4997120 | tf_op jit(solution)/shard_map/weigh/pallas_call | solution.py:33
  20.0 27.9 %all_to_all.10.got_ref = bf16[32,4,1152]{2,1,0:T(4,128)(2,1)S(1)} all-to-all(bf16[32,4,1152]{2,1,0:T(4,128)(2,1)S(1)} %get-tuple-element.49), channel_id=1, replica_groups=mesh['clip'=4,'seq'=16,'plane'=2,'core'=2] {'seq','plane'}, dimensions={0} | all-to-all | bytes 589824 | tf_op jit(solution)/shard_map/all_to_all | solution.py:423
  47.9 1.2 %experts.1 = (bf16[8,256]{1,0:T(8,128)(2,1)S(1)}, bf16[2,8,256]{2,1,0:T(8,128)(2,1)S(1)}) custom-call(bf16[32,4,1152]{2,1,0:T(4,128)(2,1)S(1)} %all_to_all.10.got_ref, bf16[8,1024,256]{2,1,0:T(8,128)(2,1)S(1)} %get-tuple-element.50.w_in_ref, bf16[8,256,1024]{2,1,0:T(8,128)(2,1)S(1)} %get-tuple-element.51.w_out_ref), custom_call_target="tpu_custom_call" | custom-call | flops 67108864 | bytes 8388608 | tf_op jit(solution)/shard_map/experts/pallas_call | solution.py:336
  49.0 0.8 %collective-permute-start.5 = (bf16[2,8,256]{2,1,0:T(8,128)(2,1)S(1)}, bf16[2,8,256]{2,1,0:T(8,128)(2,1)S(1)}, u32[]{:S(2)}, u32[]{:S(2)}) collective-permute-start(bf16[2,8,256]{2,1,0:T(8,128)(2,1)S(1)} %get-tuple-element.56), channel_id=1, source_target_pairs={{0,1},{1,0},{2,3},{3,2},{4,5},{5,4},{6,7},{7,6},{8,9},{9,8},{10,11... | collective-permute-start | bytes 24584 | tf_op jit(solution)/shard_map/ppermute | solution.py:18
  49.9 0.5 kept.1
  50.3 0.3 collective-permute-done.5.taken_ref
  50.7 15.9 %all_to_all.11.back_ref = bf16[32,16,256]{2,1,0:T(8,128)(2,1)S(1)} all-to-all(bf16[32,16,256]{2,1,0:T(8,128)(2,1)S(1)} %packed.1), channel_id=1, replica_groups=mesh['clip'=4,'seq'=16,'plane'=2,'core'=2] {'seq','plane'}, dimensions={0} | all-to-all | bytes 524288 | tf_op jit(solution)/shard_map/all_to_all | solution.py:428
  66.6 2.4 %mix.1 = f32[4096,256]{1,0:T(8,128)} custom-call(bf16[32,4096]{1,0:T(8,128)(2,1)S(1)} %get-tuple-element.54.combine_ref, bf16[32,16,256]{2,1,0:T(8,128)(2,1)S(1)} %all_to_all.11.back_ref), custom_call_target="tpu_custom_call" | custom-call | flops 67108864 | bytes 4194304 | tf_op jit(solution)/shard_map/mix/pallas_call | solution.py:387
  (1 shorter events, 0.0 us)
Async XLA Ops:
  1.6 2.4 %collective-permute-start = (f32[32,2048]{1,0:T(8,128)S(1)}, f32[32,2048]{1,0:T(8,128)S(1)}, u32[]{:S(2)}, u32[]{:S(2)}) collective-permute-start(f32[32,2048]{1,0:T(8,128)S(1)} %get-tuple-element.32), channel_id=1, source_target_pairs={{0,1},{1,0},{2,3},{3,2},{4,5},{5,4},{6,7},{7,6},{8,9},{9,8},{10,11... | collective-permute-start | bytes 786440 | tf_op jit(solution)/shard_map/ppermute | solution.py:18
  4.2 14.9 %collective-permute-start.4 = (bf16[4096,256]{1,0:T(8,128)(2,1)S(1)}, bf16[4096,256]{1,0:T(8,128)(2,1)S(1)}, u32[]{:S(2)}, u32[]{:S(2)}) collective-permute-start(bf16[4096,256]{1,0:T(8,128)(2,1)S(1)} %get-tuple-element.48.refs_0_), channel_id=1, source_target_pairs={{0,1},{1,0},{2,3},{3,2},{4,5},{5,4},{6,7},{7,6},{8,9},{9,8},{10,11... | collective-permute-start | bytes 6291464 | tf_op jit(solution)/shard_map/ppermute | solution.py:18
  4.3 12.8 %collective-permute-start.2 = (bf16[32,2176]{1,0:T(8,128)(2,1)S(1)}, bf16[32,2176]{1,0:T(8,128)(2,1)S(1)}, u32[]{:S(2)}, u32[]{:S(2)}) collective-permute-start(bf16[32,2176]{1,0:T(8,128)(2,1)S(1)} %get-tuple-element.42), channel_id=1, source_target_pairs={{0,2},{2,0},{1,3},{3,1},{4,6},{6,4},{5,7},{7,5},{8,10},{10,8},{9,1... | collective-permute-start | bytes 417800 | tf_op jit(solution)/shard_map/ppermute | solution.py:18
  10.4 7.7 %collective-permute-start.1 = (f32[32,2048]{1,0:T(8,128)S(1)}, f32[32,2048]{1,0:T(8,128)S(1)}, u32[]{:S(2)}, u32[]{:S(2)}) collective-permute-start(f32[32,2048]{1,0:T(8,128)S(1)} %get-tuple-element.41.mine_ref), channel_id=1, source_target_pairs={{0,1},{1,0},{2,3},{3,2},{4,5},{5,4},{6,7},{7,6},{8,9},{9,8},{10,11... | collective-permute-start | bytes 786440 | tf_op jit(solution)/shard_map/ppermute | solution.py:18
  17.1 2.0 %collective-permute-start.3 = (bf16[32,2176]{1,0:T(8,128)(2,1)S(1)}, bf16[32,2176]{1,0:T(8,128)(2,1)S(1)}, u32[]{:S(2)}, u32[]{:S(2)}) collective-permute-start(bf16[32,2176]{1,0:T(8,128)(2,1)S(1)} %collective-permute-done.2.code_ref), channel_id=1, source_target_pairs={{0,1},{1,0},{2,3},{3,2},{4,5},{5,4},{6,7},{7,6},{8,9},{9,8},{10,11... | collective-permute-start | bytes 417800 | tf_op jit(solution)/shard_map/ppermute | solution.py:18
  49.0 1.7 %collective-permute-start.5 = (bf16[2,8,256]{2,1,0:T(8,128)(2,1)S(1)}, bf16[2,8,256]{2,1,0:T(8,128)(2,1)S(1)}, u32[]{:S(2)}, u32[]{:S(2)}) collective-permute-start(bf16[2,8,256]{2,1,0:T(8,128)(2,1)S(1)} %get-tuple-element.56), channel_id=1, source_target_pairs={{0,1},{1,0},{2,3},{3,2},{4,5},{5,4},{6,7},{7,6},{8,9},{9,8},{10,11... | collective-permute-start | bytes 24584 | tf_op jit(solution)/shard_map/ppermute | solution.py:18

commit v9 on v8

--- a/solution.py
+++ b/solution.py
@@ -412,7 +412,7 @@
     mine, held = scores(tokens, slot_keys, held)
     gained, mine = lax.optimization_barrier((gained, mine))
     mine, sent = encode(mine, gained)
-    sent, mine, held, w_in, w_out = lax.optimization_barrier((sent, mine, held, w_in, w_out))
+    sent, w_in, w_out = lax.optimization_barrier((sent, w_in, w_out))
     code = swap(sent, "plane")
     other = swap(mine, "core")
     held = (held, swap(held, "core"))

time: 70.3 us -> 74.3 us (1.057)
  waiting for transfers between devices: 3.83 us -> 7.96 us
    ppermute x6, waiting for transfers between devices: 3.83 us -> 7.96 us  [swap(): return lax.ppermute(value, axis, [(0, 1), (1, 0)])]
  transfers between devices with their start and end apart: 6 -> 6, of which waited for: 3 -> 4; matrix products, arithmetic and copies ran while one was open for 0% -> 0% of each run, Pallas kernels for 8% -> 6%
where the time goes in v9:
time: 74.3 us; the launch traced here: 73.1 us
  blocking collectives  43.8 us (59%)
  Pallas kernels  11.9 us (16%)
  starting transfers between devices  9.37 us (13%)
  waiting for transfers between devices  7.96 us (11%)
    all_to_all x1, blocking collectives, local(): got = lax.all_to_all(send, ('seq', 'plane'), 0, 0)  27.9 us
    all_to_all x1, blocking collectives, local(): back = lax.all_to_all(back, ('seq', 'plane'), 0, 0)  15.9 us
    ppermute x6, starting transfers between devices, swap(): return lax.ppermute(value, axis, [(0, 1), (1, 0)])  9.37 us
    ppermute x6, waiting for transfers between devices, swap(): return lax.ppermute(value, axis, [(0, 1), (1, 0)])  7.96 us
    pallas_call x1, Pallas kernels, staged(): pl.pallas_call(kernel, out_shape=(pltpu.VMEM(first.shape, first.dtype), p...  3.51 us
    pallas_call x2, Pallas kernels, scores(): pl.pallas_call(kernel, out_shape=(jax.ShapeDtypeStruct((slots, half), F32...  3.23 us
    pallas_call x1, Pallas kernels, mix(): pl.pallas_call(kernel, out_shape=jax.ShapeDtypeStruct((count, width), F32...  2.4 us
    pallas_call x4, Pallas kernels, call(): pl.pallas_call(kernel, out_shape=out_shape, in_specs=[whole] * len(inputs...  1.6 us
  transfers between devices with their start and end apart: 6, of which 4 were waited for; matrix products, arithmetic and copies ran while one was open for 0% of the time, Pallas kernels for 6%

profile of v9, /device:TPU:33, one launch (start us, length us, event | category | flops | bytes accessed | tf_op | source)
XLA Modules:
  0.0 73.1 jit_solution(16989439507412963037)
XLA Ops:
  0.0 1.6 %scores_theirs.1 = (f32[32,2048]{1,0:T(8,128)S(1)}, bf16[4096,256]{1,0:T(8,128)(2,1)S(1)}) custom-call(bf16[32,256]{1,0:T(8,128)(2,1)} %bitcast.1, bf16[4096,256]{1,0:T(8,128)(2,1)} %tokens_ref.2), custom_call_target="tpu_custom_call" | custom-call | flops 33554432 | bytes 2097152 | tf_op jit(solution)/shard_map/scores_theirs/pallas_call | solution.py:174
  1.6 1.6 %scores_mine.1 = (f32[32,2048]{1,0:T(8,128)S(1)}, bf16[4096,256]{1,0:T(8,128)(2,1)S(1)}) custom-call(bf16[32,256]{1,0:T(8,128)(2,1)} %bitcast.2, bf16[4096,256]{1,0:T(8,128)(2,1)} %tokens_ref.2, bf16[4096,256]{1,0:T(8,128)(2,1)S(1)} %get-tuple-element.32.refs_0_), custom_call_target="tpu_custom_call", output_to_operand_aliasing={{1}: (2, {})} | custom-call | flops 33554432 | bytes 2097152 | tf_op jit(solution)/shard_map/scores_mine/pallas_call | solution.py:174
  3.2 0.8 %collective-permute-start.4 = (bf16[4096,256]{1,0:T(8,128)(2,1)S(1)}, bf16[4096,256]{1,0:T(8,128)(2,1)S(1)}, u32[]{:S(2)}, u32[]{:S(2)}) collective-permute-start(bf16[4096,256]{1,0:T(8,128)(2,1)S(1)} %get-tuple-element.44.refs_0_), channel_id=1, source_target_pairs={{0,1},{1,0},{2,3},{3,2},{4,5},{5,4},{6,7},{7,6},{8,9},{9,8},{10,11... | collective-permute-start | bytes 6291464 | tf_op jit(solution)/shard_map/ppermute | solution.py:18
  4.0 0.1 collective-permute-start
  4.1 4.1 %collective-permute-done.gained_ref = f32[32,2048]{1,0:T(8,128)S(1)} collective-permute-done((f32[32,2048]{1,0:T(8,128)S(1)}, f32[32,2048]{1,0:T(8,128)S(1)}, u32[]{:S(2)}, u32[]{:S(2)}) %collective-permute-start) | collective-permute-done | bytes 262176 | tf_op jit(solution)/shard_map/ppermute | solution.py:18
  8.2 0.2 encode.1
  8.3 6.1 %collective-permute-start.2 = (bf16[32,2176]{1,0:T(8,128)(2,1)S(1)}, bf16[32,2176]{1,0:T(8,128)(2,1)S(1)}, u32[]{:S(2)}, u32[]{:S(2)}) collective-permute-start(bf16[32,2176]{1,0:T(8,128)(2,1)S(1)} %get-tuple-element.38), channel_id=1, source_target_pairs={{0,2},{2,0},{1,3},{3,1},{4,6},{6,4},{5,7},{7,5},{8,10},{10,8},{9,1... | collective-permute-start | bytes 417800 | tf_op jit(solution)/shard_map/ppermute | solution.py:18
  14.4 0.7 collective-permute-start.1
  15.1 3.5 %staged.1 = (bf16[8,1024,256]{2,1,0:T(8,128)(2,1)S(1)}, bf16[8,256,1024]{2,1,0:T(8,128)(2,1)S(1)}) custom-call(bf16[8,1024,256]{2,1,0:T(8,128)(2,1)} %first_ref, bf16[8,256,1024]{2,1,0:T(8,128)(2,1)} %second_ref), custom_call_target="tpu_custom_call" | custom-call | bytes 16777216 | tf_op jit(solution)/shard_map/staged/pallas_call | solution.py:218
  18.6 2.6 %collective-permute-done.2.code_ref = bf16[32,2176]{1,0:T(8,128)(2,1)S(1)} collective-permute-done((bf16[32,2176]{1,0:T(8,128)(2,1)S(1)}, bf16[32,2176]{1,0:T(8,128)(2,1)S(1)}, u32[]{:S(2)}, u32[]{:S(2)}) %collective-permute-start.2) | collective-permute-done | bytes 139296 | tf_op jit(solution)/shard_map/ppermute | solution.py:18
  21.2 0.9 %collective-permute-start.3 = (bf16[32,2176]{1,0:T(8,128)(2,1)S(1)}, bf16[32,2176]{1,0:T(8,128)(2,1)S(1)}, u32[]{:S(2)}, u32[]{:S(2)}) collective-permute-start(bf16[32,2176]{1,0:T(8,128)(2,1)S(1)} %collective-permute-done.2.code_ref), channel_id=1, source_target_pairs={{0,1},{1,0},{2,3},{3,2},{4,5},{5,4},{6,7},{7,6},{8,9},{9,8},{10,11... | collective-permute-start | bytes 417800 | tf_op jit(solution)/shard_map/ppermute | solution.py:18
  22.1 0.0 collective-permute-done.1.other_ref
  22.1 1.0 %collective-permute-done.3.sent_ref = bf16[32,2176]{1,0:T(8,128)(2,1)S(1)} collective-permute-done((bf16[32,2176]{1,0:T(8,128)(2,1)S(1)}, bf16[32,2176]{1,0:T(8,128)(2,1)S(1)}, u32[]{:S(2)}, u32[]{:S(2)}) %collective-permute-start.3) | collective-permute-done | bytes 139296 | tf_op jit(solution)/shard_map/ppermute | solution.py:18
  23.1 0.0 collective-permute-done.4.refs_1_
  23.1 0.9 %weigh.1 = (bf16[32,4,1152]{2,1,0:T(4,128)(2,1)S(1)}, f32[32,4096]{1,0:T(8,128)S(1)}) custom-call(f32[32,2048]{1,0:T(8,128)S(1)} %get-tuple-element.36.mine_ref, f32[32,2048]{1,0:T(8,128)S(1)} %collective-permute-done.1.other_ref, bf16[32,2176]{1,0:T(8,128)(2,1)S(1)} %collective-permute-done.2.code_ref, ...), custom_call_target="tpu_custom_call" | custom-call | flops 67108864 | bytes 4997120 | tf_op jit(solution)/shard_map/weigh/pallas_call | solution.py:33
  24.0 27.9 %all_to_all.10.got_ref = bf16[32,4,1152]{2,1,0:T(4,128)(2,1)S(1)} all-to-all(bf16[32,4,1152]{2,1,0:T(4,128)(2,1)S(1)} %get-tuple-element.45), channel_id=1, replica_groups=mesh['clip'=4,'seq'=16,'plane'=2,'core'=2] {'seq','plane'}, dimensions={0} | all-to-all | bytes 589824 | tf_op jit(solution)/shard_map/all_to_all | solution.py:423
  51.9 1.2 %experts.1 = (bf16[8,256]{1,0:T(8,128)(2,1)S(1)}, bf16[2,8,256]{2,1,0:T(8,128)(2,1)S(1)}) custom-call(bf16[32,4,1152]{2,1,0:T(4,128)(2,1)S(1)} %all_to_all.10.got_ref, bf16[8,1024,256]{2,1,0:T(8,128)(2,1)S(1)} %get-tuple-element.46.w_in_ref, bf16[8,256,1024]{2,1,0:T(8,128)(2,1)S(1)} %get-tuple-element.47.w_out_ref), custom_call_target="tpu_custom_call" | custom-call | flops 67108864 | bytes 8388608 | tf_op jit(solution)/shard_map/experts/pallas_call | solution.py:336
  53.1 0.8 %collective-permute-start.5 = (bf16[2,8,256]{2,1,0:T(8,128)(2,1)S(1)}, bf16[2,8,256]{2,1,0:T(8,128)(2,1)S(1)}, u32[]{:S(2)}, u32[]{:S(2)}) collective-permute-start(bf16[2,8,256]{2,1,0:T(8,128)(2,1)S(1)} %get-tuple-element.52), channel_id=1, source_target_pairs={{0,1},{1,0},{2,3},{3,2},{4,5},{5,4},{6,7},{7,6},{8,9},{9,8},{10,11... | collective-permute-start | bytes 24584 | tf_op jit(solution)/shard_map/ppermute | solution.py:18
  53.9 0.5 kept.1
  54.4 0.3 collective-permute-done.5.taken_ref
  54.8 15.9 %all_to_all.11.back_ref = bf16[32,16,256]{2,1,0:T(8,128)(2,1)S(1)} all-to-all(bf16[32,16,256]{2,1,0:T(8,128)(2,1)S(1)} %packed.1), channel_id=1, replica_groups=mesh['clip'=4,'seq'=16,'plane'=2,'core'=2] {'seq','plane'}, dimensions={0} | all-to-all | bytes 524288 | tf_op jit(solution)/shard_map/all_to_all | solution.py:428
  70.7 2.4 %mix.1 = f32[4096,256]{1,0:T(8,128)} custom-call(bf16[32,4096]{1,0:T(8,128)(2,1)S(1)} %get-tuple-element.50.combine_ref, bf16[32,16,256]{2,1,0:T(8,128)(2,1)S(1)} %all_to_all.11.back_ref), custom_call_target="tpu_custom_call" | custom-call | flops 67108864 | bytes 4194304 | tf_op jit(solution)/shard_map/mix/pallas_call | solution.py:387
  (1 shorter events, 0.0 us)
Async XLA Ops:
  3.2 19.9 %collective-permute-start.4 = (bf16[4096,256]{1,0:T(8,128)(2,1)S(1)}, bf16[4096,256]{1,0:T(8,128)(2,1)S(1)}, u32[]{:S(2)}, u32[]{:S(2)}) collective-permute-start(bf16[4096,256]{1,0:T(8,128)(2,1)S(1)} %get-tuple-element.44.refs_0_), channel_id=1, source_target_pairs={{0,1},{1,0},{2,3},{3,2},{4,5},{5,4},{6,7},{7,6},{8,9},{9,8},{10,11... | collective-permute-start | bytes 6291464 | tf_op jit(solution)/shard_map/ppermute | solution.py:18
  4.0 4.2 %collective-permute-start = (f32[32,2048]{1,0:T(8,128)S(1)}, f32[32,2048]{1,0:T(8,128)S(1)}, u32[]{:S(2)}, u32[]{:S(2)}) collective-permute-start(f32[32,2048]{1,0:T(8,128)S(1)} %get-tuple-element.30), channel_id=1, source_target_pairs={{0,1},{1,0},{2,3},{3,2},{4,5},{5,4},{6,7},{7,6},{8,9},{9,8},{10,11... | collective-permute-start | bytes 786440 | tf_op jit(solution)/shard_map/ppermute | solution.py:18
  8.3 12.8 %collective-permute-start.2 = (bf16[32,2176]{1,0:T(8,128)(2,1)S(1)}, bf16[32,2176]{1,0:T(8,128)(2,1)S(1)}, u32[]{:S(2)}, u32[]{:S(2)}) collective-permute-start(bf16[32,2176]{1,0:T(8,128)(2,1)S(1)} %get-tuple-element.38), channel_id=1, source_target_pairs={{0,2},{2,0},{1,3},{3,1},{4,6},{6,4},{5,7},{7,5},{8,10},{10,8},{9,1... | collective-permute-start | bytes 417800 | tf_op jit(solution)/shard_map/ppermute | solution.py:18
  14.4 7.7 %collective-permute-start.1 = (f32[32,2048]{1,0:T(8,128)S(1)}, f32[32,2048]{1,0:T(8,128)S(1)}, u32[]{:S(2)}, u32[]{:S(2)}) collective-permute-start(f32[32,2048]{1,0:T(8,128)S(1)} %get-tuple-element.36.mine_ref), channel_id=1, source_target_pairs={{0,1},{1,0},{2,3},{3,2},{4,5},{5,4},{6,7},{7,6},{8,9},{9,8},{10,11... | collective-permute-start | bytes 786440 | tf_op jit(solution)/shard_map/ppermute | solution.py:18
  21.2 1.9 %collective-permute-start.3 = (bf16[32,2176]{1,0:T(8,128)(2,1)S(1)}, bf16[32,2176]{1,0:T(8,128)(2,1)S(1)}, u32[]{:S(2)}, u32[]{:S(2)}) collective-permute-start(bf16[32,2176]{1,0:T(8,128)(2,1)S(1)} %collective-permute-done.2.code_ref), channel_id=1, source_target_pairs={{0,1},{1,0},{2,3},{3,2},{4,5},{5,4},{6,7},{7,6},{8,9},{9,8},{10,11... | collective-permute-start | bytes 417800 | tf_op jit(solution)/shard_map/ppermute | solution.py:18
  53.1 1.7 %collective-permute-start.5 = (bf16[2,8,256]{2,1,0:T(8,128)(2,1)S(1)}, bf16[2,8,256]{2,1,0:T(8,128)(2,1)S(1)}, u32[]{:S(2)}, u32[]{:S(2)}) collective-permute-start(bf16[2,8,256]{2,1,0:T(8,128)(2,1)S(1)} %get-tuple-element.52), channel_id=1, source_target_pairs={{0,1},{1,0},{2,3},{3,2},{4,5},{5,4},{6,7},{7,6},{8,9},{9,8},{10,11... | collective-permute-start | bytes 24584 | tf_op jit(solution)/shard_map/ppermute | solution.py:18
